TPU v7x, 256 devices: a whole 4x4x8 slice. The times are simulated.
256 devices in a mesh: row: 16 (over z, core), col: 8 (over y_hi, x), rep: 2 (over y_lo).
Axes of the slice: x: 4, y: 4 (y_hi: 2, y_lo: 2; y = y_hi * 2 + y_lo), z: 8, core: 2. Of those that a mesh axis runs over, the one named last changes fastest.
Arguments:
- node_features: bfloat16 [65536, 256], P(('row', 'col', 'rep')), may hold values from -6 to 6
- weight: bfloat16 [256, 256], replicated, may hold values from -0.375 to 0.375
- cotangent: bfloat16 [65536, 256], P(('col', 'rep', 'row')), may hold values from -6 to 6
- adjacency_blocks: bfloat16 [16, 16, 256, 128, 128], P(('col', 'rep'), 'row'), may hold values from -0.0625 to 0.0625
- block_coords: int32 [16, 16, 2, 256], P(('col', 'rep'), 'row'), may hold values from 0 to 31, as said below
- block_counts: int32 [16, 16], P(('col', 'rep'), 'row'), may hold values from 1 to 256, as said below
Outputs:
- hidden: bfloat16 [65536, 256], P(('col', 'rep', 'row'))
- weight_grad: float32 [256, 256], replicated
- feature_grad: bfloat16 [65536, 256], P(('row', 'col', 'rep'))
Inputs may be any that keep to these rules, and one draw needn't show every extreme that they name: block_coords[i, r, 0, k] is a block row below 32 and block_coords[i, r, 1, k] a block column below 32; within a tile the first min(256, 1024) slots name distinct positions. Only the first block_counts[i, r] slots of tile (i, r) belong to the adjacency; the values and coordinates in its other slots are not part of it.
All inputs are finite; a program needn't handle non-finite values.
Results may differ from a plain program's by a relative error of at most 0.029.
Values may be sent and summed in bfloat16 or wider, within the bound.
No kernel may reach another device: no remote copies, remote signals or barrier semaphores. Data moves between devices by JAX's collectives and lax.ppermute only.
A program may use at most 128 MiB of HBM per device.

v0:
```python
import math

import jax
import jax.numpy as jnp
from jax import lax
from jax.sharding import PartitionSpec as P


def silu_slope(values):
    sigma = jax.nn.sigmoid(values)
    return sigma * (1.0 + values * (1.0 - sigma))


def tile_product(blocks, coords, filled, source, out_blocks, flipped):
    slot_total = blocks.shape[0]
    block_size = blocks.shape[1]
    feature_width = source.shape[1]
    group_size = math.gcd(slot_total, 64)
    groups = slot_total // group_size
    source_blocks = source.reshape(-1, block_size, feature_width)
    take_index = coords[0] if flipped else coords[1]
    put_index = coords[1] if flipped else coords[0]
    active = (jnp.arange(slot_total, dtype=jnp.int32) < filled).astype(jnp.float32)
    einsum_form = "kba,kbf->kaf" if flipped else "kab,kbf->kaf"
    targets = jnp.arange(out_blocks, dtype=jnp.int32)

    def accumulate(running, pieces):
        block_group, take_group, put_group, active_group = pieces
        gathered = source_blocks[take_group]
        product = jnp.einsum(einsum_form, block_group, gathered, preferred_element_type=jnp.float32)
        placing = (put_group[:, None] == targets[None, :]).astype(jnp.float32) * active_group[
            :, None
        ]
        flat = product.reshape(group_size, block_size * feature_width)
        placed = lax.dot_general(
            placing,
            flat,
            (((0,), (0,)), ((), ())),
            precision=lax.Precision.HIGHEST,
            preferred_element_type=jnp.float32,
        )
        return (running + placed, None)

    running = jnp.zeros((out_blocks, block_size * feature_width), jnp.float32)
    running, _ = lax.scan(
        accumulate,
        running,
        (
            blocks.reshape(groups, group_size, block_size, block_size),
            take_index.reshape(groups, group_size),
            put_index.reshape(groups, group_size),
            active.reshape(groups, group_size),
        ),
    )
    return running.reshape(out_blocks * block_size, feature_width)


def body(node_features, weight, cotangent, adjacency_blocks, block_coords, block_counts):
    blocks = adjacency_blocks[0, 0]
    coords = block_coords[0, 0]
    filled = block_counts[0, 0]
    block_size = blocks.shape[-1]
    local_nodes = node_features.shape[0]
    row_devices = lax.axis_size("row")
    node_total = local_nodes * row_devices * lax.axis_size("col") * lax.axis_size("rep")
    tile_rows = local_nodes * row_devices
    column_feats = lax.all_gather(node_features, ("col", "rep"), axis=0, tiled=True)
    tile_cols = column_feats.shape[0]
    partial_value = tile_product(
        blocks, coords, filled, column_feats, tile_rows // block_size, False
    )
    own_sum = lax.psum_scatter(
        partial_value.astype(jnp.bfloat16), "row", scatter_dimension=0, tiled=True
    )
    pre_act = jnp.dot(own_sum, weight, preferred_element_type=jnp.float32)
    hidden = jax.nn.silu(pre_act).astype(jnp.bfloat16)
    own_grad = (cotangent.astype(jnp.float32) * silu_slope(pre_act)).astype(jnp.bfloat16)
    own_mixed_grad = jnp.dot(own_grad, weight.T, preferred_element_type=jnp.float32).astype(
        jnp.bfloat16
    )
    panel_grad = lax.all_gather(own_mixed_grad, "row", axis=0, tiled=True)
    weight_part = lax.dot_general(
        own_sum, own_grad, (((0,), (0,)), ((), ())), preferred_element_type=jnp.float32
    )
    weight_grad = lax.psum(weight_part, ("row", "col", "rep")) / math.sqrt(node_total)
    back_terms = tile_product(blocks, coords, filled, panel_grad, tile_cols // block_size, True)
    feature_grad = lax.psum_scatter(
        back_terms.astype(jnp.bfloat16), ("col", "rep"), scatter_dimension=0, tiled=True
    )
    return (hidden, weight_grad, feature_grad)


def solution(mesh):
    in_specs = (
        P(("row", "col", "rep"), None),
        P(),
        P(("col", "rep", "row"), None),
        P(("col", "rep"), "row", None, None, None),
        P(("col", "rep"), "row", None, None),
        P(("col", "rep"), "row"),
    )
    out_specs = (P(("col", "rep", "row"), None), P(), P(("row", "col", "rep"), None))
    return jax.shard_map(body, mesh=mesh, in_specs=in_specs, out_specs=out_specs, check_vma=False)
```

profile of v0, /device:TPU:1, one launch (start us, length us, event | category | flops | bytes accessed | tf_op | source)
XLA Modules:
  0.0 633.6 jit_solution(17018396184696318942)
XLA Ops:
  7.2 0.0 copy-start
  7.2 0.0 all-gather.3.cloned.1.call-start
  7.2 0.7 all-gather.3.cloned.1.call-update
  7.9 0.0 reduce-scatter.3.cloned.1.call-start
  8.0 0.8 slice_reduce_fusion
  8.7 0.1 reshape_squeeze.12
  8.8 0.1 reshape_squeeze.14
  9.6 73.2 %all-gather.3.cloned.1.call-done = bf16[4096,256]{1,0:T(8,128)(2,1)} async-done(((bf16[256,256]{1,0:T(8,128)(2,1)}), bf16[4096,256]{1,0:T(8,128)(2,1)}) %all-gather.3.cloned.1.call-update) | async-done | bytes 2097168 | tf_op jit(solution)/shard_map/all_gather | solution.py:67
  82.8 99.7 %while.22 = (s32[]{:T(128)}, f32[32,32768]{1,0:T(8,128)}, s32[4,64]{1,0:T(4,128)S(1)}, f32[4,64]{1,0:T(4,128)S(1)}, bf16[4,64,128,128]{3,2,1,0:T(8,128)(2,1)}, /...) while((s32[]{:T(128)}, f32[32,32768]{1,0:T(8,128)}, ...), condition=%wide.region_1.2_spmd.clone, body=%wide.region_0.1_spmd.clone.sunk | while | flops 1344279808 | bytes 56630384 | solution.py:45
  82.8 4.3 gather_fusion
  87.1 4.1 fusion.63
  91.2 8.0 %copy.16 = f32[8,8,128,256]{3,1,2,0:T(8,128)} copy(f32[8,8,128,256]{3,2,1,0:T(8,128)S(1)} %bitcast.88) | data formatting | bytes 16777216 | tf_op jit(solution)/shard_map/while
  99.2 8.0 %convolution_add_fusion.4 = f32[32,32768]{1,0:T(8,128)} fusion(f32[64,32768]{1,0:T(8,128)} %bitcast.86, f32[32,32768]{1,0:T(8,128)} %get-tuple-element.276, pred[]{:T(512)S(6)} %compare.6, f32[64]{0:T(128)S(1)} %fusion.64, s32[64]{0:T(128)S(1)} %fusion.65), kind=kOutput, calls=%fused_computation.4.clone.1 | convolution fusion | flops 807407616 | bytes 16777728 | tf_op jit(solution)/shard_map/while/body/eval_jaxpr/dot_general | solution.py:35
  107.2 4.3 gather_fusion
  111.5 4.1 fusion.63
  115.6 8.0 %copy.16 = f32[8,8,128,256]{3,1,2,0:T(8,128)} copy(f32[8,8,128,256]{3,2,1,0:T(8,128)S(1)} %bitcast.88) | data formatting | bytes 16777216 | tf_op jit(solution)/shard_map/while
  123.6 8.7 %convolution_add_fusion.4 = f32[32,32768]{1,0:T(8,128)} fusion(f32[64,32768]{1,0:T(8,128)} %bitcast.86, f32[32,32768]{1,0:T(8,128)} %get-tuple-element.276, pred[]{:T(512)S(6)} %compare.6, f32[64]{0:T(128)S(1)} %fusion.64, s32[64]{0:T(128)S(1)} %fusion.65), kind=kOutput, calls=%fused_computation.4.clone.1 | convolution fusion | flops 807407616 | bytes 16777728 | tf_op jit(solution)/shard_map/while/body/eval_jaxpr/dot_general | solution.py:35
  132.3 4.3 gather_fusion
  136.6 4.1 fusion.63
  140.7 8.0 %copy.16 = f32[8,8,128,256]{3,1,2,0:T(8,128)} copy(f32[8,8,128,256]{3,2,1,0:T(8,128)S(1)} %bitcast.88) | data formatting | bytes 16777216 | tf_op jit(solution)/shard_map/while
  148.7 8.7 %convolution_add_fusion.4 = f32[32,32768]{1,0:T(8,128)} fusion(f32[64,32768]{1,0:T(8,128)} %bitcast.86, f32[32,32768]{1,0:T(8,128)} %get-tuple-element.276, pred[]{:T(512)S(6)} %compare.6, f32[64]{0:T(128)S(1)} %fusion.64, s32[64]{0:T(128)S(1)} %fusion.65), kind=kOutput, calls=%fused_computation.4.clone.1 | convolution fusion | flops 807407616 | bytes 16777728 | tf_op jit(solution)/shard_map/while/body/eval_jaxpr/dot_general | solution.py:35
  157.4 4.3 gather_fusion
  161.7 4.1 fusion.63
  165.8 8.0 %copy.16 = f32[8,8,128,256]{3,1,2,0:T(8,128)} copy(f32[8,8,128,256]{3,2,1,0:T(8,128)S(1)} %bitcast.88) | data formatting | bytes 16777216 | tf_op jit(solution)/shard_map/while
  173.8 8.7 %convolution_add_fusion.4 = f32[32,32768]{1,0:T(8,128)} fusion(f32[64,32768]{1,0:T(8,128)} %bitcast.86, f32[32,32768]{1,0:T(8,128)} %get-tuple-element.276, pred[]{:T(512)S(6)} %compare.6, f32[64]{0:T(128)S(1)} %fusion.64, s32[64]{0:T(128)S(1)} %fusion.65), kind=kOutput, calls=%fused_computation.4.clone.1 | convolution fusion | flops 807407616 | bytes 16777728 | tf_op jit(solution)/shard_map/while/body/eval_jaxpr/dot_general | solution.py:35
  182.4 2.4 convert_element_type.32
  184.8 0.0 copy-start.3
  184.8 2.4 convert_element_type.33
  187.2 0.0 reduce-scatter.3.cloned.1.call-update
  187.2 0.0 all-gather.5.cloned.1.call-start
  187.3 66.4 %reduce-scatter.3.cloned.1.call-done = bf16[256,256]{1,0:T(8,128)(2,1)} async-done(((bf16[4096,256]{1,0:T(8,128)(2,1)}), bf16[256,256]{1,0:T(8,128)(2,1)}) %reduce-scatter.3.cloned.1.call-update) | async-done | bytes 131088 | tf_op jit(solution)/shard_map/reduce_scatter | solution.py:72
  253.7 0.0 copy-done
  253.7 1.8 multiply_convert_fusion
  255.5 0.9 convolution_convert_fusion
  256.4 0.0 all-gather.5.cloned.1.call-update
  256.4 0.0 all-reduce.2.cloned.1.call-start
  256.5 12.0 %copy.9 = bf16[1,1,256,128,128]{3,4,2,1,0:T(8,128)(2,1)} copy(bf16[1,1,256,128,128]{4,3,2,1,0:T(8,128)(2,1)} %bitcast.93) | data formatting | bytes 16777216 | tf_op args[3]
  268.5 0.9 fusion.31
  269.4 0.0 all-reduce.2.cloned.1.call-update
  269.4 0.2 reduce-scatter.5.cloned.1.call-start
  269.7 28.7 %all-gather.5.cloned.1.call-done = bf16[4096,256]{1,0:T(8,128)(2,1)} async-done(((bf16[256,256]{1,0:T(8,128)(2,1)}), bf16[4096,256]{1,0:T(8,128)(2,1)}) %all-gather.5.cloned.1.call-update) | async-done | bytes 2097168 | tf_op jit(solution)/shard_map/all_gather | solution.py:81
  298.4 99.8 %while.23 = (s32[]{:T(128)}, f32[32,32768]{1,0:T(8,128)}, s32[4,64]{1,0:T(4,128)S(1)}, f32[4,64]{1,0:T(4,128)S(1)}, bf16[4,64,128,128]{2,3,1,0:T(8,128)(2,1)}, /...) while((s32[]{:T(128)}, f32[32,32768]{1,0:T(8,128)}, ...), condition=%wide.region_5.6_spmd.clone, body=%wide.region_4.5_spmd.clone.sunk | while | flops 1344279808 | bytes 56630384 | solution.py:45
  298.4 4.4 gather_fusion.1
  302.7 4.1 fusion.71
  306.8 8.0 %copy.17 = f32[8,8,128,256]{3,1,2,0:T(8,128)} copy(f32[8,8,128,256]{3,2,1,0:T(8,128)S(1)} %bitcast.89) | data formatting | bytes 16777216 | tf_op jit(solution)/shard_map/while
  314.8 8.0 %convolution_add_fusion.5 = f32[32,32768]{1,0:T(8,128)} fusion(f32[64,32768]{1,0:T(8,128)} %bitcast.87, f32[32,32768]{1,0:T(8,128)} %get-tuple-element.303, pred[]{:T(512)S(6)} %compare.7, f32[64]{0:T(128)S(1)} %fusion.72, s32[64]{0:T(128)S(1)} %fusion.73), kind=kOutput, calls=%fused_computation.24.clone.1 | convolution fusion | flops 807407616 | bytes 16777728 | tf_op jit(solution)/shard_map/while/body/eval_jaxpr/dot_general | solution.py:35
  322.8 4.4 gather_fusion.1
  327.2 4.1 fusion.71
  331.3 8.0 %copy.17 = f32[8,8,128,256]{3,1,2,0:T(8,128)} copy(f32[8,8,128,256]{3,2,1,0:T(8,128)S(1)} %bitcast.89) | data formatting | bytes 16777216 | tf_op jit(solution)/shard_map/while
  339.2 8.7 %convolution_add_fusion.5 = f32[32,32768]{1,0:T(8,128)} fusion(f32[64,32768]{1,0:T(8,128)} %bitcast.87, f32[32,32768]{1,0:T(8,128)} %get-tuple-element.303, pred[]{:T(512)S(6)} %compare.7, f32[64]{0:T(128)S(1)} %fusion.72, s32[64]{0:T(128)S(1)} %fusion.73), kind=kOutput, calls=%fused_computation.24.clone.1 | convolution fusion | flops 807407616 | bytes 16777728 | tf_op jit(solution)/shard_map/while/body/eval_jaxpr/dot_general | solution.py:35
  347.9 4.4 gather_fusion.1
  352.3 4.1 fusion.71
  356.4 8.0 %copy.17 = f32[8,8,128,256]{3,1,2,0:T(8,128)} copy(f32[8,8,128,256]{3,2,1,0:T(8,128)S(1)} %bitcast.89) | data formatting | bytes 16777216 | tf_op jit(solution)/shard_map/while
  364.4 8.6 %convolution_add_fusion.5 = f32[32,32768]{1,0:T(8,128)} fusion(f32[64,32768]{1,0:T(8,128)} %bitcast.87, f32[32,32768]{1,0:T(8,128)} %get-tuple-element.303, pred[]{:T(512)S(6)} %compare.7, f32[64]{0:T(128)S(1)} %fusion.72, s32[64]{0:T(128)S(1)} %fusion.73), kind=kOutput, calls=%fused_computation.24.clone.1 | convolution fusion | flops 807407616 | bytes 16777728 | tf_op jit(solution)/shard_map/while/body/eval_jaxpr/dot_general | solution.py:35
  373.1 4.4 gather_fusion.1
  377.4 4.1 fusion.71
  381.5 8.0 %copy.17 = f32[8,8,128,256]{3,1,2,0:T(8,128)} copy(f32[8,8,128,256]{3,2,1,0:T(8,128)S(1)} %bitcast.89) | data formatting | bytes 16777216 | tf_op jit(solution)/shard_map/while
  389.5 8.7 %convolution_add_fusion.5 = f32[32,32768]{1,0:T(8,128)} fusion(f32[64,32768]{1,0:T(8,128)} %bitcast.87, f32[32,32768]{1,0:T(8,128)} %get-tuple-element.303, pred[]{:T(512)S(6)} %compare.7, f32[64]{0:T(128)S(1)} %fusion.72, s32[64]{0:T(128)S(1)} %fusion.73), kind=kOutput, calls=%fused_computation.24.clone.1 | convolution fusion | flops 807407616 | bytes 16777728 | tf_op jit(solution)/shard_map/while/body/eval_jaxpr/dot_general | solution.py:35
  398.2 2.4 convert_element_type.38
  400.6 2.4 convert_element_type.39
  402.9 0.0 reduce-scatter.5.cloned.1.call-update
  403.0 147.9 %all-reduce.2.cloned.1.call-done = f32[256,256]{1,0:T(8,128)} async-done(((f32[256,256]{1,0:T(8,128)}), f32[256,256]{1,0:T(8,128)}) %all-reduce.2.cloned.1.call-update) | async-done | bytes 262160 | tf_op jit(solution)/shard_map/psum | solution.py:85
  550.8 1.7 broadcast_multiply_fusion
  552.5 74.5 %reduce-scatter.5.cloned.1.call-done = bf16[256,256]{1,0:T(8,128)(2,1)} async-done(((bf16[4096,256]{1,0:T(8,128)(2,1)}), bf16[256,256]{1,0:T(8,128)(2,1)}) %reduce-scatter.5.cloned.1.call-update) | async-done | bytes 131088 | tf_op jit(solution)/shard_map/reduce_scatter | solution.py:87
  (40 shorter events, 0.2 us)
Async XLA Ops:
  7.2 246.5 %copy-start = (bf16[256,256]{1,0:T(8,128)(2,1)S(1)}, bf16[256,256]{1,0:T(8,128)(2,1)}, u32[]{:S(2)}) copy-start(bf16[256,256]{1,0:T(8,128)(2,1)} %param.11) | copy-start | bytes 393220
  7.2 75.6 %all-gather.3.cloned.1.call-start = ((), (), s32[]{:S(2)}) async-start(), calls=%async_computation.2 | async-start | bytes 2228224 | tf_op jit(solution)/shard_map/all_gather | solution.py:67
  7.9 245.7 %reduce-scatter.3.cloned.1.call-start = ((), (), s32[]{:S(2)}) async-start(), calls=%async_computation.3 | async-start | bytes 2228224 | tf_op jit(solution)/shard_map/reduce_scatter | solution.py:72
  184.8 68.8 %copy-start.3 = (bf16[256,256]{1,0:T(8,128)(2,1)S(1)}, bf16[256,256]{1,0:T(8,128)(2,1)}, u32[]{:S(2)}) copy-start(bf16[256,256]{1,0:T(8,128)(2,1)} %param.12) | copy-start | bytes 393220
  187.2 111.2 %all-gather.5.cloned.1.call-start = ((), (), s32[]{:S(2)}) async-start(), calls=%async_computation.5 | async-start | bytes 2228224 | tf_op jit(solution)/shard_map/all_gather | solution.py:81
  256.4 12.1 %copy-start.2 = (bf16[256,256]{1,0:T(8,128)(2,1)S(1)}, bf16[256,256]{1,0:T(8,128)(2,1)}, u32[]{:S(2)}) copy-start(bf16[256,256]{1,0:T(8,128)(2,1)} %reduce-scatter.3.cloned.1.call-done) | copy-start | bytes 393220
  256.4 294.4 %all-reduce.2.cloned.1.call-start = ((), (), s32[]{:S(2)}) async-start(), calls=%async_computation.4 | async-start | bytes 524288 | tf_op jit(solution)/shard_map/psum | solution.py:85
  269.4 357.6 %reduce-scatter.5.cloned.1.call-start = ((), (), s32[]{:S(2)}) async-start(), calls=%async_computation.6 | async-start | bytes 2228224 | tf_op jit(solution)/shard_map/reduce_scatter | solution.py:87
  398.2 228.9 %copy-start.1 = (bf16[256,256]{1,0:T(8,128)(2,1)S(1)}, bf16[256,256]{1,0:T(8,128)(2,1)}, u32[]{:S(2)}) copy-start(bf16[256,256]{1,0:T(8,128)(2,1)} %param.11) | copy-start | bytes 393220
Sparse Core Ops, SparseCore 0:
  9.8 72.9 all-gather.2
  187.3 66.2 reduce-scatter.2
  256.5 41.7 all-gather.4
  304.2 246.5 all-reduce.1
  553.8 73.1 reduce-scatter.4
where the time goes:
time: 643 us; the launch traced here: 634 us
  waiting for transfers between devices  391 us (61%)
  local copies, waits for them, and re-layouts  116 us (18%)
  matrix products  104 us (16%)
  between operations  14.5 us (2%)
  other arithmetic  6.61 us (1%)
    psum x1, waiting for transfers between devices, body(): lax.psum(weight_part, ('row', 'col', 'rep')) / math.sqrt(node_total)  148 us
    reduce_scatter x1, waiting for transfers between devices, body(): lax.psum_scatter(back_terms.astype(jnp.bfloat16), ('col', 'rep'), scatter...  74.5 us
    all_gather x1, waiting for transfers between devices, body(): lax.all_gather(node_features, ('col', 'rep'), axis=0, tiled=True)  73.2 us
    dot_general x8, matrix products, accumulate(): lax.dot_general(placing, flat, (((0,), (0,)), ((), ())), precision=lax.Pr...  68 us
    reduce_scatter x1, waiting for transfers between devices, body(): lax.psum_scatter(partial_value.astype(jnp.bfloat16), 'row', scatter_dimen...  66.4 us
    while x8, local copies, waits for them, and re-layouts  63.7 us
    gather x8, local copies, waits for them, and re-layouts, accumulate(): gathered = source_blocks[take_group]  34.8 us
    dot_general x8, matrix products, accumulate(): jnp.einsum(einsum_form, block_group, gathered, preferred_element_type=jnp...  32.6 us
  transfers between devices with their start and end apart: 5, of which 5 were waited for; matrix products, arithmetic and copies ran while one was open for 19% of the time, Pallas kernels for 0%

commit v1 on v0

v1 whole, which is shorter than its diff:
```python
import functools
import math

import jax
import jax.numpy as jnp
from jax import lax
from jax.experimental import pallas as pl
from jax.experimental.pallas import tpu as pltpu
from jax.sharding import Mesh, PartitionSpec as P

BLK = 128
UNROLL = 4
PLANE = ("yh", "x", "yl")
BF16 = jnp.bfloat16
F32 = jnp.float32
VMEM_LIMIT = 48 * 1024 * 1024


def slot_tables_kernel(coords_ref, count_ref, table_ref):
    slots = coords_ref.shape[1]
    coords = jnp.concatenate([coords_ref[...], jnp.zeros((6, slots), jnp.int32)], axis=0).astype(F32)
    columns = jnp.transpose(coords)
    lane = lax.broadcasted_iota(jnp.int32, (slots, slots), 1)
    sublane = lax.broadcasted_iota(jnp.int32, (slots, slots), 0)
    filled = count_ref[0]
    rows = []
    for by in range(2):
        key_lane = jnp.where(lane < filled, jnp.broadcast_to(coords[by : by + 1], (slots, slots)), 99.0)
        key_sub = jnp.where(sublane < filled, jnp.broadcast_to(columns[:, by : by + 1], (slots, slots)), 99.0)
        ahead = (key_lane < key_sub) | ((key_lane == key_sub) & (lane < sublane))
        place = jnp.sum(ahead.astype(F32), axis=1, keepdims=True)
        here = (jnp.broadcast_to(place, (slots, slots)) == lane.astype(F32)).astype(F32)
        other = jnp.broadcast_to(columns[:, 1 - by : 2 - by], (slots, slots))
        rows.append(jnp.sum(here * sublane.astype(F32), axis=0, keepdims=True))
        rows.append(jnp.sum(here * other, axis=0, keepdims=True))
        rows.append(jnp.sum((key_sub < lane.astype(F32)).astype(F32), axis=0, keepdims=True))
    rows.append(jnp.zeros((2, slots), F32))
    table_ref[...] = jnp.concatenate(rows, axis=0).astype(jnp.int32)


def slot_tables(coords, count):
    slots = coords.shape[1]
    return pl.pallas_call(
        slot_tables_kernel,
        out_shape=jax.ShapeDtypeStruct((8, slots), jnp.int32),
        in_specs=[pl.BlockSpec(memory_space=pltpu.VMEM), pl.BlockSpec(memory_space=pltpu.SMEM)],
        out_specs=pl.BlockSpec(memory_space=pltpu.VMEM),
    )(coords, count)


def line_sum(table_ref, base, line, blocks_ref, read_source, width, contract):
    begin = table_ref[base + 2, line]
    end = table_ref[base + 2, line + 1]

    def step(i, running):
        for u in range(UNROLL):
            at = begin + i * UNROLL + u
            inside = at < end
            safe = jnp.minimum(at, end - 1)
            block = blocks_ref[table_ref[base, safe]]
            block = jnp.where(inside, block, jnp.zeros_like(block))
            running += lax.dot_general(
                block,
                read_source(table_ref[base + 1, safe]),
                (((contract,), (0,)), ((), ())),
                preferred_element_type=F32,
            )
        return running

    return lax.fori_loop(
        0, (end - begin + UNROLL - 1) // UNROLL, step, jnp.zeros((BLK, width), F32)
    )


def forward_kernel(depth, table_ref, place_ref, blocks_ref, source_ref, sibling_ref, own_ref):
    width = source_ref.shape[1]
    layer, core = place_ref[0], place_ref[1]

    def read_source(at):
        return source_ref[pl.ds(pl.multiple_of(at * BLK, BLK), BLK), :]

    for out_ref, side in ((sibling_ref, 1 - core), (own_ref, core)):

        @pl.loop(0, 2 * depth)
        def _(i, out_ref=out_ref, side=side):
            target = lax.rem(layer + i // 2, depth)
            line = (target * 2 + side) * 2 + lax.rem(i, 2)
            total = line_sum(table_ref, 0, line, blocks_ref, read_source, width, 1)
            out_ref[pl.ds(pl.multiple_of(i * BLK, BLK), BLK), :] = total.astype(BF16)


def forward_product(table, place, blocks, source, depth):
    rows, width = source.shape
    half = jax.ShapeDtypeStruct((rows // 2, width), BF16)
    return pl.pallas_call(
        functools.partial(forward_kernel, depth),
        out_shape=(half, half),
        in_specs=[pl.BlockSpec(memory_space=pltpu.SMEM)] * 2
        + [pl.BlockSpec(memory_space=pltpu.VMEM)] * 2,
        out_specs=(pl.BlockSpec(memory_space=pltpu.VMEM),) * 2,
        compiler_params=pltpu.CompilerParams(vmem_limit_bytes=VMEM_LIMIT),
    )(table, place, blocks, source)


def backward_kernel(depth, table_ref, place_ref, blocks_ref, own_ref, sibling_ref, tail_ref, out_ref, source_ref):
    rows, width = own_ref.shape
    layer, core = place_ref[0], place_ref[1]
    source_ref[pl.ds(0, rows), :] = own_ref[...]
    source_ref[pl.ds(rows, rows), :] = sibling_ref[...]

    def read_source(line):
        side = jnp.bitwise_and(lax.shift_right_logical(line, 1), 1)
        step = lax.rem(lax.shift_right_logical(line, 2) + depth - layer, depth)
        away = jnp.where(side == core, 0, rows)
        at = away + (step * 2 + jnp.bitwise_and(line, 1)) * BLK
        return source_ref[pl.ds(pl.multiple_of(at, BLK), BLK), :]

    parts, padded = out_ref.shape[0], out_ref.shape[1]
    tail = tail_ref.shape[0]

    @pl.loop(0, parts)
    def _(part):
        for h in range(2):
            total = line_sum(table_ref, 3, part * 2 + h, blocks_ref, read_source, width, 0)
            out_ref[part, pl.ds(h * BLK, BLK), :] = total.astype(BF16)
        out_ref[part, pl.ds(padded - tail, tail), :] = tail_ref[...]


def backward_product(table, place, blocks, own, sibling, tail, depth, parts):
    rows, width = own.shape
    return pl.pallas_call(
        functools.partial(backward_kernel, depth),
        out_shape=jax.ShapeDtypeStruct((parts, 2 * BLK + tail.shape[0], width), BF16),
        in_specs=[pl.BlockSpec(memory_space=pltpu.SMEM)] * 2
        + [pl.BlockSpec(memory_space=pltpu.VMEM)] * 4,
        out_specs=pl.BlockSpec(memory_space=pltpu.VMEM),
        scratch_shapes=[pltpu.VMEM((2 * rows, width), BF16)],
        compiler_params=pltpu.CompilerParams(vmem_limit_bytes=VMEM_LIMIT),
    )(table, place, blocks, own, sibling, tail)


def dense_kernel(mine_ref, sibling_ref, up_ref, down_ref, weight_ref, cotangent_ref, hidden_ref, grad_ref, part_ref):
    summed = (mine_ref[...].astype(F32) + sibling_ref[...].astype(F32)) + (
        up_ref[...].astype(F32) + down_ref[...].astype(F32)
    )
    mixed = summed.astype(BF16)
    weight = weight_ref[...]
    pre_act = jnp.dot(mixed, weight, preferred_element_type=F32)
    sigma = jax.nn.sigmoid(pre_act)
    hidden_ref[...] = (pre_act * sigma).astype(BF16)
    slope = sigma * (1.0 + pre_act * (1.0 - sigma))
    act_grad = (cotangent_ref[...].astype(F32) * slope).astype(BF16)
    grad_ref[...] = lax.dot_general(
        act_grad, weight, (((1,), (1,)), ((), ())), preferred_element_type=F32
    ).astype(BF16)
    part_ref[...] = lax.dot_general(
        mixed, act_grad, (((0,), (0,)), ((), ())), preferred_element_type=F32
    )


def dense(mine, sibling, up, down, weight, cotangent):
    shape = cotangent.shape
    return pl.pallas_call(
        dense_kernel,
        out_shape=(
            jax.ShapeDtypeStruct(shape, BF16),
            jax.ShapeDtypeStruct(shape, BF16),
            jax.ShapeDtypeStruct(weight.shape, F32),
        ),
    )(mine, sibling, up, down, weight, cotangent)


def body(sizes, node_features, weight, cotangent, adjacency_blocks, block_coords, block_counts):
    depth, nx, ny = sizes
    plane = nx * ny
    blocks = adjacency_blocks[0, 0]
    local, width = node_features.shape
    node_total = local * plane * depth * 2
    layer = lax.axis_index("z")
    core = lax.axis_index("c")
    place = jnp.stack([layer, core]).astype(jnp.int32)
    across = [(0, 1), (1, 0)]

    def around(shift):
        return [(i, (i + shift) % depth) for i in range(depth)]

    def rank(x, y):
        return ((y % ny) // 2 * nx + x % nx) * 2 + y % 2

    def along(dx, dy):
        return [(rank(x, y), rank(x + dx, y + dy)) for x in range(nx) for y in range(ny)]

    table = slot_tables(block_coords[0, 0], block_counts.reshape(1))
    spread = jnp.broadcast_to(node_features[None], (plane, local, width))
    column_feats = lax.all_to_all(spread, PLANE, 0, 0, tiled=True).reshape(plane * local, width)

    for_sibling, own = forward_product(table, place, blocks, column_feats, depth)
    sibling = lax.ppermute(for_sibling, "c", across)
    own = own.reshape(depth, local, width)
    sibling = sibling.reshape(depth, local, width)

    def term(step):
        return own[step].astype(F32) + sibling[step].astype(F32)

    half = local // 2
    middle = depth // 2
    far = term(middle).astype(BF16)
    up = lax.ppermute(far[:half], "z", around(1))
    down = lax.ppermute(far[half:], "z", around(-1))
    up = jnp.concatenate([up, jnp.zeros_like(up)], axis=0)
    down = jnp.concatenate([jnp.zeros_like(down), down], axis=0)
    for step in range(middle - 1, 0, -1):
        up = lax.ppermute((term(step) + up.astype(F32)).astype(BF16), "z", around(1))
        down = lax.ppermute((term(depth - step) + down.astype(F32)).astype(BF16), "z", around(-1))

    hidden, mixed_grad, weight_part = dense(own[0], sibling[0], up, down, weight, cotangent)

    chunks = {0: mixed_grad}
    ahead = behind = mixed_grad
    for step in range(1, middle):
        ahead = lax.ppermute(ahead, "z", around(1))
        behind = lax.ppermute(behind, "z", around(-1))
        chunks[depth - step] = ahead
        chunks[step] = behind
    chunks[middle] = jnp.concatenate(
        [
            lax.ppermute(ahead[:half], "z", around(1)),
            lax.ppermute(behind[half:], "z", around(-1)),
        ],
        axis=0,
    )
    own_panel = jnp.concatenate([chunks[step] for step in range(depth)], axis=0)
    sibling_panel = lax.ppermute(own_panel, "c", across)

    at_x = lax.axis_index("x")
    at_y = lax.axis_index("yh") * 2 + lax.axis_index("yl")
    for at, size, shift in ((at_x, nx, lambda d: along(d, 0)), (at_y, ny, lambda d: along(0, d))):
        shares = weight_part.reshape(size, -1, width)

        def share(d, shares=shares, at=at, size=size):
            return lax.dynamic_index_in_dim(shares, lax.rem(at + d, size), 0, keepdims=False)

        weight_part = share(0)
        for d in range(1, size):
            weight_part += lax.ppermute(share(d), PLANE, shift(d))
    weight_part += lax.ppermute(weight_part, "c", across)
    hop = 1
    while hop < depth:
        weight_part += lax.ppermute(weight_part, "z", [(i, i ^ hop) for i in range(depth)])
        hop *= 2
    tail = weight_part.astype(BF16)

    back = backward_product(table, place, blocks, own_panel, sibling_panel, tail, depth, plane)
    arrived = lax.all_to_all(back, PLANE, 0, 0, tiled=True)
    feature_grad = jnp.sum(arrived[:, :local].astype(F32), axis=0).astype(BF16)
    gathered = arrived[:, local:].reshape(ny // 2, nx, 2, -1, width)
    weight_sum = gathered.transpose(1, 0, 2, 3, 4).reshape(weight.shape)
    weight_grad = weight_sum.astype(F32) / math.sqrt(node_total)
    return (hidden, weight_grad, feature_grad)


def solution(mesh):
    depth = mesh.shape["row"] // 2
    nx = mesh.shape["col"] // 2
    ny = mesh.shape["rep"] * 2
    fine = Mesh(mesh.devices.reshape(depth, 2, ny // 2, nx, 2), ("z", "c", "yh", "x", "yl"))
    row, col = ("z", "c"), ("yh", "x")
    in_specs = (
        P((*row, *PLANE), None),
        P(),
        P((*PLANE, *row), None),
        P(PLANE, row, None, None, None),
        P(PLANE, row, None, None),
        P(PLANE, row),
    )
    out_specs = (P((*PLANE, *row), None), P(), P((*row, *PLANE), None))
    return jax.shard_map(
        functools.partial(body, (depth, nx, ny)),
        mesh=fine,
        in_specs=in_specs,
        out_specs=out_specs,
        check_vma=False,
    )
```

time: 643 us -> 225 us (0.35)
  waiting for transfers between devices: 391 us -> 78.2 us
  local copies, waits for them, and re-layouts: 116 us -> 6.91 us
  matrix products: 104 us -> 0 us
  starting transfers between devices: 0.38 us -> 66.2 us
  blocking collectives: 0 us -> 40.1 us
  Pallas kernels: 0 us -> 27.1 us
  between operations: 14.5 us -> 1.52 us
    psum x1 -> x0, waiting for transfers between devices: 148 us -> none  [body(): lax.psum(weight_part, ('row', 'col', 'rep')) / math.sqrt(node_total)]
    reduce_scatter x2 -> x0, waiting for transfers between devices: 141 us -> none  [the longest x1 74.5 us: body(): lax.psum_scatter(back_terms.astype(jnp.bfloat16), ('col', 'rep'), scatter...]
    dot_general x19 -> x0, matrix products: 104 us -> none  [the longest x8 68 us: accumulate(): lax.dot_general(placing, flat, (((0,), (0,)), ((), ())), precision=lax.Pr...]
    all_gather x2 -> x0, waiting for transfers between devices: 102 us -> none  [the longest x1 73.2 us: body(): lax.all_gather(node_features, ('col', 'rep'), axis=0, tiled=True)]
    while x8 -> x0, local copies, waits for them, and re-layouts: 63.7 us -> none
    ppermute x0 -> x28, starting transfers between devices: none -> 58.6 us  [the longest x3 13.2 us: body(): lax.ppermute((term(depth - step) + down.astype(F32)).astype(BF16), 'z', a...]
    ppermute x0 -> x28, waiting for transfers between devices: none -> 49.8 us  [the longest x3 13 us: body(): lax.ppermute((term(step) + up.astype(F32)).astype(BF16), 'z', around(1))]
    all_to_all x0 -> x1, blocking collectives: none -> 40.1 us  [body(): arrived = lax.all_to_all(back, PLANE, 0, 0, tiled=True)]
  transfers between devices with their start and end apart: 5 -> 29, of which waited for: 5 -> 20; matrix products, arithmetic and copies ran while one was open for 19% -> 1% of each run, Pallas kernels for 0% -> 1%
where the time goes in v1:
time: 225 us; the launch traced here: 221 us
  waiting for transfers between devices  78.2 us (35%)
  starting transfers between devices  66.2 us (29%)
  blocking collectives  40.1 us (18%)
  Pallas kernels  27.1 us (12%)
  local copies, waits for them, and re-layouts  6.91 us (3%)
    all_to_all x1, blocking collectives, body(): arrived = lax.all_to_all(back, PLANE, 0, 0, tiled=True)  40.1 us
    all_to_all x1, waiting for transfers between devices, body(): lax.all_to_all(spread, PLANE, 0, 0, tiled=True)  28.4 us
    ppermute x3, starting transfers between devices, body(): lax.ppermute((term(depth - step) + down.astype(F32)).astype(BF16), 'z', a...  13.2 us
    ppermute x3, waiting for transfers between devices, body(): lax.ppermute((term(step) + up.astype(F32)).astype(BF16), 'z', around(1))  13 us
    pallas_call x1, Pallas kernels, backward_product(): pl.pallas_call(functools.partial(backward_kernel, depth), out_shape=jax.S...  12.2 us
    ppermute x1, starting transfers between devices, body(): sibling_panel = lax.ppermute(own_panel, 'c', across)  11.7 us
    pallas_call x1, Pallas kernels, forward_product(): pl.pallas_call(functools.partial(forward_kernel, depth), out_shape=(half,...  10.8 us
    ppermute x3, waiting for transfers between devices, body(): lax.ppermute(weight_part, 'z', [(i, i ^ hop) for i in range(depth)])  9.98 us
  transfers between devices with their start and end apart: 29, of which 20 were waited for; matrix products, arithmetic and copies ran while one was open for 1% of the time, Pallas kernels for 1%

profile of v1, /device:TPU:1, one launch (start us, length us, event | category | flops | bytes accessed | tf_op | source)
XLA Modules:
  0.0 221.4 jit_solution(3511111915344701125)
XLA Ops:
  0.6 2.5 %broadcast_in_dim.2 = bf16[16,256,256]{2,1,0:T(8,128)(2,1)} broadcast(bf16[256,256]{1,0:T(8,128)(2,1)} %param.6), dimensions={1,2} | broadcast | bytes 2228224 | tf_op jit(solution)/shard_map/broadcast_in_dim | solution.py:194
  3.1 7.6 %all-to-all-start = ((bf16[16,256,256]{2,1,0:T(8,128)(2,1)}), bf16[16,256,256]{2,1,0:T(8,128)(2,1)S(1)}, u32[]{:S(2)}, u32[]{:S(2)}) async-start(bf16[16,256,256]{2,1,0:T(8,128)(2,1)} %broadcast_in_dim.2), calls=%async_computation | async-start | bytes 4194304 | tf_op jit(solution)/shard_map/all_to_all | solution.py:195
  11.4 1.8 shard_map.85.table_ref
  13.1 0.1 pad_add_fusion.place_ref
  13.2 28.4 %all-to-all-done = bf16[16,256,256]{2,1,0:T(8,128)(2,1)S(1)} async-done(((bf16[16,256,256]{2,1,0:T(8,128)(2,1)}), bf16[16,256,256]{2,1,0:T(8,128)(2,1)S(1)}, u32[]{:S(2)}, u32[]{:S(2)}) %all-to-all-start) | async-done | bytes 2097184 | tf_op jit(solution)/shard_map/all_to_all | solution.py:195
  41.7 0.7 copy-done
  42.4 10.8 %shard_map.86 = (bf16[2048,256]{1,0:T(8,128)(2,1)S(1)}, bf16[2048,256]{1,0:T(8,128)(2,1)S(1)}) custom-call(s32[8,256]{1,0:T(8,128)S(1)} %copy-done, s32[2]{0:T(128)S(1)} %pad_add_fusion.place_ref, bf16[256,128,128]{2,1,0:T(8,128)(2,1)} %bitcast.38, bf16[4096,256]{1,0:T(8,128)(2,1)S(1)} %bitcast.37), custom_call_target="tpu_custom_call" | custom-call | tf_op jit(solution)/shard_map/pallas_call | solution.py:95
  53.2 2.1 collective-permute-start
  55.3 2.3 %collective-permute-done = bf16[2048,256]{1,0:T(8,128)(2,1)S(1)} collective-permute-done((bf16[2048,256]{1,0:T(8,128)(2,1)S(1)}, bf16[2048,256]{1,0:T(8,128)(2,1)S(1)}, u32[]{:S(2)}, u32[]{:S(2)}) %collective-permute-start) | collective-permute-done | bytes 1048608 | tf_op jit(solution)/shard_map/ppermute | solution.py:198
  57.6 5.5 %collective-permute-start.5 = (bf16[128,256]{1,0:T(8,128)(2,1)S(1)}, bf16[128,256]{1,0:T(8,128)(2,1)S(1)}, u32[]{:S(2)}, u32[]{:S(2)}) collective-permute-start(bf16[128,256]{1,0:T(8,128)(2,1)S(1)} %get-tuple-element.18), channel_id=1, source_target_pairs={{0,224},{32,0},{64,32},{96,64},{128,96},{160,128},{192,160},{224,1... | collective-permute-start | bytes 196616 | tf_op jit(solution)/shard_map/ppermute | solution.py:209
  63.2 1.3 collective-permute-done.5
  64.6 8.0 %collective-permute-start.6 = (bf16[256,256]{1,0:T(8,128)(2,1)S(1)}, bf16[256,256]{1,0:T(8,128)(2,1)S(1)}, u32[]{:S(2)}, u32[]{:S(2)}) collective-permute-start(bf16[256,256]{1,0:T(8,128)(2,1)S(1)} %add_convert_fusion.2), channel_id=1, source_target_pairs={{0,224},{32,0},{64,32},{96,64},{128,96},{160,128},{192,160},{224,1... | collective-permute-start | bytes 393224 | tf_op jit(solution)/shard_map/ppermute | solution.py:214
  72.5 2.5 %collective-permute-done.6 = bf16[256,256]{1,0:T(8,128)(2,1)S(1)} collective-permute-done((bf16[256,256]{1,0:T(8,128)(2,1)S(1)}, bf16[256,256]{1,0:T(8,128)(2,1)S(1)}, u32[]{:S(2)}, u32[]{:S(2)}) %collective-permute-start.6) | collective-permute-done | bytes 131104 | tf_op jit(solution)/shard_map/ppermute | solution.py:214
  75.1 0.1 add_convert_fusion.1
  75.1 2.6 %collective-permute-start.7 = (bf16[256,256]{1,0:T(8,128)(2,1)S(1)}, bf16[256,256]{1,0:T(8,128)(2,1)S(1)}, u32[]{:S(2)}, u32[]{:S(2)}) collective-permute-start(bf16[256,256]{1,0:T(8,128)(2,1)S(1)} %add_convert_fusion.1), channel_id=1, source_target_pairs={{0,224},{32,0},{64,32},{96,64},{128,96},{160,128},{192,160},{224,1... | collective-permute-start | bytes 393224 | tf_op jit(solution)/shard_map/ppermute | solution.py:214
  77.7 4.3 %collective-permute-done.1 = bf16[128,256]{1,0:T(8,128)(2,1)S(1)} collective-permute-done((bf16[128,256]{1,0:T(8,128)(2,1)S(1)}, bf16[128,256]{1,0:T(8,128)(2,1)S(1)}, u32[]{:S(2)}, u32[]{:S(2)}) %collective-permute-start.1) | collective-permute-done | bytes 65568 | tf_op jit(solution)/shard_map/ppermute | solution.py:208
  82.0 0.0 collective-permute-done.7
  82.0 0.1 add_convert_fusion
  82.1 0.1 collective-permute-start.2
  82.2 5.0 %collective-permute-done.2 = bf16[256,256]{1,0:T(8,128)(2,1)S(1)} collective-permute-done((bf16[256,256]{1,0:T(8,128)(2,1)S(1)}, bf16[256,256]{1,0:T(8,128)(2,1)S(1)}, u32[]{:S(2)}, u32[]{:S(2)}) %collective-permute-start.2) | collective-permute-done | bytes 131104 | tf_op jit(solution)/shard_map/ppermute | solution.py:213
  87.2 0.1 add_convert_fusion.4
  87.3 0.1 collective-permute-start.3
  87.4 2.7 %collective-permute-start.8 = (bf16[256,256]{1,0:T(8,128)(2,1)S(1)}, bf16[256,256]{1,0:T(8,128)(2,1)S(1)}, u32[]{:S(2)}, u32[]{:S(2)}) collective-permute-start(bf16[256,256]{1,0:T(8,128)(2,1)S(1)} %get-tuple-element.13), channel_id=1, source_target_pairs={{0,224},{32,0},{64,32},{96,64},{128,96},{160,128},{192,160},{224,1... | collective-permute-start | bytes 393224 | tf_op jit(solution)/shard_map/ppermute | solution.py:214
  90.0 2.9 %collective-permute-done.3 = bf16[256,256]{1,0:T(8,128)(2,1)S(1)} collective-permute-done((bf16[256,256]{1,0:T(8,128)(2,1)S(1)}, bf16[256,256]{1,0:T(8,128)(2,1)S(1)}, u32[]{:S(2)}, u32[]{:S(2)}) %collective-permute-start.3) | collective-permute-done | bytes 131104 | tf_op jit(solution)/shard_map/ppermute | solution.py:213
  92.9 0.1 add_convert_fusion.3
  93.0 0.1 collective-permute-start.4
  93.1 0.7 slice.82.mine_ref
  93.7 0.7 slice.104.sibling_ref
  94.4 0.0 collective-permute-done.8.down_ref
  94.4 5.1 %collective-permute-done.4.up_ref = bf16[256,256]{1,0:T(8,128)(2,1)S(1)} collective-permute-done((bf16[256,256]{1,0:T(8,128)(2,1)S(1)}, bf16[256,256]{1,0:T(8,128)(2,1)S(1)}, u32[]{:S(2)}, u32[]{:S(2)}) %collective-permute-start.4) | collective-permute-done | bytes 131104 | tf_op jit(solution)/shard_map/ppermute | solution.py:213
  99.5 0.6 copy-done.4
  100.2 2.3 %shard_map.87 = (bf16[256,256]{1,0:T(8,128)(2,1)}, bf16[256,256]{1,0:T(8,128)(2,1)}, f32[256,256]{1,0:T(8,128)}) custom-call(bf16[256,256]{1,0:T(8,128)(2,1)} %slice.82.mine_ref, bf16[256,256]{1,0:T(8,128)(2,1)} %slice.104.sibling_ref, bf16[256,256]{1,0:T(8,128)(2,1)} %copy-done.4, bf16[256,256]{1,0:T(8,128)(2,1)} %copy-done.3, bf16[256,256]{1,0:T(8,128)(2,1)} %weight_ref.1, ...), custom_call_target="tpu_custom_call" | custom-call | tf_op jit(solution)/shard_map/pallas_call | solution.py:163
  102.5 0.0 collective-permute-start.12
  102.5 2.7 %collective-permute-start.9 = (bf16[256,256]{1,0:T(8,128)(2,1)}, bf16[256,256]{1,0:T(8,128)(2,1)S(1)}, u32[]{:S(2)}, u32[]{:S(2)}) collective-permute-start(bf16[256,256]{1,0:T(8,128)(2,1)} %get-tuple-element.11), channel_id=1, source_target_pairs={{0,224},{32,0},{64,32},{96,64},{128,96},{160,128},{192,160},{224,1... | collective-permute-start | bytes 393224 | tf_op jit(solution)/shard_map/ppermute | solution.py:222
  105.2 2.6 %collective-permute-done.12 = bf16[256,256]{1,0:T(8,128)(2,1)S(1)} collective-permute-done((bf16[256,256]{1,0:T(8,128)(2,1)}, bf16[256,256]{1,0:T(8,128)(2,1)S(1)}, u32[]{:S(2)}, u32[]{:S(2)}) %collective-permute-start.12) | collective-permute-done | bytes 131104 | tf_op jit(solution)/shard_map/ppermute | solution.py:221
  107.7 0.0 collective-permute-start.13
  107.7 2.7 %collective-permute-start.10 = (bf16[256,256]{1,0:T(8,128)(2,1)S(1)}, bf16[256,256]{1,0:T(8,128)(2,1)S(1)}, u32[]{:S(2)}, u32[]{:S(2)}) collective-permute-start(bf16[256,256]{1,0:T(8,128)(2,1)S(1)} %collective-permute-done.9), channel_id=1, source_target_pairs={{0,224},{32,0},{64,32},{96,64},{128,96},{160,128},{192,160},{224,1... | collective-permute-start | bytes 393224 | tf_op jit(solution)/shard_map/ppermute | solution.py:222
  110.4 0.9 constant_dynamic-update-slice_fusion.8
  111.3 1.4 collective-permute-done.13
  112.7 0.0 collective-permute-start.14
  112.8 2.7 %collective-permute-start.11 = (bf16[256,256]{1,0:T(8,128)(2,1)S(1)}, bf16[256,256]{1,0:T(8,128)(2,1)S(1)}, u32[]{:S(2)}, u32[]{:S(2)}) collective-permute-start(bf16[256,256]{1,0:T(8,128)(2,1)S(1)} %collective-permute-done.10), channel_id=1, source_target_pairs={{0,224},{32,0},{64,32},{96,64},{128,96},{160,128},{192,160},{224,1... | collective-permute-start | bytes 393224 | tf_op jit(solution)/shard_map/ppermute | solution.py:222
  115.5 2.3 %collective-permute-done.14 = bf16[256,256]{1,0:T(8,128)(2,1)S(1)} collective-permute-done((bf16[256,256]{1,0:T(8,128)(2,1)S(1)}, bf16[256,256]{1,0:T(8,128)(2,1)S(1)}, u32[]{:S(2)}, u32[]{:S(2)}) %collective-permute-start.14) | collective-permute-done | bytes 131104 | tf_op jit(solution)/shard_map/ppermute | solution.py:221
  117.8 2.7 %collective-permute-start.16 = (bf16[128,256]{1,0:T(8,128)(2,1)S(1)}, bf16[128,256]{1,0:T(8,128)(2,1)S(1)}, u32[]{:S(2)}, u32[]{:S(2)}) collective-permute-start(bf16[128,256]{1,0:T(8,128)(2,1)S(1)} %slice.115), channel_id=1, source_target_pairs={{0,224},{32,0},{64,32},{96,64},{128,96},{160,128},{192,160},{224,1... | collective-permute-start | bytes 196616 | tf_op jit(solution)/shard_map/ppermute | solution.py:228
  120.6 1.5 collective-permute-done.15
  122.2 11.7 %collective-permute-start.17 = (bf16[2048,256]{1,0:T(8,128)(2,1)S(1)}, bf16[2048,256]{1,0:T(8,128)(2,1)S(1)}, u32[]{:S(2)}, u32[]{:S(2)}) collective-permute-start(bf16[2048,256]{1,0:T(8,128)(2,1)S(1)} %constant_dynamic-update-slice_fusion.own_ref), channel_id=1, source_target_pairs={{0,16},{16,0},{1,17},{17,1},{2,18},{18,2},{3,19},{19,3},{4,20},{20... | collective-permute-start | bytes 3145736 | tf_op jit(solution)/shard_map/ppermute | solution.py:233
  133.9 0.1 collective-permute-start.18
  134.0 2.7 %collective-permute-start.20 = (f32[64,256]{1,0:T(8,128)S(1)}, f32[64,256]{1,0:T(8,128)S(1)}, u32[]{:S(2)}, u32[]{:S(2)}) collective-permute-start(f32[64,256]{1,0:T(8,128)S(1)} %get-tuple-element.16), channel_id=1, source_target_pairs={{0,6},{1,7},{8,14},{9,15},{2,0},{3,1},{10,8},{11,9},{4,2},{5,3},{1... | collective-permute-start | bytes 196616 | tf_op jit(solution)/shard_map/ppermute | solution.py:245
  136.6 2.2 %collective-permute-done.18 = f32[64,256]{1,0:T(8,128)S(1)} collective-permute-done((f32[64,256]{1,0:T(8,128)S(1)}, f32[64,256]{1,0:T(8,128)S(1)}, u32[]{:S(2)}, u32[]{:S(2)}) %collective-permute-start.18) | collective-permute-done | bytes 65568 | tf_op jit(solution)/shard_map/ppermute | solution.py:245
  138.8 0.6 collective-permute-done.20
  139.4 1.8 collective-permute-done.19
  141.3 2.7 %collective-permute-start.21 = (f32[16,256]{1,0:T(8,128)S(1)}, f32[16,256]{1,0:T(8,128)S(1)}, u32[]{:S(2)}, u32[]{:S(2)}) collective-permute-start(f32[16,256]{1,0:T(8,128)S(1)} %get-tuple-element.20), channel_id=1, source_target_pairs={{0,1},{1,8},{8,9},{9,0},{2,3},{3,10},{10,11},{11,2},{4,5},{5,12},{... | collective-permute-start | bytes 49160 | tf_op jit(solution)/shard_map/ppermute | solution.py:245
  144.0 2.7 %collective-permute-start.23 = (f32[16,256]{1,0:T(8,128)S(1)}, f32[16,256]{1,0:T(8,128)S(1)}, u32[]{:S(2)}, u32[]{:S(2)}) collective-permute-start(f32[16,256]{1,0:T(8,128)S(1)} %get-tuple-element.21), channel_id=1, source_target_pairs={{0,9},{1,0},{8,1},{9,8},{2,11},{3,2},{10,3},{11,10},{4,13},{5,4},{... | collective-permute-start | bytes 49160 | tf_op jit(solution)/shard_map/ppermute | solution.py:245
  146.7 1.1 collective-permute-start.22
  147.8 3.0 %collective-permute-done.22 = f32[16,256]{1,0:T(8,128)S(1)} collective-permute-done((f32[16,256]{1,0:T(8,128)S(1)}, f32[16,256]{1,0:T(8,128)S(1)}, u32[]{:S(2)}, u32[]{:S(2)}) %collective-permute-start.22) | collective-permute-done | bytes 16416 | tf_op jit(solution)/shard_map/ppermute | solution.py:245
  150.8 3.3 %collective-permute-start.24 = (f32[16,256]{1,0:T(8,128)S(1)}, f32[16,256]{1,0:T(8,128)S(1)}, u32[]{:S(2)}, u32[]{:S(2)}) collective-permute-start(f32[16,256]{1,0:T(8,128)S(1)} %fusion.3), channel_id=1, source_target_pairs={{0,16},{16,0},{1,17},{17,1},{2,18},{18,2},{3,19},{19,3},{4,20},{20... | collective-permute-start | bytes 49160 | tf_op jit(solution)/shard_map/ppermute | solution.py:246
  154.0 0.8 collective-permute-done.24
  154.9 2.6 %collective-permute-done.25 = f32[16,256]{1,0:T(8,128)S(1)} collective-permute-done((f32[16,256]{1,0:T(8,128)S(1)}, f32[16,256]{1,0:T(8,128)S(1)}, u32[]{:S(2)}, u32[]{:S(2)}) %collective-permute-start.25) | collective-permute-done | bytes 16416 | tf_op jit(solution)/shard_map/ppermute | solution.py:249
  157.5 3.5 %collective-permute-done.26 = f32[16,256]{1,0:T(8,128)S(1)} collective-permute-done((f32[16,256]{1,0:T(8,128)S(1)}, f32[16,256]{1,0:T(8,128)S(1)}, u32[]{:S(2)}, u32[]{:S(2)}) %collective-permute-start.26) | collective-permute-done | bytes 16416 | tf_op jit(solution)/shard_map/ppermute | solution.py:249
  161.0 2.6 %collective-permute-start.27 = (f32[16,256]{1,0:T(8,128)S(1)}, f32[16,256]{1,0:T(8,128)S(1)}, u32[]{:S(2)}, u32[]{:S(2)}) collective-permute-start(f32[16,256]{1,0:T(8,128)S(1)} %add.156), channel_id=1, source_target_pairs={{0,128},{32,160},{64,192},{96,224},{128,0},{160,32},{192,64},{224,... | collective-permute-start | bytes 49160 | tf_op jit(solution)/shard_map/ppermute | solution.py:249
  163.5 3.9 %collective-permute-done.27 = f32[16,256]{1,0:T(8,128)S(1)} collective-permute-done((f32[16,256]{1,0:T(8,128)S(1)}, f32[16,256]{1,0:T(8,128)S(1)}, u32[]{:S(2)}, u32[]{:S(2)}) %collective-permute-start.27) | collective-permute-done | bytes 16416 | tf_op jit(solution)/shard_map/ppermute | solution.py:249
  167.5 12.2 %shard_map.88 = bf16[16,272,256]{2,1,0:T(8,128)(2,1)S(1)} custom-call(s32[8,256]{1,0:T(8,128)S(1)} %copy-done.1, s32[2]{0:T(128)S(1)} %pad_add_fusion.place_ref, bf16[256,128,128]{2,1,0:T(8,128)(2,1)} %bitcast.39, bf16[2048,256]{1,0:T(8,128)(2,1)S(1)} %constant_dynamic-update-slice_fusion.own_ref, bf16[2048,256]{1,0:T(8,128)(2,1)S(1)} %collective-permute-done.17.sibling_ref, ...), custom_call_target="tpu_custom_call" | custom-call | tf_op jit(solution)/shard_map/pallas_call | solution.py:131
  179.6 40.1 %all_to_all.10 = bf16[16,272,256]{2,1,0:T(8,128)(2,1)S(1)} all-to-all(bf16[16,272,256]{2,1,0:T(8,128)(2,1)S(1)} %shard_map.88), channel_id=1, replica_groups=mesh['z'=8,'c'=2,'yh'=2,'x'=4,'yl'=2] {'yh','x','yl'}, dimensions={0} | all-to-all | bytes 4456448 | tf_op jit(solution)/shard_map/all_to_all | solution.py:254
  219.8 0.7 copy.9
  220.5 1.0 slice_reduce_fusion
  (42 shorter events, 0.3 us)
Async XLA Ops:
  3.1 38.6 %all-to-all-start = ((bf16[16,256,256]{2,1,0:T(8,128)(2,1)}), bf16[16,256,256]{2,1,0:T(8,128)(2,1)S(1)}, u32[]{:S(2)}, u32[]{:S(2)}) async-start(bf16[16,256,256]{2,1,0:T(8,128)(2,1)} %broadcast_in_dim.2), calls=%async_computation | async-start | bytes 4194304 | tf_op jit(solution)/shard_map/all_to_all | solution.py:195
  41.7 0.7 copy-start
  53.2 4.4 %collective-permute-start = (bf16[2048,256]{1,0:T(8,128)(2,1)S(1)}, bf16[2048,256]{1,0:T(8,128)(2,1)S(1)}, u32[]{:S(2)}, u32[]{:S(2)}) collective-permute-start(bf16[2048,256]{1,0:T(8,128)(2,1)S(1)} %get-tuple-element.9), channel_id=1, source_target_pairs={{0,16},{16,0},{1,17},{17,1},{2,18},{18,2},{3,19},{19,3},{4,20},{20... | collective-permute-start | bytes 3145736 | tf_op jit(solution)/shard_map/ppermute | solution.py:198
  57.6 6.9 %collective-permute-start.5 = (bf16[128,256]{1,0:T(8,128)(2,1)S(1)}, bf16[128,256]{1,0:T(8,128)(2,1)S(1)}, u32[]{:S(2)}, u32[]{:S(2)}) collective-permute-start(bf16[128,256]{1,0:T(8,128)(2,1)S(1)} %get-tuple-element.18), channel_id=1, source_target_pairs={{0,224},{32,0},{64,32},{96,64},{128,96},{160,128},{192,160},{224,1... | collective-permute-start | bytes 196616 | tf_op jit(solution)/shard_map/ppermute | solution.py:209
  64.6 10.5 %collective-permute-start.6 = (bf16[256,256]{1,0:T(8,128)(2,1)S(1)}, bf16[256,256]{1,0:T(8,128)(2,1)S(1)}, u32[]{:S(2)}, u32[]{:S(2)}) collective-permute-start(bf16[256,256]{1,0:T(8,128)(2,1)S(1)} %add_convert_fusion.2), channel_id=1, source_target_pairs={{0,224},{32,0},{64,32},{96,64},{128,96},{160,128},{192,160},{224,1... | collective-permute-start | bytes 393224 | tf_op jit(solution)/shard_map/ppermute | solution.py:214
  75.1 6.9 %collective-permute-start.7 = (bf16[256,256]{1,0:T(8,128)(2,1)S(1)}, bf16[256,256]{1,0:T(8,128)(2,1)S(1)}, u32[]{:S(2)}, u32[]{:S(2)}) collective-permute-start(bf16[256,256]{1,0:T(8,128)(2,1)S(1)} %add_convert_fusion.1), channel_id=1, source_target_pairs={{0,224},{32,0},{64,32},{96,64},{128,96},{160,128},{192,160},{224,1... | collective-permute-start | bytes 393224 | tf_op jit(solution)/shard_map/ppermute | solution.py:214
  77.7 4.3 %collective-permute-start.1 = (bf16[128,256]{1,0:T(8,128)(2,1)S(1)}, bf16[128,256]{1,0:T(8,128)(2,1)S(1)}, u32[]{:S(2)}, u32[]{:S(2)}) collective-permute-start(bf16[128,256]{1,0:T(8,128)(2,1)S(1)} %get-tuple-element.19), channel_id=1, source_target_pairs={{0,32},{32,64},{64,96},{96,128},{128,160},{160,192},{192,224},{224... | collective-permute-start | bytes 196616 | tf_op jit(solution)/shard_map/ppermute | solution.py:208
  82.1 5.1 %collective-permute-start.2 = (bf16[256,256]{1,0:T(8,128)(2,1)S(1)}, bf16[256,256]{1,0:T(8,128)(2,1)S(1)}, u32[]{:S(2)}, u32[]{:S(2)}) collective-permute-start(bf16[256,256]{1,0:T(8,128)(2,1)S(1)} %get-tuple-element.14), channel_id=1, source_target_pairs={{0,32},{32,64},{64,96},{96,128},{128,160},{160,192},{192,224},{224... | collective-permute-start | bytes 393224 | tf_op jit(solution)/shard_map/ppermute | solution.py:213
  87.3 5.6 %collective-permute-start.3 = (bf16[256,256]{1,0:T(8,128)(2,1)S(1)}, bf16[256,256]{1,0:T(8,128)(2,1)S(1)}, u32[]{:S(2)}, u32[]{:S(2)}) collective-permute-start(bf16[256,256]{1,0:T(8,128)(2,1)S(1)} %add_convert_fusion.4), channel_id=1, source_target_pairs={{0,32},{32,64},{64,96},{96,128},{128,160},{160,192},{192,224},{224... | collective-permute-start | bytes 393224 | tf_op jit(solution)/shard_map/ppermute | solution.py:213
  87.4 7.0 %collective-permute-start.8 = (bf16[256,256]{1,0:T(8,128)(2,1)S(1)}, bf16[256,256]{1,0:T(8,128)(2,1)S(1)}, u32[]{:S(2)}, u32[]{:S(2)}) collective-permute-start(bf16[256,256]{1,0:T(8,128)(2,1)S(1)} %get-tuple-element.13), channel_id=1, source_target_pairs={{0,224},{32,0},{64,32},{96,64},{128,96},{160,128},{192,160},{224,1... | collective-permute-start | bytes 393224 | tf_op jit(solution)/shard_map/ppermute | solution.py:214
  93.0 6.5 %collective-permute-start.4 = (bf16[256,256]{1,0:T(8,128)(2,1)S(1)}, bf16[256,256]{1,0:T(8,128)(2,1)S(1)}, u32[]{:S(2)}, u32[]{:S(2)}) collective-permute-start(bf16[256,256]{1,0:T(8,128)(2,1)S(1)} %add_convert_fusion.3), channel_id=1, source_target_pairs={{0,32},{32,64},{64,96},{96,128},{128,160},{160,192},{192,224},{224... | collective-permute-start | bytes 393224 | tf_op jit(solution)/shard_map/ppermute | solution.py:213
  94.4 73.1 %copy-start.1 = (s32[8,256]{1,0:T(8,128)S(1)}, s32[8,256]{1,0:T(8,128)}, u32[]{:S(2)}) copy-start(s32[8,256]{1,0:T(8,128)} %shard_map.85.table_ref) | copy-start | bytes 24580
  94.4 5.1 %copy-start.3 = (bf16[256,256]{1,0:T(8,128)(2,1)}, bf16[256,256]{1,0:T(8,128)(2,1)S(1)}, u32[]{:S(2)}) copy-start(bf16[256,256]{1,0:T(8,128)(2,1)S(1)} %collective-permute-done.8.down_ref) | copy-start | bytes 393220
  99.5 0.7 copy-start.4
  102.5 31.4 %copy-start.2 = (f32[256,256]{1,0:T(8,128)S(1)}, f32[256,256]{1,0:T(8,128)}, u32[]{:S(2)}) copy-start(f32[256,256]{1,0:T(8,128)} %get-tuple-element.12) | copy-start | bytes 786436
  102.5 5.2 %collective-permute-start.12 = (bf16[256,256]{1,0:T(8,128)(2,1)}, bf16[256,256]{1,0:T(8,128)(2,1)S(1)}, u32[]{:S(2)}, u32[]{:S(2)}) collective-permute-start(bf16[256,256]{1,0:T(8,128)(2,1)} %get-tuple-element.11), channel_id=1, source_target_pairs={{0,32},{32,64},{64,96},{96,128},{128,160},{160,192},{192,224},{224... | collective-permute-start | bytes 393224 | tf_op jit(solution)/shard_map/ppermute | solution.py:221
  102.5 5.2 %collective-permute-start.9 = (bf16[256,256]{1,0:T(8,128)(2,1)}, bf16[256,256]{1,0:T(8,128)(2,1)S(1)}, u32[]{:S(2)}, u32[]{:S(2)}) collective-permute-start(bf16[256,256]{1,0:T(8,128)(2,1)} %get-tuple-element.11), channel_id=1, source_target_pairs={{0,224},{32,0},{64,32},{96,64},{128,96},{160,128},{192,160},{224,1... | collective-permute-start | bytes 393224 | tf_op jit(solution)/shard_map/ppermute | solution.py:222
  107.7 5.0 %collective-permute-start.13 = (bf16[256,256]{1,0:T(8,128)(2,1)S(1)}, bf16[256,256]{1,0:T(8,128)(2,1)S(1)}, u32[]{:S(2)}, u32[]{:S(2)}) collective-permute-start(bf16[256,256]{1,0:T(8,128)(2,1)S(1)} %collective-permute-done.12), channel_id=1, source_target_pairs={{0,32},{32,64},{64,96},{96,128},{128,160},{160,192},{192,224},{224... | collective-permute-start | bytes 393224 | tf_op jit(solution)/shard_map/ppermute | solution.py:221
  107.7 5.0 %collective-permute-start.10 = (bf16[256,256]{1,0:T(8,128)(2,1)S(1)}, bf16[256,256]{1,0:T(8,128)(2,1)S(1)}, u32[]{:S(2)}, u32[]{:S(2)}) collective-permute-start(bf16[256,256]{1,0:T(8,128)(2,1)S(1)} %collective-permute-done.9), channel_id=1, source_target_pairs={{0,224},{32,0},{64,32},{96,64},{128,96},{160,128},{192,160},{224,1... | collective-permute-start | bytes 393224 | tf_op jit(solution)/shard_map/ppermute | solution.py:222
  112.7 5.0 %collective-permute-start.14 = (bf16[256,256]{1,0:T(8,128)(2,1)S(1)}, bf16[256,256]{1,0:T(8,128)(2,1)S(1)}, u32[]{:S(2)}, u32[]{:S(2)}) collective-permute-start(bf16[256,256]{1,0:T(8,128)(2,1)S(1)} %collective-permute-done.13), channel_id=1, source_target_pairs={{0,32},{32,64},{64,96},{96,128},{128,160},{160,192},{192,224},{224... | collective-permute-start | bytes 393224 | tf_op jit(solution)/shard_map/ppermute | solution.py:221
  112.8 5.0 %collective-permute-start.11 = (bf16[256,256]{1,0:T(8,128)(2,1)S(1)}, bf16[256,256]{1,0:T(8,128)(2,1)S(1)}, u32[]{:S(2)}, u32[]{:S(2)}) collective-permute-start(bf16[256,256]{1,0:T(8,128)(2,1)S(1)} %collective-permute-done.10), channel_id=1, source_target_pairs={{0,224},{32,0},{64,32},{96,64},{128,96},{160,128},{192,160},{224,1... | collective-permute-start | bytes 393224 | tf_op jit(solution)/shard_map/ppermute | solution.py:222
  117.8 4.3 %collective-permute-start.15 = (bf16[128,256]{1,0:T(8,128)(2,1)S(1)}, bf16[128,256]{1,0:T(8,128)(2,1)S(1)}, u32[]{:S(2)}, u32[]{:S(2)}) collective-permute-start(bf16[128,256]{1,0:T(8,128)(2,1)S(1)} %slice.114), channel_id=1, source_target_pairs={{0,32},{32,64},{64,96},{96,128},{128,160},{160,192},{192,224},{224... | collective-permute-start | bytes 196616 | tf_op jit(solution)/shard_map/ppermute | solution.py:227
  117.8 4.3 %collective-permute-start.16 = (bf16[128,256]{1,0:T(8,128)(2,1)S(1)}, bf16[128,256]{1,0:T(8,128)(2,1)S(1)}, u32[]{:S(2)}, u32[]{:S(2)}) collective-permute-start(bf16[128,256]{1,0:T(8,128)(2,1)S(1)} %slice.115), channel_id=1, source_target_pairs={{0,224},{32,0},{64,32},{96,64},{128,96},{160,128},{192,160},{224,1... | collective-permute-start | bytes 196616 | tf_op jit(solution)/shard_map/ppermute | solution.py:228
  122.2 45.3 %collective-permute-start.17 = (bf16[2048,256]{1,0:T(8,128)(2,1)S(1)}, bf16[2048,256]{1,0:T(8,128)(2,1)S(1)}, u32[]{:S(2)}, u32[]{:S(2)}) collective-permute-start(bf16[2048,256]{1,0:T(8,128)(2,1)S(1)} %constant_dynamic-update-slice_fusion.own_ref), channel_id=1, source_target_pairs={{0,16},{16,0},{1,17},{17,1},{2,18},{18,2},{3,19},{19,3},{4,20},{20... | collective-permute-start | bytes 3145736 | tf_op jit(solution)/shard_map/ppermute | solution.py:233
  133.9 5.0 %collective-permute-start.18 = (f32[64,256]{1,0:T(8,128)S(1)}, f32[64,256]{1,0:T(8,128)S(1)}, u32[]{:S(2)}, u32[]{:S(2)}) collective-permute-start(f32[64,256]{1,0:T(8,128)S(1)} %get-tuple-element.15), channel_id=1, source_target_pairs={{0,2},{1,3},{8,10},{9,11},{2,4},{3,5},{10,12},{11,13},{4,6},{5,7},... | collective-permute-start | bytes 196616 | tf_op jit(solution)/shard_map/ppermute | solution.py:245
  134.0 5.5 %collective-permute-start.20 = (f32[64,256]{1,0:T(8,128)S(1)}, f32[64,256]{1,0:T(8,128)S(1)}, u32[]{:S(2)}, u32[]{:S(2)}) collective-permute-start(f32[64,256]{1,0:T(8,128)S(1)} %get-tuple-element.16), channel_id=1, source_target_pairs={{0,6},{1,7},{8,14},{9,15},{2,0},{3,1},{10,8},{11,9},{4,2},{5,3},{1... | collective-permute-start | bytes 196616 | tf_op jit(solution)/shard_map/ppermute | solution.py:245
  136.6 4.6 %collective-permute-start.19 = (f32[64,256]{1,0:T(8,128)S(1)}, f32[64,256]{1,0:T(8,128)S(1)}, u32[]{:S(2)}, u32[]{:S(2)}) collective-permute-start(f32[64,256]{1,0:T(8,128)S(1)} %get-tuple-element.17), channel_id=1, source_target_pairs={{0,4},{1,5},{8,12},{9,13},{2,6},{3,7},{10,14},{11,15},{4,0},{5,1},... | collective-permute-start | bytes 196616 | tf_op jit(solution)/shard_map/ppermute | solution.py:245
  141.3 6.5 %collective-permute-start.21 = (f32[16,256]{1,0:T(8,128)S(1)}, f32[16,256]{1,0:T(8,128)S(1)}, u32[]{:S(2)}, u32[]{:S(2)}) collective-permute-start(f32[16,256]{1,0:T(8,128)S(1)} %get-tuple-element.20), channel_id=1, source_target_pairs={{0,1},{1,8},{8,9},{9,0},{2,3},{3,10},{10,11},{11,2},{4,5},{5,12},{... | collective-permute-start | bytes 49160 | tf_op jit(solution)/shard_map/ppermute | solution.py:245
  144.0 3.8 %collective-permute-start.23 = (f32[16,256]{1,0:T(8,128)S(1)}, f32[16,256]{1,0:T(8,128)S(1)}, u32[]{:S(2)}, u32[]{:S(2)}) collective-permute-start(f32[16,256]{1,0:T(8,128)S(1)} %get-tuple-element.21), channel_id=1, source_target_pairs={{0,9},{1,0},{8,1},{9,8},{2,11},{3,2},{10,3},{11,10},{4,13},{5,4},{... | collective-permute-start | bytes 49160 | tf_op jit(solution)/shard_map/ppermute | solution.py:245
  146.7 4.1 %collective-permute-start.22 = (f32[16,256]{1,0:T(8,128)S(1)}, f32[16,256]{1,0:T(8,128)S(1)}, u32[]{:S(2)}, u32[]{:S(2)}) collective-permute-start(f32[16,256]{1,0:T(8,128)S(1)} %get-tuple-element.22), channel_id=1, source_target_pairs={{0,8},{1,9},{8,0},{9,1},{2,10},{3,11},{10,2},{11,3},{4,12},{5,13},... | collective-permute-start | bytes 49160 | tf_op jit(solution)/shard_map/ppermute | solution.py:245
  150.8 4.1 %collective-permute-start.24 = (f32[16,256]{1,0:T(8,128)S(1)}, f32[16,256]{1,0:T(8,128)S(1)}, u32[]{:S(2)}, u32[]{:S(2)}) collective-permute-start(f32[16,256]{1,0:T(8,128)S(1)} %fusion.3), channel_id=1, source_target_pairs={{0,16},{16,0},{1,17},{17,1},{2,18},{18,2},{3,19},{19,3},{4,20},{20... | collective-permute-start | bytes 49160 | tf_op jit(solution)/shard_map/ppermute | solution.py:246
  154.9 2.6 %collective-permute-start.25 = (f32[16,256]{1,0:T(8,128)S(1)}, f32[16,256]{1,0:T(8,128)S(1)}, u32[]{:S(2)}, u32[]{:S(2)}) collective-permute-start(f32[16,256]{1,0:T(8,128)S(1)} %add.154), channel_id=1, source_target_pairs={{0,32},{32,0},{64,96},{96,64},{128,160},{160,128},{192,224},{224,1... | collective-permute-start | bytes 49160 | tf_op jit(solution)/shard_map/ppermute | solution.py:249
  157.5 3.5 %collective-permute-start.26 = (f32[16,256]{1,0:T(8,128)S(1)}, f32[16,256]{1,0:T(8,128)S(1)}, u32[]{:S(2)}, u32[]{:S(2)}) collective-permute-start(f32[16,256]{1,0:T(8,128)S(1)} %add.155), channel_id=1, source_target_pairs={{0,64},{32,96},{64,0},{96,32},{128,192},{160,224},{192,128},{224,1... | collective-permute-start | bytes 49160 | tf_op jit(solution)/shard_map/ppermute | solution.py:249
  161.0 6.5 %collective-permute-start.27 = (f32[16,256]{1,0:T(8,128)S(1)}, f32[16,256]{1,0:T(8,128)S(1)}, u32[]{:S(2)}, u32[]{:S(2)}) collective-permute-start(f32[16,256]{1,0:T(8,128)S(1)} %add.156), channel_id=1, source_target_pairs={{0,128},{32,160},{64,192},{96,224},{128,0},{160,32},{192,64},{224,... | collective-permute-start | bytes 49160 | tf_op jit(solution)/shard_map/ppermute | solution.py:249

commit v2 on v0

v2 whole, which is shorter than its diff:
```python
import functools
import math

import jax
import jax.numpy as jnp
from jax import lax
from jax.experimental import pallas as pl
from jax.experimental.pallas import tpu as pltpu
from jax.sharding import Mesh, PartitionSpec as P

BLK = 128
QUAD = 4
QUADS_A_STEP = 4
PARTS = 8
TABLE = 384
PLANE = ("yh", "x", "yl")
BF16 = jnp.bfloat16
F32 = jnp.float32
VMEM_LIMIT = 24 * 1024 * 1024
SMALL_LIMIT = 8 * 1024 * 1024
VMEM = pl.BlockSpec(memory_space=pltpu.VMEM)
SMEM = pl.BlockSpec(memory_space=pltpu.SMEM)


def slot_tables_kernel(sizes, coords_ref, count_ref, place_ref, table_ref):
    depth, nx, ny = sizes
    slots = coords_ref.shape[1]
    at_z, at_c, at_x, at_y = (place_ref[i] for i in range(4))
    row = coords_ref[0:1, :]
    col = coords_ref[1:2, :]
    away = jnp.bitwise_and((row >> 2) - at_z, depth - 1)
    line_row = jnp.where(jnp.bitwise_and(row >> 1, 1) == at_c, 2 * depth, 0) + away * 2 + jnp.bitwise_and(row, 1)
    rank = col >> 1
    col_x = jnp.bitwise_and(rank >> 1, nx - 1)
    col_y = rank // (2 * nx) * 2 + jnp.bitwise_and(rank, 1)
    off_x = jnp.bitwise_and(col_x - at_x, nx - 1)
    off_y = jnp.bitwise_and(col_y - at_y, ny - 1)
    line_col = (off_y * nx + off_x) * 2 + jnp.bitwise_and(col, 1)
    lines = jnp.concatenate([line_row, line_col, jnp.zeros((6, slots), jnp.int32)], axis=0).astype(F32)
    columns = jnp.transpose(lines)
    filled = count_ref[0]

    def iota(width, axis):
        return lax.broadcasted_iota(jnp.int32, (slots, width), axis)

    lane, sublane = iota(slots, 1), iota(slots, 0)
    rows = []
    for by in range(2):
        key = jnp.where(iota(1, 0) < filled, columns[:, by : by + 1], 99.0)
        key_lane = jnp.where(lane < filled, jnp.broadcast_to(lines[by : by + 1], (slots, slots)), 99.0)
        key_sub = jnp.broadcast_to(key, (slots, slots))
        ahead = (key_lane == key_sub) & (lane < sublane)
        order = jnp.sum(ahead.astype(F32), axis=1, keepdims=True)
        spot = iota(BLK, 1).astype(F32)
        key_spot = jnp.broadcast_to(key, (slots, BLK))
        held = jnp.sum((key_spot == spot).astype(F32), axis=0, keepdims=True)
        quads = jnp.where(spot[:1] < 99.0, jnp.floor((held + (QUAD - 1)) * (1.0 / QUAD)), 0.0)
        before = jnp.where(spot < key_spot, jnp.broadcast_to(quads, (slots, BLK)), 0.0)
        entry = jnp.sum(before, axis=1, keepdims=True) * QUAD + order
        target = iota(TABLE, 1).astype(F32)
        active = iota(TABLE, 0) < filled
        here = (jnp.broadcast_to(entry, (slots, TABLE)) == target) & active

        def placed(value):
            return jnp.sum(jnp.where(here, jnp.broadcast_to(value, (slots, TABLE)), 0.0), axis=0, keepdims=True)

        rows.append(placed(iota(1, 0).astype(F32) + 1.0))
        rows.append(placed(columns[:, 1 - by : 2 - by]))
        rows.append(placed(columns[:, by : by + 1]))
        whole = jnp.sum(quads, axis=1, keepdims=True)
        first = jnp.sum(jnp.where(spot[:1] < 2 * depth, quads, 0.0), axis=1, keepdims=True)
        which = lax.broadcasted_iota(jnp.int32, (1, TABLE), 1)
        rows.append(jnp.where(which == 0, jnp.broadcast_to(whole, (1, TABLE)), jnp.broadcast_to(first, (1, TABLE))))
    table_ref[...] = jnp.concatenate(rows, axis=0).astype(jnp.int32)


def slot_tables(coords, count, place, sizes):
    return pl.pallas_call(
        functools.partial(slot_tables_kernel, sizes),
        out_shape=jax.ShapeDtypeStruct((8, TABLE), jnp.int32),
        in_specs=[VMEM, SMEM, SMEM],
        out_specs=VMEM,
        compiler_params=pltpu.CompilerParams(vmem_limit_bytes=SMALL_LIMIT),
    )(coords, count, place)


def add_quads(table_ref, base, begin, end, first_line, blocks_ref, source_ref, total_ref, contract):
    def quad(at):
        inside = at < end
        parts = []
        for u in range(QUAD):
            tag = table_ref[base, at * QUAD + u]
            block = blocks_ref[jnp.maximum(tag - 1, 0)]
            valid = jnp.logical_and(inside, tag > 0)
            parts.append(
                (jnp.where(valid, block, jnp.zeros_like(block)), source_ref[table_ref[base + 1, at * QUAD + u]])
            )
        product = None
        for u in range(0, QUAD, 2):
            left = jnp.concatenate([parts[u][0], parts[u + 1][0]], axis=contract)
            right = jnp.concatenate([parts[u][1], parts[u + 1][1]], axis=0)
            term = lax.dot_general(left, right, (((contract,), (0,)), ((), ())), preferred_element_type=F32)
            product = term if product is None else product + term
        line = jnp.where(inside, table_ref[base + 2, at * QUAD] - first_line, 0)
        return line, product

    @pl.loop(0, (end - begin + QUADS_A_STEP - 1) // QUADS_A_STEP)
    def _(i):
        found = [quad(begin + i * QUADS_A_STEP + j) for j in range(QUADS_A_STEP)]
        for line, product in found:
            total_ref[line] += product


def forward_kernel(own_half, sizes, table_ref, blocks_ref, *refs):
    depth, nx, ny = sizes
    *piece_refs, out_ref, source_ref, total_ref = refs
    lanes = piece_refs[0].shape[-1]
    for oy in range(ny):
        for ox in range(nx):
            for h in range(2):
                for half, major, minor in ((0, oy, ox), (1, ox, oy)):
                    piece = piece_refs[half * ny + major]
                    source_ref[(oy * nx + ox) * 2 + h, :, half * lanes : (half + 1) * lanes] = piece[
                        pl.ds((minor * 2 + h) * BLK, BLK), :
                    ]
    total_ref[...] = jnp.zeros_like(total_ref)
    whole, first = table_ref[3, 0], table_ref[3, 1]
    begin, end, line = (first, whole, 2 * depth) if own_half else (0, first, 0)
    add_quads(table_ref, 0, begin, end, line, blocks_ref, source_ref, total_ref, 1)
    out_ref[...] = total_ref[...].astype(BF16)


def forward_product(own_half, table, blocks, pieces, sizes):
    depth, nx, ny = sizes
    width = 2 * pieces[0].shape[-1]
    lines = 2 * depth
    return pl.pallas_call(
        functools.partial(forward_kernel, own_half, sizes),
        out_shape=jax.ShapeDtypeStruct((lines, BLK, width), BF16),
        in_specs=[SMEM] + [VMEM] * (1 + len(pieces)),
        out_specs=VMEM,
        scratch_shapes=[
            pltpu.VMEM((nx * ny * 2, BLK, width), BF16),
            pltpu.VMEM((lines, BLK, width), F32),
        ],
        compiler_params=pltpu.CompilerParams(vmem_limit_bytes=VMEM_LIMIT),
    )(table, blocks, *pieces)


def backward_kernel(sizes, table_ref, place_ref, blocks_ref, sibling_ref, own_ref, tail_ref, out_ref, source_ref, total_ref):
    depth, nx, ny = sizes
    source_ref[0 : 2 * depth] = sibling_ref[...]
    source_ref[2 * depth :] = own_ref[...]
    total_ref[...] = jnp.zeros_like(total_ref)
    add_quads(table_ref, 4, 0, table_ref[7, 0], 0, blocks_ref, source_ref, total_ref, 0)
    at_x, at_y = place_ref[2], place_ref[3]
    local = 2 * BLK
    for oy in range(ny):
        for ox in range(nx):
            y = jnp.bitwise_and(at_y + oy, ny - 1)
            rank = (y // 2 * nx + jnp.bitwise_and(at_x + ox, nx - 1)) * 2 + jnp.bitwise_and(y, 1)
            for h in range(2):
                out_ref[rank, h * BLK : (h + 1) * BLK, :] = total_ref[(oy * nx + ox) * 2 + h].astype(BF16)
            out_ref[rank, local:, :] = tail_ref[...]


def backward_product(table, place, blocks, sibling, own, tail, sizes):
    depth, nx, ny = sizes
    lines, _, width = own.shape
    return pl.pallas_call(
        functools.partial(backward_kernel, sizes),
        out_shape=jax.ShapeDtypeStruct((nx * ny, 2 * BLK + tail.shape[0], width), BF16),
        in_specs=[SMEM] * 2 + [VMEM] * 4,
        out_specs=VMEM,
        scratch_shapes=[
            pltpu.VMEM((2 * lines, BLK, width), BF16),
            pltpu.VMEM((nx * ny * 2, BLK, width), F32),
        ],
        compiler_params=pltpu.CompilerParams(vmem_limit_bytes=VMEM_LIMIT),
    )(table, place, blocks, sibling, own, tail)


def hold_kernel(count_ref, blocks_ref, held_ref, sem):
    size = blocks_ref.shape[0] // PARTS
    filled = count_ref[0]

    def part(i):
        at = pl.ds(i * size, size)
        return pltpu.make_async_copy(blocks_ref.at[at], held_ref.at[at], sem.at[i])

    for i in range(PARTS):

        @pl.when(filled > i * size)
        def _(i=i):
            part(i).start()

        @pl.when(filled <= i * size)
        def _(i=i):
            held_ref[pl.ds(i * size, size)] = jnp.zeros((size, *held_ref.shape[1:]), held_ref.dtype)

    for i in range(PARTS):

        @pl.when(filled > i * size)
        def _(i=i):
            part(i).wait()


def hold_blocks(blocks, count):
    return pl.pallas_call(
        hold_kernel,
        out_shape=pltpu.VMEM(blocks.shape, blocks.dtype),
        in_specs=[SMEM, pl.BlockSpec(memory_space=pltpu.MemorySpace.HBM)],
        out_specs=VMEM,
        scratch_shapes=[pltpu.SemaphoreType.DMA((PARTS,))],
        compiler_params=pltpu.CompilerParams(vmem_limit_bytes=VMEM_LIMIT),
    )(count, pltpu.with_memory_space_constraint(blocks, pltpu.MemorySpace.HBM))


def dense_kernel(mixed_ref, weight_ref, cotangent_ref, hidden_ref, grad_ref, part_ref):
    mixed = mixed_ref[...]
    weight = weight_ref[...]
    pre_act = jnp.dot(mixed, weight, preferred_element_type=F32)
    sigma = jax.nn.sigmoid(pre_act)
    hidden_ref[...] = (pre_act * sigma).astype(BF16)
    slope = sigma * (1.0 + pre_act * (1.0 - sigma))
    act_grad = (cotangent_ref[...].astype(F32) * slope).astype(BF16)
    grad_ref[...] = lax.dot_general(
        act_grad, weight, (((1,), (1,)), ((), ())), preferred_element_type=F32
    ).astype(BF16)
    part_ref[...] = lax.dot_general(
        mixed, act_grad, (((0,), (0,)), ((), ())), preferred_element_type=F32
    )


def dense(mixed, weight, cotangent):
    shape = cotangent.shape
    return pl.pallas_call(
        dense_kernel,
        out_shape=(
            jax.ShapeDtypeStruct(shape, BF16),
            jax.ShapeDtypeStruct(shape, BF16),
            jax.ShapeDtypeStruct(weight.shape, F32),
        ),
        compiler_params=pltpu.CompilerParams(vmem_limit_bytes=SMALL_LIMIT),
    )(mixed, weight, cotangent)


def last_sums_kernel(nx, ny, scale, arrived_ref, feature_ref, weight_ref):
    local = feature_ref.shape[0]
    share = arrived_ref.shape[1] - local
    value = arrived_ref[0, 0:local, :].astype(F32)
    for i in range(1, nx * ny):
        value = value + arrived_ref[i, 0:local, :].astype(F32)
    feature_ref[...] = value.astype(BF16)
    for y in range(ny):
        for x in range(nx):
            rank = (y // 2 * nx + x) * 2 + y % 2
            at = (x * ny + y) * share
            weight_ref[at : at + share, :] = arrived_ref[rank, local:, :].astype(F32) * scale


def last_sums(arrived, local, weight_shape, node_total, sizes):
    _, nx, ny = sizes
    return pl.pallas_call(
        functools.partial(last_sums_kernel, nx, ny, 1.0 / math.sqrt(node_total)),
        out_shape=(
            jax.ShapeDtypeStruct((local, weight_shape[1]), BF16),
            jax.ShapeDtypeStruct(weight_shape, F32),
        ),
        in_specs=[VMEM],
        out_specs=(VMEM,) * 2,
        compiler_params=pltpu.CompilerParams(vmem_limit_bytes=VMEM_LIMIT),
    )(arrived)


def body(sizes, node_features, weight, cotangent, adjacency_blocks, block_coords, block_counts):
    depth, nx, ny = sizes
    together = lax.optimization_barrier
    local, width = node_features.shape
    lanes = width // 2
    node_total = local * nx * ny * depth * 2
    at_x = lax.axis_index("x")
    at_y = lax.axis_index("yh") * 2 + lax.axis_index("yl")
    place = jnp.stack([lax.axis_index("z"), lax.axis_index("c"), at_x, at_y]).astype(jnp.int32)
    count = block_counts.reshape(1)

    def rank(x, y):
        return ((y % ny) // 2 * nx + x % nx) * 2 + y % 2

    def send(value, dx, dy):
        pairs = [(rank(x, y), rank(x + dx, y + dy)) for x in range(nx) for y in range(ny)]
        return lax.ppermute(value, PLANE, pairs)

    def climb(value, dz):
        return lax.ppermute(value, "z", [(i, (i + dz) % depth) for i in range(depth)])

    def swap(value, dz=0, core=True):
        pairs = [(z * 2 + c, (z ^ dz) * 2 + (c ^ int(core))) for z in range(depth) for c in range(2)]
        return lax.ppermute(value, ("z", "c"), pairs)

    with jax.named_scope("gather_features"):
        upright, level = node_features[:, :lanes], node_features[:, lanes:]
        got = together(
            tuple(send(upright, -o, 0) for o in range(1, nx)) + tuple(send(level, 0, -o) for o in range(1, ny))
        )
        upright = jnp.concatenate((upright,) + got[: nx - 1], axis=0)
        level = jnp.concatenate((level,) + got[nx - 1 :], axis=0)
        got = together(
            tuple(send(upright, 0, -o) for o in range(1, ny)) + tuple(send(level, -o, 0) for o in range(1, nx))
        )
        pieces = (upright,) + got[: ny - 1] + (level,) + got[ny - 1 :]

    with jax.named_scope("tables"):
        table = slot_tables(block_coords[0, 0], count, place, sizes)
        table, early = together((table, count))
        blocks = hold_blocks(adjacency_blocks[0, 0], early)

    with jax.named_scope("forward"):
        for_sibling = forward_product(False, table, blocks, pieces, sizes)
        sibling = swap(for_sibling)
        own = forward_product(True, table, blocks, pieces, sizes)
        sibling, own = together((sibling, own))
        own = own.reshape(depth, local, width)
        sibling = sibling.reshape(depth, local, width)

    def term(step):
        return own[step].astype(F32) + sibling[step].astype(F32)

    with jax.named_scope("sum_rows"):
        half = local // 2
        middle = depth // 2
        far = term(middle).astype(BF16)
        up, down = together((climb(far[:half], 1), climb(far[half:], -1)))
        up = jnp.concatenate([up, jnp.zeros_like(up)], axis=0)
        down = jnp.concatenate([jnp.zeros_like(down), down], axis=0)
        for step in range(middle - 1, 0, -1):
            up, down = together(
                ((term(step) + up.astype(F32)).astype(BF16), (term(depth - step) + down.astype(F32)).astype(BF16))
            )
            up, down = together((climb(up, 1), climb(down, -1)))
        mixed = (term(0) + (up.astype(F32) + down.astype(F32))).astype(BF16)

    with jax.named_scope("dense"):
        hidden, mixed_grad, weight_part = dense(mixed, weight, cotangent)

    with jax.named_scope("gather_rows"):

        def shares(value, at, size):
            cut = value.reshape(size, -1, width)
            return [lax.dynamic_index_in_dim(cut, lax.rem(at + d, size), 0, keepdims=False) for d in range(size)]

        chunks = {0: mixed_grad}
        ahead = behind = mixed_grad
        part = weight_part
        for step in range(1, middle + 1):
            if step > 1:
                part, ahead, behind = together((part, ahead, behind))
            if step < middle:
                moved = (climb(ahead, 1), climb(behind, -1))
            else:
                moved = (climb(ahead[:half], 1), climb(behind[half:], -1))
            if step == 1:
                cut = shares(part, at_x, nx)
                extra = [send(cut[d], d, 0) for d in range(1, nx)]
                part = cut[0] + (extra[0] + extra[1] + extra[2])
            elif step == 2:
                cut = shares(part, at_y, ny)
                extra = [send(cut[d], 0, d) for d in range(1, ny)]
                part = cut[0] + (extra[0] + extra[1] + extra[2])
            elif step == 3:
                part = part + swap(part)
                part = part + swap(part, 1, False)
            else:
                part = part + swap(part, 2, False)
            ahead, behind = together(moved)
            if step < middle:
                chunks[depth - step] = ahead
                chunks[step] = behind
        chunks[middle] = jnp.concatenate([ahead, behind], axis=0)
        own_panel = jnp.concatenate([chunks[step] for step in range(depth)], axis=0)
        own_panel = own_panel.reshape(2 * depth, BLK, width)
        part, own_panel, late = together((part, own_panel, count))
        sibling_panel = swap(own_panel)
        part = part + swap(part, 4, False)
        blocks = hold_blocks(adjacency_blocks[0, 0], late)
        tail = part.astype(BF16)

    with jax.named_scope("backward"):
        outs = backward_product(table, place, blocks, sibling_panel, own_panel, tail, sizes)

    with jax.named_scope("sum_columns"):
        arrived = lax.all_to_all(outs, PLANE, 0, 0, tiled=True)
        feature_grad, weight_grad = last_sums(arrived, local, weight.shape, node_total, sizes)
    return (hidden, weight_grad, feature_grad)


def solution(mesh):
    depth = mesh.shape["row"] // 2
    nx = mesh.shape["col"] // 2
    ny = mesh.shape["rep"] * 2
    fine = Mesh(mesh.devices.reshape(depth, 2, ny // 2, nx, 2), ("z", "c", "yh", "x", "yl"))
    row = ("z", "c")
    in_specs = (
        P((*row, *PLANE), None),
        P(),
        P((*PLANE, *row), None),
        P(PLANE, row, None, None, None),
        P(PLANE, row, None, None),
        P(PLANE, row),
    )
    out_specs = (P((*PLANE, *row), None), P(), P((*row, *PLANE), None))
    return jax.shard_map(
        functools.partial(body, (depth, nx, ny)),
        mesh=fine,
        in_specs=in_specs,
        out_specs=out_specs,
        check_vma=False,
    )
```

time: 643 us -> 165 us (0.26); the launches traced: 634 us -> 165 us
  waiting for transfers between devices: 391 us -> 38.4 us
  local copies, waits for them, and re-layouts: 116 us -> 1.7 us
  matrix products: 104 us -> 0 us
  starting transfers between devices: 0.38 us -> 72.9 us
  blocking collectives: 0 us -> 36.1 us
  Pallas kernels: 0 us -> 13.7 us
  between operations: 14.5 us -> 1.61 us
    psum x1 -> x0, waiting for transfers between devices: 148 us -> none  [body(): lax.psum(weight_part, ('row', 'col', 'rep')) / math.sqrt(node_total)]
    reduce_scatter x2 -> x0, waiting for transfers between devices: 141 us -> none  [the longest x1 74.5 us: body(): lax.psum_scatter(back_terms.astype(jnp.bfloat16), ('col', 'rep'), scatter...]
    dot_general x19 -> x0, matrix products: 104 us -> none  [the longest x8 68 us: accumulate(): lax.dot_general(placing, flat, (((0,), (0,)), ((), ())), precision=lax.Pr...]
    all_gather x2 -> x0, waiting for transfers between devices: 102 us -> none  [the longest x1 73.2 us: body(): lax.all_gather(node_features, ('col', 'rep'), axis=0, tiled=True)]
    ppermute x0 -> x40, starting transfers between devices: none -> 72.9 us  [the longest x18 25.2 us: send(): return lax.ppermute(value, PLANE, pairs)]
    while x8 -> x0, local copies, waits for them, and re-layouts: 63.7 us -> none
    ppermute x0 -> x40, waiting for transfers between devices: none -> 38.4 us  [the longest x16 20.5 us: climb(): lax.ppermute(value, 'z', [(i, (i + dz) % depth) for i in range(depth)])]
    all_to_all x0 -> x1, blocking collectives: none -> 36.1 us  [body(): arrived = lax.all_to_all(outs, PLANE, 0, 0, tiled=True)]
  transfers between devices with their start and end apart: 5 -> 40, of which waited for: 5 -> 23; matrix products, arithmetic and copies ran while one was open for 19% -> 0% of each run, Pallas kernels for 0% -> 4%
where the time goes in v2:
time: 165 us
  starting transfers between devices  72.9 us (44%)
  waiting for transfers between devices  38.4 us (23%)
  blocking collectives  36.1 us (22%)
  Pallas kernels  13.7 us (8%)
  local copies, waits for them, and re-layouts  1.7 us (1%)
    all_to_all x1, blocking collectives, body(): arrived = lax.all_to_all(outs, PLANE, 0, 0, tiled=True)  36.1 us
    ppermute x18, starting transfers between devices, send(): return lax.ppermute(value, PLANE, pairs)  25.2 us
    ppermute x16, starting transfers between devices, climb(): lax.ppermute(value, 'z', [(i, (i + dz) % depth) for i in range(depth)])  24.2 us
    ppermute x6, starting transfers between devices, swap(): return lax.ppermute(value, ('z', 'c'), pairs)  23.5 us
    ppermute x16, waiting for transfers between devices, climb(): lax.ppermute(value, 'z', [(i, (i + dz) % depth) for i in range(depth)])  20.5 us
    ppermute x18, waiting for transfers between devices, send(): return lax.ppermute(value, PLANE, pairs)  11.2 us
    ppermute x6, waiting for transfers between devices, swap(): return lax.ppermute(value, ('z', 'c'), pairs)  6.6 us
    pallas_call x2, Pallas kernels, forward_product(): pl.pallas_call(functools.partial(forward_kernel, own_half, sizes), out_sh...  4.66 us
  transfers between devices with their start and end apart: 40, of which 23 were waited for; matrix products, arithmetic and copies ran while one was open for 0% of the time, Pallas kernels for 4%

profile of v2, /device:TPU:1, one launch (start us, length us, event | category | flops | bytes accessed | tf_op | source)
XLA Modules:
  0.0 165.1 jit_solution(10967769053827064492)
XLA Ops:
  0.6 0.9 fusion.7
  1.5 2.2 %collective-permute-start.5 = (bf16[256,128]{1,0:T(8,128)(2,1)S(1)}, bf16[256,128]{1,0:T(8,128)(2,1)S(1)}, u32[]{:S(2)}, u32[]{:S(2)}) collective-permute-start(bf16[256,128]{1,0:T(8,128)(2,1)S(1)} %get-tuple-element.126), channel_id=1, source_target_pairs={{0,1},{1,8},{8,9},{9,0},{2,3},{3,10},{10,11},{11,2},{4,5},{5,12},{... | collective-permute-start | bytes 196616 | tf_op jit(solution)/shard_map/gather_features/ppermute | solution.py:292
  3.7 2.6 %collective-permute-start.4 = (bf16[256,128]{1,0:T(8,128)(2,1)S(1)}, bf16[256,128]{1,0:T(8,128)(2,1)S(1)}, u32[]{:S(2)}, u32[]{:S(2)}) collective-permute-start(bf16[256,128]{1,0:T(8,128)(2,1)S(1)} %get-tuple-element.126), channel_id=1, source_target_pairs={{0,8},{1,9},{8,0},{9,1},{2,10},{3,11},{10,2},{11,3},{4,12},{5,13},... | collective-permute-start | bytes 196616 | tf_op jit(solution)/shard_map/gather_features/ppermute | solution.py:292
  6.3 1.1 collective-permute-start.3
  7.4 1.2 collective-permute-start.2
  8.6 2.5 %collective-permute-start.1 = (bf16[256,128]{1,0:T(8,128)(2,1)S(1)}, bf16[256,128]{1,0:T(8,128)(2,1)S(1)}, u32[]{:S(2)}, u32[]{:S(2)}) collective-permute-start(bf16[256,128]{1,0:T(8,128)(2,1)S(1)} %get-tuple-element.127), channel_id=1, source_target_pairs={{0,4},{1,5},{8,12},{9,13},{2,6},{3,7},{10,14},{11,15},{4,0},{5,1},... | collective-permute-start | bytes 196616 | tf_op jit(solution)/shard_map/gather_features/ppermute | solution.py:292
  11.1 1.2 collective-permute-start
  12.2 1.2 collective-permute-done.1
  13.5 1.4 collective-permute-done
  15.0 3.5 %collective-permute-start.10 = (bf16[1024,128]{1,0:T(8,128)(2,1)S(1)}, bf16[1024,128]{1,0:T(8,128)(2,1)S(1)}, u32[]{:S(2)}, u32[]{:S(2)}) collective-permute-start(bf16[1024,128]{1,0:T(8,128)(2,1)S(1)} %pad_maximum_fusion.1.refs_4_), channel_id=1, source_target_pairs={{0,4},{1,5},{8,12},{9,13},{2,6},{3,7},{10,14},{11,15},{4,0},{5,1},... | collective-permute-start | bytes 786440 | tf_op jit(solution)/shard_map/gather_features/ppermute | solution.py:292
  18.5 0.5 collective-permute-start.8
  19.0 0.9 collective-permute-start.7
  19.9 1.5 collective-permute-done.11.refs_7_
  21.4 0.5 collective-permute-start.6
  22.7 0.7 copy-done.2
  23.4 1.3 tables.2.table_ref
  24.7 1.3 tables.3.blocks_ref
  26.0 1.6 collective-permute-done.10.refs_6_
  27.6 1.2 collective-permute-done.9.refs_5_
  28.8 0.2 collective-permute-done.7.refs_2_
  29.0 1.4 collective-permute-done.6.refs_1_
  30.4 2.3 %forward.2 = bf16[16,128,256]{2,1,0:T(8,128)(2,1)S(1)} custom-call(s32[8,384]{1,0:T(8,128)S(1)} %tables.2.table_ref, bf16[256,128,128]{2,1,0:T(8,128)(2,1)S(1)} %tables.3.blocks_ref, bf16[1024,128]{1,0:T(8,128)(2,1)S(1)} %pad_maximum_fusion.refs_0_, bf16[1024,128]{1,0:T(8,128)(2,1)S(1)} %collective-permute-done.6.refs_1_, ...), custom_call_target="tpu_custom_call" | custom-call | tf_op jit(solution)/shard_map/forward/pallas_call | solution.py:137
  32.8 6.7 %collective-permute-start.12 = (bf16[16,128,256]{2,1,0:T(8,128)(2,1)S(1)}, bf16[16,128,256]{2,1,0:T(8,128)(2,1)S(1)}, u32[]{:S(2)}, u32[]{:S(2)}) collective-permute-start(bf16[16,128,256]{2,1,0:T(8,128)(2,1)S(1)} %forward.2), channel_id=1, source_target_pairs={{0,16},{16,0},{32,48},{48,32},{64,80},{80,64},{96,112},{112,96},{1... | collective-permute-start | bytes 3145736 | tf_op jit(solution)/shard_map/forward/ppermute | solution.py:299
  39.5 2.3 %forward.3 = bf16[16,128,256]{2,1,0:T(8,128)(2,1)S(1)} custom-call(s32[8,384]{1,0:T(8,128)S(1)} %tables.2.table_ref, bf16[256,128,128]{2,1,0:T(8,128)(2,1)S(1)} %tables.3.blocks_ref, bf16[1024,128]{1,0:T(8,128)(2,1)S(1)} %pad_maximum_fusion.refs_0_, bf16[1024,128]{1,0:T(8,128)(2,1)S(1)} %collective-permute-done.6.refs_1_, ...), custom_call_target="tpu_custom_call" | custom-call | tf_op jit(solution)/shard_map/forward/pallas_call | solution.py:137
  41.8 0.3 convert_add_fusion
  42.1 4.6 %collective-permute-start.14 = (bf16[128,256]{1,0:T(8,128)(2,1)S(1)}, bf16[128,256]{1,0:T(8,128)(2,1)S(1)}, u32[]{:S(2)}, u32[]{:S(2)}) collective-permute-start(bf16[128,256]{1,0:T(8,128)(2,1)S(1)} %get-tuple-element.124), channel_id=1, source_target_pairs={{0,224},{32,0},{64,32},{96,64},{128,96},{160,128},{192,160},{224,1... | collective-permute-start | bytes 196616 | tf_op jit(solution)/shard_map/sum_rows/ppermute | solution.py:295
  46.7 1.3 collective-permute-done.14
  48.1 3.0 %collective-permute-done.13 = bf16[128,256]{1,0:T(8,128)(2,1)S(1)} collective-permute-done((bf16[128,256]{1,0:T(8,128)(2,1)S(1)}, bf16[128,256]{1,0:T(8,128)(2,1)S(1)}, u32[]{:S(2)}, u32[]{:S(2)}) %collective-permute-start.13) | collective-permute-done | bytes 65568 | tf_op jit(solution)/shard_map/sum_rows/ppermute | solution.py:295
  51.1 0.1 collective-permute-start.15
  51.2 2.7 %collective-permute-start.16 = (bf16[256,256]{1,0:T(8,128)(2,1)S(1)}, bf16[256,256]{1,0:T(8,128)(2,1)S(1)}, u32[]{:S(2)}, u32[]{:S(2)}) collective-permute-start(bf16[256,256]{1,0:T(8,128)(2,1)S(1)} %fusion.2), channel_id=1, source_target_pairs={{0,224},{32,0},{64,32},{96,64},{128,96},{160,128},{192,160},{224,1... | collective-permute-start | bytes 393224 | tf_op jit(solution)/shard_map/sum_rows/ppermute | solution.py:295
  53.9 2.4 %collective-permute-done.15 = bf16[256,256]{1,0:T(8,128)(2,1)S(1)} collective-permute-done((bf16[256,256]{1,0:T(8,128)(2,1)S(1)}, bf16[256,256]{1,0:T(8,128)(2,1)S(1)}, u32[]{:S(2)}, u32[]{:S(2)}) %collective-permute-start.15) | collective-permute-done | bytes 131104 | tf_op jit(solution)/shard_map/sum_rows/ppermute | solution.py:295
  56.4 2.7 %collective-permute-start.18 = (bf16[256,256]{1,0:T(8,128)(2,1)S(1)}, bf16[256,256]{1,0:T(8,128)(2,1)S(1)}, u32[]{:S(2)}, u32[]{:S(2)}) collective-permute-start(bf16[256,256]{1,0:T(8,128)(2,1)S(1)} %fusion.1), channel_id=1, source_target_pairs={{0,224},{32,0},{64,32},{96,64},{128,96},{160,128},{192,160},{224,1... | collective-permute-start | bytes 393224 | tf_op jit(solution)/shard_map/sum_rows/ppermute | solution.py:295
  59.1 2.3 %collective-permute-done.17 = bf16[256,256]{1,0:T(8,128)(2,1)S(1)} collective-permute-done((bf16[256,256]{1,0:T(8,128)(2,1)S(1)}, bf16[256,256]{1,0:T(8,128)(2,1)S(1)}, u32[]{:S(2)}, u32[]{:S(2)}) %collective-permute-start.17) | collective-permute-done | bytes 131104 | tf_op jit(solution)/shard_map/sum_rows/ppermute | solution.py:295
  61.6 2.8 %collective-permute-start.20 = (bf16[256,256]{1,0:T(8,128)(2,1)S(1)}, bf16[256,256]{1,0:T(8,128)(2,1)S(1)}, u32[]{:S(2)}, u32[]{:S(2)}) collective-permute-start(bf16[256,256]{1,0:T(8,128)(2,1)S(1)} %get-tuple-element.85), channel_id=1, source_target_pairs={{0,224},{32,0},{64,32},{96,64},{128,96},{160,128},{192,160},{224,1... | collective-permute-start | bytes 393224 | tf_op jit(solution)/shard_map/sum_rows/ppermute | solution.py:295
  64.4 2.6 %collective-permute-done.19 = bf16[256,256]{1,0:T(8,128)(2,1)S(1)} collective-permute-done((bf16[256,256]{1,0:T(8,128)(2,1)S(1)}, bf16[256,256]{1,0:T(8,128)(2,1)S(1)}, u32[]{:S(2)}, u32[]{:S(2)}) %collective-permute-start.19) | collective-permute-done | bytes 131104 | tf_op jit(solution)/shard_map/sum_rows/ppermute | solution.py:295
  67.0 0.9 dense.1
  68.0 3.5 %collective-permute-start.22 = (f32[64,256]{1,0:T(8,128)S(1)}, f32[64,256]{1,0:T(8,128)S(1)}, u32[]{:S(2)}, u32[]{:S(2)}) collective-permute-start(f32[64,256]{1,0:T(8,128)S(1)} %get-tuple-element.121), channel_id=1, source_target_pairs={{0,4},{1,5},{8,12},{9,13},{2,6},{3,7},{10,14},{11,15},{4,0},{5,1},... | collective-permute-start | bytes 196616 | tf_op jit(solution)/shard_map/gather_rows/ppermute | solution.py:292
  71.4 1.5 collective-permute-start.23
  73.0 2.8 %collective-permute-start.25 = (bf16[256,256]{1,0:T(8,128)(2,1)S(1)}, bf16[256,256]{1,0:T(8,128)(2,1)S(1)}, u32[]{:S(2)}, u32[]{:S(2)}) collective-permute-start(bf16[256,256]{1,0:T(8,128)(2,1)S(1)} %get-tuple-element.90), channel_id=1, source_target_pairs={{0,224},{32,0},{64,32},{96,64},{128,96},{160,128},{192,160},{224,1... | collective-permute-start | bytes 393224 | tf_op jit(solution)/shard_map/gather_rows/ppermute | solution.py:295
  75.7 1.6 collective-permute-done.21
  77.3 0.4 collective-permute-done.25
  77.7 3.1 %collective-permute-done.24 = bf16[256,256]{1,0:T(8,128)(2,1)S(1)} collective-permute-done((bf16[256,256]{1,0:T(8,128)(2,1)S(1)}, bf16[256,256]{1,0:T(8,128)(2,1)S(1)}, u32[]{:S(2)}, u32[]{:S(2)}) %collective-permute-start.24) | collective-permute-done | bytes 131104 | tf_op jit(solution)/shard_map/gather_rows/ppermute | solution.py:295
  80.8 2.6 %collective-permute-start.27 = (f32[16,256]{1,0:T(8,128)S(1)}, f32[16,256]{1,0:T(8,128)S(1)}, u32[]{:S(2)}, u32[]{:S(2)}) collective-permute-start(f32[16,256]{1,0:T(8,128)S(1)} %get-tuple-element.128), channel_id=1, source_target_pairs={{0,8},{1,9},{8,0},{9,1},{2,10},{3,11},{10,2},{11,3},{4,12},{5,13},... | collective-permute-start | bytes 49160 | tf_op jit(solution)/shard_map/gather_rows/ppermute | solution.py:292
  83.3 1.5 collective-permute-start.28
  84.8 0.1 collective-permute-start.29
  84.9 2.7 %collective-permute-start.30 = (bf16[256,256]{1,0:T(8,128)(2,1)S(1)}, bf16[256,256]{1,0:T(8,128)(2,1)S(1)}, u32[]{:S(2)}, u32[]{:S(2)}) collective-permute-start(bf16[256,256]{1,0:T(8,128)(2,1)S(1)} %collective-permute-done.25), channel_id=1, source_target_pairs={{0,224},{32,0},{64,32},{96,64},{128,96},{160,128},{192,160},{224,1... | collective-permute-start | bytes 393224 | tf_op jit(solution)/shard_map/gather_rows/ppermute | solution.py:295
  87.6 1.0 collective-permute-done.26
  88.6 1.3 collective-permute-done.29
  89.9 11.9 %collective-permute-start.31 = (f32[16,256]{1,0:T(8,128)S(1)}, f32[16,256]{1,0:T(8,128)S(1)}, u32[]{:S(2)}, u32[]{:S(2)}) collective-permute-start(f32[16,256]{1,0:T(8,128)S(1)} %bitcast_add_fusion.8), channel_id=1, source_target_pairs={{0,16},{16,0},{32,48},{48,32},{64,80},{80,64},{96,112},{112,96},{1... | collective-permute-start | bytes 49160 | tf_op jit(solution)/shard_map/gather_rows/ppermute | solution.py:299
  101.8 3.0 %collective-permute-start.34 = (bf16[256,256]{1,0:T(8,128)(2,1)S(1)}, bf16[256,256]{1,0:T(8,128)(2,1)S(1)}, u32[]{:S(2)}, u32[]{:S(2)}) collective-permute-start(bf16[256,256]{1,0:T(8,128)(2,1)S(1)} %collective-permute-done.30), channel_id=1, source_target_pairs={{0,224},{32,0},{64,32},{96,64},{128,96},{160,128},{192,160},{224,1... | collective-permute-start | bytes 393224 | tf_op jit(solution)/shard_map/gather_rows/ppermute | solution.py:295
  104.8 0.1 collective-permute-start.32
  104.9 2.9 %collective-permute-done.32 = f32[16,256]{1,0:T(8,128)S(1)} collective-permute-done((f32[16,256]{1,0:T(8,128)S(1)}, f32[16,256]{1,0:T(8,128)S(1)}, u32[]{:S(2)}, u32[]{:S(2)}) %collective-permute-start.32) | collective-permute-done | bytes 16416 | tf_op jit(solution)/shard_map/gather_rows/ppermute | solution.py:299
  107.8 0.9 collective-permute-done.33
  108.7 2.5 %collective-permute-start.37 = (bf16[128,256]{1,0:T(8,128)(2,1)S(1)}, bf16[128,256]{1,0:T(8,128)(2,1)S(1)}, u32[]{:S(2)}, u32[]{:S(2)}) collective-permute-start(bf16[128,256]{1,0:T(8,128)(2,1)S(1)} %slice.111), channel_id=1, source_target_pairs={{0,224},{32,0},{64,32},{96,64},{128,96},{160,128},{192,160},{224,1... | collective-permute-start | bytes 196616 | tf_op jit(solution)/shard_map/gather_rows/ppermute | solution.py:295
  111.2 0.9 collective-permute-done.35
  112.1 0.4 collective-permute-done.37
  112.5 3.0 %collective-permute-done.36 = bf16[128,256]{1,0:T(8,128)(2,1)S(1)} collective-permute-done((bf16[128,256]{1,0:T(8,128)(2,1)S(1)}, bf16[128,256]{1,0:T(8,128)(2,1)S(1)}, u32[]{:S(2)}, u32[]{:S(2)}) %collective-permute-start.36) | collective-permute-done | bytes 65568 | tf_op jit(solution)/shard_map/gather_rows/ppermute | solution.py:295
  115.6 2.5 %collective-permute-start.38 = (bf16[16,128,256]{2,1,0:T(8,128)(2,1)S(1)}, bf16[16,128,256]{2,1,0:T(8,128)(2,1)S(1)}, u32[]{:S(2)}, u32[]{:S(2)}) collective-permute-start(bf16[16,128,256]{2,1,0:T(8,128)(2,1)S(1)} %bitcast.61), channel_id=1, source_target_pairs={{0,16},{16,0},{32,48},{48,32},{64,80},{80,64},{96,112},{112,96},{1... | collective-permute-start | bytes 3145736 | tf_op jit(solution)/shard_map/gather_rows/ppermute | solution.py:299
  118.1 2.4 %collective-permute-start.39 = (f32[16,256]{1,0:T(8,128)S(1)}, f32[16,256]{1,0:T(8,128)S(1)}, u32[]{:S(2)}, u32[]{:S(2)}) collective-permute-start(f32[16,256]{1,0:T(8,128)S(1)} %add.197), channel_id=1, source_target_pairs={{0,128},{16,144},{32,160},{48,176},{64,192},{80,208},{96,224},{112... | collective-permute-start | bytes 49160 | tf_op jit(solution)/shard_map/gather_rows/ppermute | solution.py:299
  120.5 1.3 gather_rows.1.blocks_ref
  121.8 2.8 %collective-permute-done.39 = f32[16,256]{1,0:T(8,128)S(1)} collective-permute-done((f32[16,256]{1,0:T(8,128)S(1)}, f32[16,256]{1,0:T(8,128)S(1)}, u32[]{:S(2)}, u32[]{:S(2)}) %collective-permute-start.39) | collective-permute-done | bytes 16416 | tf_op jit(solution)/shard_map/gather_rows/ppermute | solution.py:299
  124.7 3.2 %backward.1 = bf16[16,272,256]{2,1,0:T(8,128)(2,1)S(1)} custom-call(s32[8,384]{1,0:T(8,128)S(1)} %tables.2.table_ref, s32[4]{0:T(128)S(1)} %pad_add_fusion.place_ref, bf16[256,128,128]{2,1,0:T(8,128)(2,1)S(1)} %gather_rows.1.blocks_ref, bf16[16,128,256]{2,1,0:T(8,128)(2,1)S(1)} %collective-permute-done.38.sibling_ref, bf16[16,128,256]{2,1,0:T(8,128)(2,1)S(1)} %bitcast.62, ...), custom_call_target="tpu_custom_call" | custom-call | tf_op jit(solution)/shard_map/backward/pallas_call | solution.py:170
  127.9 36.1 %all_to_all.5.arrived_ref = bf16[16,272,256]{2,1,0:T(8,128)(2,1)S(1)} all-to-all(bf16[16,272,256]{2,1,0:T(8,128)(2,1)S(1)} %backward.1), channel_id=1, replica_groups=mesh['z'=8,'c'=2,'yh'=2,'x'=4,'yl'=2] {'yh','x','yl'}, dimensions={0} | all-to-all | bytes 4456448 | tf_op jit(solution)/shard_map/sum_columns/all_to_all | solution.py:392
  164.0 1.0 sum_columns.1
  (62 shorter events, 0.8 us)
Async XLA Ops:
  1.5 9.6 %collective-permute-start.5 = (bf16[256,128]{1,0:T(8,128)(2,1)S(1)}, bf16[256,128]{1,0:T(8,128)(2,1)S(1)}, u32[]{:S(2)}, u32[]{:S(2)}) collective-permute-start(bf16[256,128]{1,0:T(8,128)(2,1)S(1)} %get-tuple-element.126), channel_id=1, source_target_pairs={{0,1},{1,8},{8,9},{9,0},{2,3},{3,10},{10,11},{11,2},{4,5},{5,12},{... | collective-permute-start | bytes 196616 | tf_op jit(solution)/shard_map/gather_features/ppermute | solution.py:292
  3.7 8.5 %collective-permute-start.4 = (bf16[256,128]{1,0:T(8,128)(2,1)S(1)}, bf16[256,128]{1,0:T(8,128)(2,1)S(1)}, u32[]{:S(2)}, u32[]{:S(2)}) collective-permute-start(bf16[256,128]{1,0:T(8,128)(2,1)S(1)} %get-tuple-element.126), channel_id=1, source_target_pairs={{0,8},{1,9},{8,0},{9,1},{2,10},{3,11},{10,2},{11,3},{4,12},{5,13},... | collective-permute-start | bytes 196616 | tf_op jit(solution)/shard_map/gather_features/ppermute | solution.py:292
  6.3 5.9 %collective-permute-start.3 = (bf16[256,128]{1,0:T(8,128)(2,1)S(1)}, bf16[256,128]{1,0:T(8,128)(2,1)S(1)}, u32[]{:S(2)}, u32[]{:S(2)}) collective-permute-start(bf16[256,128]{1,0:T(8,128)(2,1)S(1)} %get-tuple-element.126), channel_id=1, source_target_pairs={{0,9},{1,0},{8,1},{9,8},{2,11},{3,2},{10,3},{11,10},{4,13},{5,4},{... | collective-permute-start | bytes 196616 | tf_op jit(solution)/shard_map/gather_features/ppermute | solution.py:292
  7.4 4.8 %collective-permute-start.2 = (bf16[256,128]{1,0:T(8,128)(2,1)S(1)}, bf16[256,128]{1,0:T(8,128)(2,1)S(1)}, u32[]{:S(2)}, u32[]{:S(2)}) collective-permute-start(bf16[256,128]{1,0:T(8,128)(2,1)S(1)} %get-tuple-element.127), channel_id=1, source_target_pairs={{0,2},{1,3},{8,10},{9,11},{2,4},{3,5},{10,12},{11,13},{4,6},{5,7},... | collective-permute-start | bytes 196616 | tf_op jit(solution)/shard_map/gather_features/ppermute | solution.py:292
  8.6 4.8 %collective-permute-start.1 = (bf16[256,128]{1,0:T(8,128)(2,1)S(1)}, bf16[256,128]{1,0:T(8,128)(2,1)S(1)}, u32[]{:S(2)}, u32[]{:S(2)}) collective-permute-start(bf16[256,128]{1,0:T(8,128)(2,1)S(1)} %get-tuple-element.127), channel_id=1, source_target_pairs={{0,4},{1,5},{8,12},{9,13},{2,6},{3,7},{10,14},{11,15},{4,0},{5,1},... | collective-permute-start | bytes 196616 | tf_op jit(solution)/shard_map/gather_features/ppermute | solution.py:292
  11.1 3.8 %collective-permute-start = (bf16[256,128]{1,0:T(8,128)(2,1)S(1)}, bf16[256,128]{1,0:T(8,128)(2,1)S(1)}, u32[]{:S(2)}, u32[]{:S(2)}) collective-permute-start(bf16[256,128]{1,0:T(8,128)(2,1)S(1)} %get-tuple-element.127), channel_id=1, source_target_pairs={{0,6},{1,7},{8,14},{9,15},{2,0},{3,1},{10,8},{11,9},{4,2},{5,3},{1... | collective-permute-start | bytes 196616 | tf_op jit(solution)/shard_map/gather_features/ppermute | solution.py:292
  14.9 6.5 %collective-permute-start.11 = (bf16[1024,128]{1,0:T(8,128)(2,1)S(1)}, bf16[1024,128]{1,0:T(8,128)(2,1)S(1)}, u32[]{:S(2)}, u32[]{:S(2)}) collective-permute-start(bf16[1024,128]{1,0:T(8,128)(2,1)S(1)} %pad_maximum_fusion.1.refs_4_), channel_id=1, source_target_pairs={{0,2},{1,3},{8,10},{9,11},{2,4},{3,5},{10,12},{11,13},{4,6},{5,7},... | collective-permute-start | bytes 786440 | tf_op jit(solution)/shard_map/gather_features/ppermute | solution.py:292
  15.0 12.6 %collective-permute-start.10 = (bf16[1024,128]{1,0:T(8,128)(2,1)S(1)}, bf16[1024,128]{1,0:T(8,128)(2,1)S(1)}, u32[]{:S(2)}, u32[]{:S(2)}) collective-permute-start(bf16[1024,128]{1,0:T(8,128)(2,1)S(1)} %pad_maximum_fusion.1.refs_4_), channel_id=1, source_target_pairs={{0,4},{1,5},{8,12},{9,13},{2,6},{3,7},{10,14},{11,15},{4,0},{5,1},... | collective-permute-start | bytes 786440 | tf_op jit(solution)/shard_map/gather_features/ppermute | solution.py:292
  18.5 10.3 %collective-permute-start.9 = (bf16[1024,128]{1,0:T(8,128)(2,1)S(1)}, bf16[1024,128]{1,0:T(8,128)(2,1)S(1)}, u32[]{:S(2)}, u32[]{:S(2)}) collective-permute-start(bf16[1024,128]{1,0:T(8,128)(2,1)S(1)} %pad_maximum_fusion.1.refs_4_), channel_id=1, source_target_pairs={{0,6},{1,7},{8,14},{9,15},{2,0},{3,1},{10,8},{11,9},{4,2},{5,3},{1... | collective-permute-start | bytes 786440 | tf_op jit(solution)/shard_map/gather_features/ppermute | solution.py:292
  18.5 10.3 %collective-permute-start.8 = (bf16[1024,128]{1,0:T(8,128)(2,1)S(1)}, bf16[1024,128]{1,0:T(8,128)(2,1)S(1)}, u32[]{:S(2)}, u32[]{:S(2)}) collective-permute-start(bf16[1024,128]{1,0:T(8,128)(2,1)S(1)} %pad_maximum_fusion.refs_0_), channel_id=1, source_target_pairs={{0,1},{1,8},{8,9},{9,0},{2,3},{3,10},{10,11},{11,2},{4,5},{5,12},{... | collective-permute-start | bytes 786440 | tf_op jit(solution)/shard_map/gather_features/ppermute | solution.py:292
  19.0 10.0 %collective-permute-start.7 = (bf16[1024,128]{1,0:T(8,128)(2,1)S(1)}, bf16[1024,128]{1,0:T(8,128)(2,1)S(1)}, u32[]{:S(2)}, u32[]{:S(2)}) collective-permute-start(bf16[1024,128]{1,0:T(8,128)(2,1)S(1)} %pad_maximum_fusion.refs_0_), channel_id=1, source_target_pairs={{0,8},{1,9},{8,0},{9,1},{2,10},{3,11},{10,2},{11,3},{4,12},{5,13},... | collective-permute-start | bytes 786440 | tf_op jit(solution)/shard_map/gather_features/ppermute | solution.py:292
  21.4 9.0 %collective-permute-start.6 = (bf16[1024,128]{1,0:T(8,128)(2,1)S(1)}, bf16[1024,128]{1,0:T(8,128)(2,1)S(1)}, u32[]{:S(2)}, u32[]{:S(2)}) collective-permute-start(bf16[1024,128]{1,0:T(8,128)(2,1)S(1)} %pad_maximum_fusion.refs_0_), channel_id=1, source_target_pairs={{0,9},{1,0},{8,1},{9,8},{2,11},{3,2},{10,3},{11,10},{4,13},{5,4},{... | collective-permute-start | bytes 786440 | tf_op jit(solution)/shard_map/gather_features/ppermute | solution.py:292
  22.7 0.7 copy-start.2
  32.8 34.3 %copy-start = (bf16[256,256]{1,0:T(8,128)(2,1)S(1)}, bf16[256,256]{1,0:T(8,128)(2,1)}, u32[]{:S(2)}) copy-start(bf16[256,256]{1,0:T(8,128)(2,1)} %weight_ref.1) | copy-start | bytes 393220
  32.8 34.3 %copy-start.1 = (bf16[256,256]{1,0:T(8,128)(2,1)S(1)}, bf16[256,256]{1,0:T(8,128)(2,1)}, u32[]{:S(2)}) copy-start(bf16[256,256]{1,0:T(8,128)(2,1)} %cotangent_ref.1) | copy-start | bytes 393220
  32.8 9.0 %collective-permute-start.12 = (bf16[16,128,256]{2,1,0:T(8,128)(2,1)S(1)}, bf16[16,128,256]{2,1,0:T(8,128)(2,1)S(1)}, u32[]{:S(2)}, u32[]{:S(2)}) collective-permute-start(bf16[16,128,256]{2,1,0:T(8,128)(2,1)S(1)} %forward.2), channel_id=1, source_target_pairs={{0,16},{16,0},{32,48},{48,32},{64,80},{80,64},{96,112},{112,96},{1... | collective-permute-start | bytes 3145736 | tf_op jit(solution)/shard_map/forward/ppermute | solution.py:299
  42.1 6.0 %collective-permute-start.14 = (bf16[128,256]{1,0:T(8,128)(2,1)S(1)}, bf16[128,256]{1,0:T(8,128)(2,1)S(1)}, u32[]{:S(2)}, u32[]{:S(2)}) collective-permute-start(bf16[128,256]{1,0:T(8,128)(2,1)S(1)} %get-tuple-element.124), channel_id=1, source_target_pairs={{0,224},{32,0},{64,32},{96,64},{128,96},{160,128},{192,160},{224,1... | collective-permute-start | bytes 196616 | tf_op jit(solution)/shard_map/sum_rows/ppermute | solution.py:295
  46.7 4.3 %collective-permute-start.13 = (bf16[128,256]{1,0:T(8,128)(2,1)S(1)}, bf16[128,256]{1,0:T(8,128)(2,1)S(1)}, u32[]{:S(2)}, u32[]{:S(2)}) collective-permute-start(bf16[128,256]{1,0:T(8,128)(2,1)S(1)} %get-tuple-element.125), channel_id=1, source_target_pairs={{0,32},{32,64},{64,96},{96,128},{128,160},{160,192},{192,224},{224... | collective-permute-start | bytes 196616 | tf_op jit(solution)/shard_map/sum_rows/ppermute | solution.py:295
  51.1 5.1 %collective-permute-start.15 = (bf16[256,256]{1,0:T(8,128)(2,1)S(1)}, bf16[256,256]{1,0:T(8,128)(2,1)S(1)}, u32[]{:S(2)}, u32[]{:S(2)}) collective-permute-start(bf16[256,256]{1,0:T(8,128)(2,1)S(1)} %fusion.3), channel_id=1, source_target_pairs={{0,32},{32,64},{64,96},{96,128},{128,160},{160,192},{192,224},{224... | collective-permute-start | bytes 393224 | tf_op jit(solution)/shard_map/sum_rows/ppermute | solution.py:295
  51.2 5.0 %collective-permute-start.16 = (bf16[256,256]{1,0:T(8,128)(2,1)S(1)}, bf16[256,256]{1,0:T(8,128)(2,1)S(1)}, u32[]{:S(2)}, u32[]{:S(2)}) collective-permute-start(bf16[256,256]{1,0:T(8,128)(2,1)S(1)} %fusion.2), channel_id=1, source_target_pairs={{0,224},{32,0},{64,32},{96,64},{128,96},{160,128},{192,160},{224,1... | collective-permute-start | bytes 393224 | tf_op jit(solution)/shard_map/sum_rows/ppermute | solution.py:295
  56.3 5.1 %collective-permute-start.17 = (bf16[256,256]{1,0:T(8,128)(2,1)S(1)}, bf16[256,256]{1,0:T(8,128)(2,1)S(1)}, u32[]{:S(2)}, u32[]{:S(2)}) collective-permute-start(bf16[256,256]{1,0:T(8,128)(2,1)S(1)} %fusion.4), channel_id=1, source_target_pairs={{0,32},{32,64},{64,96},{96,128},{128,160},{160,192},{192,224},{224... | collective-permute-start | bytes 393224 | tf_op jit(solution)/shard_map/sum_rows/ppermute | solution.py:295
  56.4 5.0 %collective-permute-start.18 = (bf16[256,256]{1,0:T(8,128)(2,1)S(1)}, bf16[256,256]{1,0:T(8,128)(2,1)S(1)}, u32[]{:S(2)}, u32[]{:S(2)}) collective-permute-start(bf16[256,256]{1,0:T(8,128)(2,1)S(1)} %fusion.1), channel_id=1, source_target_pairs={{0,224},{32,0},{64,32},{96,64},{128,96},{160,128},{192,160},{224,1... | collective-permute-start | bytes 393224 | tf_op jit(solution)/shard_map/sum_rows/ppermute | solution.py:295
  61.5 5.5 %collective-permute-start.19 = (bf16[256,256]{1,0:T(8,128)(2,1)S(1)}, bf16[256,256]{1,0:T(8,128)(2,1)S(1)}, u32[]{:S(2)}, u32[]{:S(2)}) collective-permute-start(bf16[256,256]{1,0:T(8,128)(2,1)S(1)} %get-tuple-element.84), channel_id=1, source_target_pairs={{0,32},{32,64},{64,96},{96,128},{128,160},{160,192},{192,224},{224... | collective-permute-start | bytes 393224 | tf_op jit(solution)/shard_map/sum_rows/ppermute | solution.py:295
  61.6 5.4 %collective-permute-start.20 = (bf16[256,256]{1,0:T(8,128)(2,1)S(1)}, bf16[256,256]{1,0:T(8,128)(2,1)S(1)}, u32[]{:S(2)}, u32[]{:S(2)}) collective-permute-start(bf16[256,256]{1,0:T(8,128)(2,1)S(1)} %get-tuple-element.85), channel_id=1, source_target_pairs={{0,224},{32,0},{64,32},{96,64},{128,96},{160,128},{192,160},{224,1... | collective-permute-start | bytes 393224 | tf_op jit(solution)/shard_map/sum_rows/ppermute | solution.py:295
  68.0 7.8 %collective-permute-start.22 = (f32[64,256]{1,0:T(8,128)S(1)}, f32[64,256]{1,0:T(8,128)S(1)}, u32[]{:S(2)}, u32[]{:S(2)}) collective-permute-start(f32[64,256]{1,0:T(8,128)S(1)} %get-tuple-element.121), channel_id=1, source_target_pairs={{0,4},{1,5},{8,12},{9,13},{2,6},{3,7},{10,14},{11,15},{4,0},{5,1},... | collective-permute-start | bytes 196616 | tf_op jit(solution)/shard_map/gather_rows/ppermute | solution.py:292
  71.4 4.3 %collective-permute-start.23 = (f32[64,256]{1,0:T(8,128)S(1)}, f32[64,256]{1,0:T(8,128)S(1)}, u32[]{:S(2)}, u32[]{:S(2)}) collective-permute-start(f32[64,256]{1,0:T(8,128)S(1)} %get-tuple-element.122), channel_id=1, source_target_pairs={{0,6},{1,7},{8,14},{9,15},{2,0},{3,1},{10,8},{11,9},{4,2},{5,3},{1... | collective-permute-start | bytes 196616 | tf_op jit(solution)/shard_map/gather_rows/ppermute | solution.py:292
  73.0 4.3 %collective-permute-start.21 = (f32[64,256]{1,0:T(8,128)S(1)}, f32[64,256]{1,0:T(8,128)S(1)}, u32[]{:S(2)}, u32[]{:S(2)}) collective-permute-start(f32[64,256]{1,0:T(8,128)S(1)} %get-tuple-element.123), channel_id=1, source_target_pairs={{0,2},{1,3},{8,10},{9,11},{2,4},{3,5},{10,12},{11,13},{4,6},{5,7},... | collective-permute-start | bytes 196616 | tf_op jit(solution)/shard_map/gather_rows/ppermute | solution.py:292
  73.0 4.7 %collective-permute-start.25 = (bf16[256,256]{1,0:T(8,128)(2,1)S(1)}, bf16[256,256]{1,0:T(8,128)(2,1)S(1)}, u32[]{:S(2)}, u32[]{:S(2)}) collective-permute-start(bf16[256,256]{1,0:T(8,128)(2,1)S(1)} %get-tuple-element.90), channel_id=1, source_target_pairs={{0,224},{32,0},{64,32},{96,64},{128,96},{160,128},{192,160},{224,1... | collective-permute-start | bytes 393224 | tf_op jit(solution)/shard_map/gather_rows/ppermute | solution.py:295
  75.7 5.0 %collective-permute-start.24 = (bf16[256,256]{1,0:T(8,128)(2,1)S(1)}, bf16[256,256]{1,0:T(8,128)(2,1)S(1)}, u32[]{:S(2)}, u32[]{:S(2)}) collective-permute-start(bf16[256,256]{1,0:T(8,128)(2,1)S(1)} %get-tuple-element.90), channel_id=1, source_target_pairs={{0,32},{32,64},{64,96},{96,128},{128,160},{160,192},{192,224},{224... | collective-permute-start | bytes 393224 | tf_op jit(solution)/shard_map/gather_rows/ppermute | solution.py:295
  80.8 6.8 %collective-permute-start.27 = (f32[16,256]{1,0:T(8,128)S(1)}, f32[16,256]{1,0:T(8,128)S(1)}, u32[]{:S(2)}, u32[]{:S(2)}) collective-permute-start(f32[16,256]{1,0:T(8,128)S(1)} %get-tuple-element.128), channel_id=1, source_target_pairs={{0,8},{1,9},{8,0},{9,1},{2,10},{3,11},{10,2},{11,3},{4,12},{5,13},... | collective-permute-start | bytes 49160 | tf_op jit(solution)/shard_map/gather_rows/ppermute | solution.py:292
  83.3 4.3 %collective-permute-start.28 = (f32[16,256]{1,0:T(8,128)S(1)}, f32[16,256]{1,0:T(8,128)S(1)}, u32[]{:S(2)}, u32[]{:S(2)}) collective-permute-start(f32[16,256]{1,0:T(8,128)S(1)} %get-tuple-element.129), channel_id=1, source_target_pairs={{0,9},{1,0},{8,1},{9,8},{2,11},{3,2},{10,3},{11,10},{4,13},{5,4},{... | collective-permute-start | bytes 49160 | tf_op jit(solution)/shard_map/gather_rows/ppermute | solution.py:292
  84.8 3.8 %collective-permute-start.26 = (f32[16,256]{1,0:T(8,128)S(1)}, f32[16,256]{1,0:T(8,128)S(1)}, u32[]{:S(2)}, u32[]{:S(2)}) collective-permute-start(f32[16,256]{1,0:T(8,128)S(1)} %get-tuple-element.130), channel_id=1, source_target_pairs={{0,1},{1,8},{8,9},{9,0},{2,3},{3,10},{10,11},{11,2},{4,5},{5,12},{... | collective-permute-start | bytes 49160 | tf_op jit(solution)/shard_map/gather_rows/ppermute | solution.py:292
  84.8 5.1 %collective-permute-start.29 = (bf16[256,256]{1,0:T(8,128)(2,1)S(1)}, bf16[256,256]{1,0:T(8,128)(2,1)S(1)}, u32[]{:S(2)}, u32[]{:S(2)}) collective-permute-start(bf16[256,256]{1,0:T(8,128)(2,1)S(1)} %collective-permute-done.24), channel_id=1, source_target_pairs={{0,32},{32,64},{64,96},{96,128},{128,160},{160,192},{192,224},{224... | collective-permute-start | bytes 393224 | tf_op jit(solution)/shard_map/gather_rows/ppermute | solution.py:295
  84.9 5.0 %collective-permute-start.30 = (bf16[256,256]{1,0:T(8,128)(2,1)S(1)}, bf16[256,256]{1,0:T(8,128)(2,1)S(1)}, u32[]{:S(2)}, u32[]{:S(2)}) collective-permute-start(bf16[256,256]{1,0:T(8,128)(2,1)S(1)} %collective-permute-done.25), channel_id=1, source_target_pairs={{0,224},{32,0},{64,32},{96,64},{128,96},{160,128},{192,160},{224,1... | collective-permute-start | bytes 393224 | tf_op jit(solution)/shard_map/gather_rows/ppermute | solution.py:295
  89.9 14.8 %collective-permute-start.31 = (f32[16,256]{1,0:T(8,128)S(1)}, f32[16,256]{1,0:T(8,128)S(1)}, u32[]{:S(2)}, u32[]{:S(2)}) collective-permute-start(f32[16,256]{1,0:T(8,128)S(1)} %bitcast_add_fusion.8), channel_id=1, source_target_pairs={{0,16},{16,0},{32,48},{48,32},{64,80},{80,64},{96,112},{112,96},{1... | collective-permute-start | bytes 49160 | tf_op jit(solution)/shard_map/gather_rows/ppermute | solution.py:299
  101.8 6.8 %collective-permute-start.33 = (bf16[256,256]{1,0:T(8,128)(2,1)S(1)}, bf16[256,256]{1,0:T(8,128)(2,1)S(1)}, u32[]{:S(2)}, u32[]{:S(2)}) collective-permute-start(bf16[256,256]{1,0:T(8,128)(2,1)S(1)} %collective-permute-done.29), channel_id=1, source_target_pairs={{0,32},{32,64},{64,96},{96,128},{128,160},{160,192},{192,224},{224... | collective-permute-start | bytes 393224 | tf_op jit(solution)/shard_map/gather_rows/ppermute | solution.py:295
  101.8 6.8 %collective-permute-start.34 = (bf16[256,256]{1,0:T(8,128)(2,1)S(1)}, bf16[256,256]{1,0:T(8,128)(2,1)S(1)}, u32[]{:S(2)}, u32[]{:S(2)}) collective-permute-start(bf16[256,256]{1,0:T(8,128)(2,1)S(1)} %collective-permute-done.30), channel_id=1, source_target_pairs={{0,224},{32,0},{64,32},{96,64},{128,96},{160,128},{192,160},{224,1... | collective-permute-start | bytes 393224 | tf_op jit(solution)/shard_map/gather_rows/ppermute | solution.py:295
  104.8 3.0 %collective-permute-start.32 = (f32[16,256]{1,0:T(8,128)S(1)}, f32[16,256]{1,0:T(8,128)S(1)}, u32[]{:S(2)}, u32[]{:S(2)}) collective-permute-start(f32[16,256]{1,0:T(8,128)S(1)} %add.195), channel_id=1, source_target_pairs={{0,32},{16,48},{32,0},{48,16},{64,96},{80,112},{96,64},{112,80},{1... | collective-permute-start | bytes 49160 | tf_op jit(solution)/shard_map/gather_rows/ppermute | solution.py:299
  108.6 3.5 %collective-permute-start.35 = (f32[16,256]{1,0:T(8,128)S(1)}, f32[16,256]{1,0:T(8,128)S(1)}, u32[]{:S(2)}, u32[]{:S(2)}) collective-permute-start(f32[16,256]{1,0:T(8,128)S(1)} %add.196), channel_id=1, source_target_pairs={{0,64},{16,80},{32,96},{48,112},{64,0},{80,16},{96,32},{112,48},{1... | collective-permute-start | bytes 49160 | tf_op jit(solution)/shard_map/gather_rows/ppermute | solution.py:299
  108.7 3.9 %collective-permute-start.37 = (bf16[128,256]{1,0:T(8,128)(2,1)S(1)}, bf16[128,256]{1,0:T(8,128)(2,1)S(1)}, u32[]{:S(2)}, u32[]{:S(2)}) collective-permute-start(bf16[128,256]{1,0:T(8,128)(2,1)S(1)} %slice.111), channel_id=1, source_target_pairs={{0,224},{32,0},{64,32},{96,64},{128,96},{160,128},{192,160},{224,1... | collective-permute-start | bytes 196616 | tf_op jit(solution)/shard_map/gather_rows/ppermute | solution.py:295
  111.2 4.3 %collective-permute-start.36 = (bf16[128,256]{1,0:T(8,128)(2,1)S(1)}, bf16[128,256]{1,0:T(8,128)(2,1)S(1)}, u32[]{:S(2)}, u32[]{:S(2)}) collective-permute-start(bf16[128,256]{1,0:T(8,128)(2,1)S(1)} %slice.110), channel_id=1, source_target_pairs={{0,32},{32,64},{64,96},{96,128},{128,160},{160,192},{192,224},{224... | collective-permute-start | bytes 196616 | tf_op jit(solution)/shard_map/gather_rows/ppermute | solution.py:295
  115.6 9.1 %collective-permute-start.38 = (bf16[16,128,256]{2,1,0:T(8,128)(2,1)S(1)}, bf16[16,128,256]{2,1,0:T(8,128)(2,1)S(1)}, u32[]{:S(2)}, u32[]{:S(2)}) collective-permute-start(bf16[16,128,256]{2,1,0:T(8,128)(2,1)S(1)} %bitcast.61), channel_id=1, source_target_pairs={{0,16},{16,0},{32,48},{48,32},{64,80},{80,64},{96,112},{112,96},{1... | collective-permute-start | bytes 3145736 | tf_op jit(solution)/shard_map/gather_rows/ppermute | solution.py:299
  118.1 6.5 %collective-permute-start.39 = (f32[16,256]{1,0:T(8,128)S(1)}, f32[16,256]{1,0:T(8,128)S(1)}, u32[]{:S(2)}, u32[]{:S(2)}) collective-permute-start(f32[16,256]{1,0:T(8,128)S(1)} %add.197), channel_id=1, source_target_pairs={{0,128},{16,144},{32,160},{48,176},{64,192},{80,208},{96,224},{112... | collective-permute-start | bytes 49160 | tf_op jit(solution)/shard_map/gather_rows/ppermute | solution.py:299

commit v3 on v2

--- a/solution.py
+++ b/solution.py
@@ -10,7 +10,7 @@
 
 BLK = 128
 QUAD = 4
-QUADS_A_STEP = 4
+QUADS_A_STEP = 8
 PARTS = 8
 TABLE = 384
 PLANE = ("yh", "x", "yl")
@@ -18,6 +18,7 @@
 F32 = jnp.float32
 VMEM_LIMIT = 24 * 1024 * 1024
 SMALL_LIMIT = 8 * 1024 * 1024
+BESIDE = pl.CostEstimate(flops=4_000_000_000, bytes_accessed=0, transcendentals=0)
 VMEM = pl.BlockSpec(memory_space=pltpu.VMEM)
 SMEM = pl.BlockSpec(memory_space=pltpu.SMEM)
 
@@ -147,40 +148,40 @@
     )(table, blocks, *pieces)
 
 
-def backward_kernel(sizes, table_ref, place_ref, blocks_ref, sibling_ref, own_ref, tail_ref, out_ref, source_ref, total_ref):
+def backward_kernel(sizes, table_ref, place_ref, blocks_ref, sibling_ref, own_ref, out_ref, source_ref, total_ref):
     depth, nx, ny = sizes
     source_ref[0 : 2 * depth] = sibling_ref[...]
     source_ref[2 * depth :] = own_ref[...]
     total_ref[...] = jnp.zeros_like(total_ref)
     add_quads(table_ref, 4, 0, table_ref[7, 0], 0, blocks_ref, source_ref, total_ref, 0)
     at_x, at_y = place_ref[2], place_ref[3]
-    local = 2 * BLK
     for oy in range(ny):
         for ox in range(nx):
             y = jnp.bitwise_and(at_y + oy, ny - 1)
             rank = (y // 2 * nx + jnp.bitwise_and(at_x + ox, nx - 1)) * 2 + jnp.bitwise_and(y, 1)
             for h in range(2):
                 out_ref[rank, h * BLK : (h + 1) * BLK, :] = total_ref[(oy * nx + ox) * 2 + h].astype(BF16)
-            out_ref[rank, local:, :] = tail_ref[...]
-
-
-def backward_product(table, place, blocks, sibling, own, tail, sizes):
+
+
+def backward_product(table, place, blocks, sibling, own, room, sizes):
     depth, nx, ny = sizes
     lines, _, width = own.shape
     return pl.pallas_call(
         functools.partial(backward_kernel, sizes),
-        out_shape=jax.ShapeDtypeStruct((nx * ny, 2 * BLK + tail.shape[0], width), BF16),
-        in_specs=[SMEM] * 2 + [VMEM] * 4,
+        out_shape=jax.ShapeDtypeStruct((nx * ny, 2 * BLK + room, width), BF16),
+        in_specs=[SMEM] * 2 + [VMEM] * 3,
         out_specs=VMEM,
         scratch_shapes=[
             pltpu.VMEM((2 * lines, BLK, width), BF16),
             pltpu.VMEM((nx * ny * 2, BLK, width), F32),
         ],
+        cost_estimate=BESIDE,
         compiler_params=pltpu.CompilerParams(vmem_limit_bytes=VMEM_LIMIT),
-    )(table, place, blocks, sibling, own, tail)
-
-
-def hold_kernel(count_ref, blocks_ref, held_ref, sem):
+    )(table, place, blocks, sibling, own)
+
+
+def hold_kernel(count_ref, blocks_ref, held_ref, mark_ref, sem):
+    mark_ref[...] = jnp.zeros_like(mark_ref)
     size = blocks_ref.shape[0] // PARTS
     filled = count_ref[0]
 
@@ -208,41 +209,85 @@
 def hold_blocks(blocks, count):
     return pl.pallas_call(
         hold_kernel,
-        out_shape=pltpu.VMEM(blocks.shape, blocks.dtype),
+        out_shape=(pltpu.VMEM(blocks.shape, blocks.dtype), jax.ShapeDtypeStruct((8, BLK), F32)),
         in_specs=[SMEM, pl.BlockSpec(memory_space=pltpu.MemorySpace.HBM)],
-        out_specs=VMEM,
+        out_specs=(VMEM, VMEM),
         scratch_shapes=[pltpu.SemaphoreType.DMA((PARTS,))],
         compiler_params=pltpu.CompilerParams(vmem_limit_bytes=VMEM_LIMIT),
     )(count, pltpu.with_memory_space_constraint(blocks, pltpu.MemorySpace.HBM))
 
 
-def dense_kernel(mixed_ref, weight_ref, cotangent_ref, hidden_ref, grad_ref, part_ref):
-    mixed = mixed_ref[...]
+def dense_kernel(mixed_ref, weight_ref, cotangent_ref, hidden_ref, act_ref, grad_ref):
     weight = weight_ref[...]
-    pre_act = jnp.dot(mixed, weight, preferred_element_type=F32)
+    pre_act = jnp.dot(mixed_ref[...], weight, preferred_element_type=F32)
     sigma = jax.nn.sigmoid(pre_act)
     hidden_ref[...] = (pre_act * sigma).astype(BF16)
     slope = sigma * (1.0 + pre_act * (1.0 - sigma))
     act_grad = (cotangent_ref[...].astype(F32) * slope).astype(BF16)
+    act_ref[...] = act_grad
     grad_ref[...] = lax.dot_general(
         act_grad, weight, (((1,), (1,)), ((), ())), preferred_element_type=F32
     ).astype(BF16)
-    part_ref[...] = lax.dot_general(
-        mixed, act_grad, (((0,), (0,)), ((), ())), preferred_element_type=F32
-    )
 
 
 def dense(mixed, weight, cotangent):
-    shape = cotangent.shape
+    shape = jax.ShapeDtypeStruct(cotangent.shape, BF16)
     return pl.pallas_call(
         dense_kernel,
-        out_shape=(
-            jax.ShapeDtypeStruct(shape, BF16),
-            jax.ShapeDtypeStruct(shape, BF16),
-            jax.ShapeDtypeStruct(weight.shape, F32),
-        ),
+        out_shape=(shape,) * 3,
         compiler_params=pltpu.CompilerParams(vmem_limit_bytes=SMALL_LIMIT),
     )(mixed, weight, cotangent)
+
+
+def cut(value_ref, at, out_refs):
+    size = out_refs[0].shape[0]
+    for d, out_ref in enumerate(out_refs):
+        owner = jnp.bitwise_and(at + d, len(out_refs) - 1)
+        out_ref[...] = value_ref[pl.ds(pl.multiple_of(owner * size, size), size), :]
+
+
+def weight_shares_kernel(place_ref, mixed_ref, act_ref, *refs):
+    *out_refs, value_ref = refs
+    value_ref[...] = lax.dot_general(
+        mixed_ref[...], act_ref[...], (((0,), (0,)), ((), ())), preferred_element_type=F32
+    )
+    cut(value_ref, place_ref[2], out_refs)
+
+
+def weight_shares(place, mixed, act_grad, count):
+    rows, width = mixed.shape
+    return pl.pallas_call(
+        weight_shares_kernel,
+        out_shape=(jax.ShapeDtypeStruct((width // count, width), F32),) * count,
+        in_specs=[SMEM, VMEM, VMEM],
+        out_specs=(VMEM,) * count,
+        scratch_shapes=[pltpu.VMEM((width, width), F32)],
+        cost_estimate=BESIDE,
+        compiler_params=pltpu.CompilerParams(vmem_limit_bytes=SMALL_LIMIT),
+    )(place, mixed, act_grad)
+
+
+def add_cut_kernel(count, place_ref, *refs):
+    *refs, value_ref = refs
+    terms, out_refs = refs[:4], refs[4:]
+    value_ref[...] = (terms[0][...] + terms[1][...]) + (terms[2][...] + terms[3][...])
+    if count == 1:
+        out_refs[0][...] = value_ref[...]
+    else:
+        cut(value_ref, place_ref[3], out_refs)
+
+
+def add_cut(place, terms, count):
+    rows, width = terms[0].shape
+    return pl.pallas_call(
+        functools.partial(add_cut_kernel, count),
+        out_shape=(jax.ShapeDtypeStruct((rows // count, width), F32),) * count,
+        in_specs=[SMEM] + [VMEM] * 4,
+        out_specs=(VMEM,) * count,
+        scratch_shapes=[pltpu.VMEM((rows, width), F32)],
+        cost_estimate=BESIDE,
+        compiler_params=pltpu.CompilerParams(vmem_limit_bytes=SMALL_LIMIT),
+    )(place, *terms)
 
 
 def last_sums_kernel(nx, ny, scale, arrived_ref, feature_ref, weight_ref):
@@ -313,7 +358,7 @@
     with jax.named_scope("tables"):
         table = slot_tables(block_coords[0, 0], count, place, sizes)
         table, early = together((table, count))
-        blocks = hold_blocks(adjacency_blocks[0, 0], early)
+        blocks, _ = hold_blocks(adjacency_blocks[0, 0], early)
 
     with jax.named_scope("forward"):
         for_sibling = forward_product(False, table, blocks, pieces, sizes)
@@ -341,52 +386,52 @@
         mixed = (term(0) + (up.astype(F32) + down.astype(F32))).astype(BF16)
 
     with jax.named_scope("dense"):
-        hidden, mixed_grad, weight_part = dense(mixed, weight, cotangent)
+        hidden, act_grad, mixed_grad = dense(mixed, weight, cotangent)
 
     with jax.named_scope("gather_rows"):
-
-        def shares(value, at, size):
-            cut = value.reshape(size, -1, width)
-            return [lax.dynamic_index_in_dim(cut, lax.rem(at + d, size), 0, keepdims=False) for d in range(size)]
 
         chunks = {0: mixed_grad}
         ahead = behind = mixed_grad
-        part = weight_part
         for step in range(1, middle + 1):
-            if step > 1:
-                part, ahead, behind = together((part, ahead, behind))
             if step < middle:
                 moved = (climb(ahead, 1), climb(behind, -1))
             else:
                 moved = (climb(ahead[:half], 1), climb(behind[half:], -1))
             if step == 1:
-                cut = shares(part, at_x, nx)
-                extra = [send(cut[d], d, 0) for d in range(1, nx)]
-                part = cut[0] + (extra[0] + extra[1] + extra[2])
-            elif step == 2:
-                cut = shares(part, at_y, ny)
-                extra = [send(cut[d], 0, d) for d in range(1, ny)]
-                part = cut[0] + (extra[0] + extra[1] + extra[2])
-            elif step == 3:
-                part = part + swap(part)
-                part = part + swap(part, 1, False)
+                first, *rest = weight_shares(place, mixed, act_grad, nx)
+                terms = [first] + [send(value, d + 1, 0) for d, value in enumerate(rest)]
+            elif step <= 3:
+                terms, _ = together((tuple(terms), ahead))
+                first, *rest = add_cut(place, terms, ny if step == 2 else 1)
+                if step == 2:
+                    terms = [first] + [send(value, 0, d + 1) for d, value in enumerate(rest)]
+                else:
+                    terms = [first, swap(first, 1, False)]
             else:
-                part = part + swap(part, 2, False)
-            ahead, behind = together(moved)
+                terms, _ = together((tuple(terms), ahead))
+                first = terms[0] + terms[1]
+                terms = [first, swap(first, 2, False)]
+            ahead, behind, terms[0] = together(moved + (terms[0],))
             if step < middle:
                 chunks[depth - step] = ahead
                 chunks[step] = behind
         chunks[middle] = jnp.concatenate([ahead, behind], axis=0)
         own_panel = jnp.concatenate([chunks[step] for step in range(depth)], axis=0)
         own_panel = own_panel.reshape(2 * depth, BLK, width)
-        part, own_panel, late = together((part, own_panel, count))
+        own_panel, part = together((own_panel, terms[0] + terms[1]))
         sibling_panel = swap(own_panel)
-        part = part + swap(part, 4, False)
-        blocks = hold_blocks(adjacency_blocks[0, 0], late)
-        tail = part.astype(BF16)
+        late, _ = together((count, own_panel))
+        part = part + swap(part)
+        blocks, mark = hold_blocks(adjacency_blocks[0, 0], late)
+        part = part + mark[:1, :1]
+        got = swap(part, 4, False)
 
     with jax.named_scope("backward"):
-        outs = backward_product(table, place, blocks, sibling_panel, own_panel, tail, sizes)
+        share = part.shape[0]
+        outs = backward_product(table, place, blocks, sibling_panel, own_panel, share, sizes)
+        outs, got, part = together((outs, got, part))
+        tail = jnp.broadcast_to((part + got).astype(BF16)[None], (nx * ny, share, width))
+        outs = lax.dynamic_update_slice(outs, tail, (0, local, 0))
 
     with jax.named_scope("sum_columns"):
         arrived = lax.all_to_all(outs, PLANE, 0, 0, tiled=True)

time: 165 us -> 152 us (0.921)
  waiting for transfers between devices: 38.4 us -> 25.8 us
  starting transfers between devices: 72.9 us -> 66.7 us
  Pallas kernels: 13.7 us -> 19 us
    ppermute x6, starting transfers between devices: 23.5 us -> 17.2 us  [swap(): return lax.ppermute(value, ('z', 'c'), pairs)]
    ppermute x16, waiting for transfers between devices: 20.5 us -> 16.1 us  [climb(): lax.ppermute(value, 'z', [(i, (i + dz) % depth) for i in range(depth)])]
    ppermute x6, waiting for transfers between devices: 6.6 us -> 2.2 us  [swap(): return lax.ppermute(value, ('z', 'c'), pairs)]
    pallas_call x3 -> x6, Pallas kernels: 3.49 us -> 7.27 us  [the longest x2 4.45 us: hold_blocks(): pl.pallas_call(hold_kernel, out_shape=(pltpu.VMEM(blocks.shape, blocks.dt...]
    ppermute x18, waiting for transfers between devices: 11.2 us -> 7.5 us  [send(): return lax.ppermute(value, PLANE, pairs)]
  transfers between devices with their start and end apart: 40 -> 40, of which waited for: 23 -> 17; matrix products, arithmetic and copies ran while one was open for 0% -> 1% of each run, Pallas kernels for 4% -> 9%
where the time goes in v3:
time: 152 us
  starting transfers between devices  66.7 us (44%)
  blocking collectives  35.1 us (23%)
  waiting for transfers between devices  25.8 us (17%)
  Pallas kernels  19 us (12%)
  local copies, waits for them, and re-layouts  2.21 us (1%)
  between operations  1.64 us (1%)
    all_to_all x1, blocking collectives, body(): arrived = lax.all_to_all(outs, PLANE, 0, 0, tiled=True)  35.1 us
    ppermute x18, starting transfers between devices, send(): return lax.ppermute(value, PLANE, pairs)  24.8 us
    ppermute x16, starting transfers between devices, climb(): lax.ppermute(value, 'z', [(i, (i + dz) % depth) for i in range(depth)])  24.8 us
    ppermute x6, starting transfers between devices, swap(): return lax.ppermute(value, ('z', 'c'), pairs)  17.2 us
    ppermute x16, waiting for transfers between devices, climb(): lax.ppermute(value, 'z', [(i, (i + dz) % depth) for i in range(depth)])  16.1 us
    ppermute x18, waiting for transfers between devices, send(): return lax.ppermute(value, PLANE, pairs)  7.5 us
    pallas_call x2, Pallas kernels, forward_product(): pl.pallas_call(functools.partial(forward_kernel, own_half, sizes), out_sh...  5.19 us
    pallas_call x2, Pallas kernels, hold_blocks(): pl.pallas_call(hold_kernel, out_shape=(pltpu.VMEM(blocks.shape, blocks.dt...  4.45 us
  transfers between devices with their start and end apart: 40, of which 17 were waited for; matrix products, arithmetic and copies ran while one was open for 1% of the time, Pallas kernels for 9%

profile of v3, /device:TPU:1, one launch (start us, length us, event | category | flops | bytes accessed | tf_op | source)
XLA Modules:
  0.0 151.7 jit_solution(629435695569643239)
XLA Ops:
  0.6 0.9 fusion.7
  1.5 3.4 %collective-permute-start = (bf16[256,128]{1,0:T(8,128)(2,1)S(1)}, bf16[256,128]{1,0:T(8,128)(2,1)S(1)}, u32[]{:S(2)}, u32[]{:S(2)}) collective-permute-start(bf16[256,128]{1,0:T(8,128)(2,1)S(1)} %get-tuple-element.162), channel_id=1, source_target_pairs={{0,6},{1,7},{8,14},{9,15},{2,0},{3,1},{10,8},{11,9},{4,2},{5,3},{1... | collective-permute-start | bytes 196616 | tf_op jit(solution)/shard_map/gather_features/ppermute | solution.py:337
  4.9 0.5 collective-permute-start.1
  5.4 0.6 collective-permute-start.2
  6.0 2.7 %collective-permute-start.3 = (bf16[256,128]{1,0:T(8,128)(2,1)S(1)}, bf16[256,128]{1,0:T(8,128)(2,1)S(1)}, u32[]{:S(2)}, u32[]{:S(2)}) collective-permute-start(bf16[256,128]{1,0:T(8,128)(2,1)S(1)} %get-tuple-element.161), channel_id=1, source_target_pairs={{0,9},{1,0},{8,1},{9,8},{2,11},{3,2},{10,3},{11,10},{4,13},{5,4},{... | collective-permute-start | bytes 196616 | tf_op jit(solution)/shard_map/gather_features/ppermute | solution.py:337
  8.8 0.3 collective-permute-start.4
  9.1 0.7 collective-permute-start.5
  9.8 0.4 collective-permute-done.2
  10.2 3.2 %collective-permute-done.4 = bf16[256,128]{1,0:T(8,128)(2,1)S(1)} collective-permute-done((bf16[256,128]{1,0:T(8,128)(2,1)S(1)}, bf16[256,128]{1,0:T(8,128)(2,1)S(1)}, u32[]{:S(2)}, u32[]{:S(2)}) %collective-permute-start.4) | collective-permute-done | bytes 65568 | tf_op jit(solution)/shard_map/gather_features/ppermute | solution.py:337
  13.4 0.6 collective-permute-done.5
  14.1 0.7 collective-permute-start.6
  14.8 0.3 collective-permute-start.7
  15.1 0.7 collective-permute-start.8
  15.8 2.1 %collective-permute-start.9 = (bf16[1024,128]{1,0:T(8,128)(2,1)S(1)}, bf16[1024,128]{1,0:T(8,128)(2,1)S(1)}, u32[]{:S(2)}, u32[]{:S(2)}) collective-permute-start(bf16[1024,128]{1,0:T(8,128)(2,1)S(1)} %pad_maximum_fusion.1.refs_4_), channel_id=1, source_target_pairs={{0,6},{1,7},{8,14},{9,15},{2,0},{3,1},{10,8},{11,9},{4,2},{5,3},{1... | collective-permute-start | bytes 786440 | tf_op jit(solution)/shard_map/gather_features/ppermute | solution.py:337
  18.0 1.2 collective-permute-start.10
  19.4 1.5 %collective-permute-start.11 = (bf16[1024,128]{1,0:T(8,128)(2,1)S(1)}, bf16[1024,128]{1,0:T(8,128)(2,1)S(1)}, u32[]{:S(2)}, u32[]{:S(2)}) collective-permute-start(bf16[1024,128]{1,0:T(8,128)(2,1)S(1)} %pad_maximum_fusion.1.refs_4_), channel_id=1, source_target_pairs={{0,2},{1,3},{8,10},{9,11},{2,4},{3,5},{10,12},{11,13},{4,6},{5,7},... | collective-permute-start | bytes 786440 | tf_op jit(solution)/shard_map/gather_features/ppermute | solution.py:337
  21.7 0.7 copy-done.2
  22.3 1.3 tables.2.table_ref
  23.7 2.5 %tables.3 = (bf16[256,128,128]{2,1,0:T(8,128)(2,1)S(1)}, f32[8,128]{1,0:T(8,128)}) custom-call(s32[1]{0:T(128)} %bitcast.41.count_ref, bf16[256,128,128]{2,1,0:T(8,128)(2,1)} %bitcast.47), custom_call_target="tpu_custom_call" | custom-call | tf_op jit(solution)/shard_map/tables/pallas_call | solution.py:210
  26.2 3.0 %collective-permute-done.8.refs_3_ = bf16[1024,128]{1,0:T(8,128)(2,1)S(1)} collective-permute-done((bf16[1024,128]{1,0:T(8,128)(2,1)S(1)}, bf16[1024,128]{1,0:T(8,128)(2,1)S(1)}, u32[]{:S(2)}, u32[]{:S(2)}) %collective-permute-start.8) | collective-permute-done | bytes 262176 | tf_op jit(solution)/shard_map/gather_features/ppermute | solution.py:337
  29.2 2.8 %forward.2 = bf16[16,128,256]{2,1,0:T(8,128)(2,1)S(1)} custom-call(s32[8,384]{1,0:T(8,128)S(1)} %tables.2.table_ref, bf16[256,128,128]{2,1,0:T(8,128)(2,1)S(1)} %get-tuple-element.79.blocks_ref, bf16[1024,128]{1,0:T(8,128)(2,1)S(1)} %pad_maximum_fusion.refs_0_, bf16[1024,128]{1,0:T(8,128)(2,1)S(1)} %collective-permute-done.6.refs_1_, ...), custom_call_target="tpu_custom_call" | custom-call | tf_op jit(solution)/shard_map/forward/pallas_call | solution.py:138
  32.1 4.4 %collective-permute-start.12 = (bf16[16,128,256]{2,1,0:T(8,128)(2,1)S(1)}, bf16[16,128,256]{2,1,0:T(8,128)(2,1)S(1)}, u32[]{:S(2)}, u32[]{:S(2)}) collective-permute-start(bf16[16,128,256]{2,1,0:T(8,128)(2,1)S(1)} %forward.2), channel_id=1, source_target_pairs={{0,16},{16,0},{32,48},{48,32},{64,80},{80,64},{96,112},{112,96},{1... | collective-permute-start | bytes 3145736 | tf_op jit(solution)/shard_map/forward/ppermute | solution.py:344
  36.5 2.3 %forward.3 = bf16[16,128,256]{2,1,0:T(8,128)(2,1)S(1)} custom-call(s32[8,384]{1,0:T(8,128)S(1)} %tables.2.table_ref, bf16[256,128,128]{2,1,0:T(8,128)(2,1)S(1)} %get-tuple-element.79.blocks_ref, bf16[1024,128]{1,0:T(8,128)(2,1)S(1)} %pad_maximum_fusion.refs_0_, bf16[1024,128]{1,0:T(8,128)(2,1)S(1)} %collective-permute-done.6.refs_1_, ...), custom_call_target="tpu_custom_call" | custom-call | tf_op jit(solution)/shard_map/forward/pallas_call | solution.py:138
  39.1 2.2 %collective-permute-start.13 = (bf16[128,256]{1,0:T(8,128)(2,1)S(1)}, bf16[128,256]{1,0:T(8,128)(2,1)S(1)}, u32[]{:S(2)}, u32[]{:S(2)}) collective-permute-start(bf16[128,256]{1,0:T(8,128)(2,1)S(1)} %get-tuple-element.160), channel_id=1, source_target_pairs={{0,32},{32,64},{64,96},{96,128},{128,160},{160,192},{192,224},{224... | collective-permute-start | bytes 196616 | tf_op jit(solution)/shard_map/sum_rows/ppermute | solution.py:340
  41.4 3.4 %collective-permute-start.14 = (bf16[128,256]{1,0:T(8,128)(2,1)S(1)}, bf16[128,256]{1,0:T(8,128)(2,1)S(1)}, u32[]{:S(2)}, u32[]{:S(2)}) collective-permute-start(bf16[128,256]{1,0:T(8,128)(2,1)S(1)} %get-tuple-element.159), channel_id=1, source_target_pairs={{0,224},{32,0},{64,32},{96,64},{128,96},{160,128},{192,160},{224,1... | collective-permute-start | bytes 196616 | tf_op jit(solution)/shard_map/sum_rows/ppermute | solution.py:340
  44.8 2.1 %collective-permute-done.13 = bf16[128,256]{1,0:T(8,128)(2,1)S(1)} collective-permute-done((bf16[128,256]{1,0:T(8,128)(2,1)S(1)}, bf16[128,256]{1,0:T(8,128)(2,1)S(1)}, u32[]{:S(2)}, u32[]{:S(2)}) %collective-permute-start.13) | collective-permute-done | bytes 65568 | tf_op jit(solution)/shard_map/sum_rows/ppermute | solution.py:340
  47.0 2.7 %collective-permute-start.16 = (bf16[256,256]{1,0:T(8,128)(2,1)S(1)}, bf16[256,256]{1,0:T(8,128)(2,1)S(1)}, u32[]{:S(2)}, u32[]{:S(2)}) collective-permute-start(bf16[256,256]{1,0:T(8,128)(2,1)S(1)} %fusion.2), channel_id=1, source_target_pairs={{0,224},{32,0},{64,32},{96,64},{128,96},{160,128},{192,160},{224,1... | collective-permute-start | bytes 393224 | tf_op jit(solution)/shard_map/sum_rows/ppermute | solution.py:340
  49.7 2.7 %collective-permute-done.15 = bf16[256,256]{1,0:T(8,128)(2,1)S(1)} collective-permute-done((bf16[256,256]{1,0:T(8,128)(2,1)S(1)}, bf16[256,256]{1,0:T(8,128)(2,1)S(1)}, u32[]{:S(2)}, u32[]{:S(2)}) %collective-permute-start.15) | collective-permute-done | bytes 131104 | tf_op jit(solution)/shard_map/sum_rows/ppermute | solution.py:340
  52.4 0.6 collective-permute-done.16
  53.0 1.4 collective-permute-start.17
  54.4 1.3 collective-permute-start.18
  55.8 2.4 %collective-permute-done.17 = bf16[256,256]{1,0:T(8,128)(2,1)S(1)} collective-permute-done((bf16[256,256]{1,0:T(8,128)(2,1)S(1)}, bf16[256,256]{1,0:T(8,128)(2,1)S(1)}, u32[]{:S(2)}, u32[]{:S(2)}) %collective-permute-start.17) | collective-permute-done | bytes 131104 | tf_op jit(solution)/shard_map/sum_rows/ppermute | solution.py:340
  58.3 2.4 %collective-permute-start.19 = (bf16[256,256]{1,0:T(8,128)(2,1)S(1)}, bf16[256,256]{1,0:T(8,128)(2,1)S(1)}, u32[]{:S(2)}, u32[]{:S(2)}) collective-permute-start(bf16[256,256]{1,0:T(8,128)(2,1)S(1)} %get-tuple-element.104), channel_id=1, source_target_pairs={{0,32},{32,64},{64,96},{96,128},{128,160},{160,192},{192,224},{224... | collective-permute-start | bytes 393224 | tf_op jit(solution)/shard_map/sum_rows/ppermute | solution.py:340
  60.7 0.4 collective-permute-start.20
  61.1 2.4 %collective-permute-done.19 = bf16[256,256]{1,0:T(8,128)(2,1)S(1)} collective-permute-done((bf16[256,256]{1,0:T(8,128)(2,1)S(1)}, bf16[256,256]{1,0:T(8,128)(2,1)S(1)}, u32[]{:S(2)}, u32[]{:S(2)}) %collective-permute-start.19) | collective-permute-done | bytes 131104 | tf_op jit(solution)/shard_map/sum_rows/ppermute | solution.py:340
  63.5 1.1 collective-permute-done.20
  64.6 0.9 dense.1
  65.5 2.3 %collective-permute-start.21 = (bf16[256,256]{1,0:T(8,128)(2,1)S(1)}, bf16[256,256]{1,0:T(8,128)(2,1)S(1)}, u32[]{:S(2)}, u32[]{:S(2)}) collective-permute-start(bf16[256,256]{1,0:T(8,128)(2,1)S(1)} %get-tuple-element.109), channel_id=1, source_target_pairs={{0,32},{32,64},{64,96},{96,128},{128,160},{160,192},{192,224},{224... | collective-permute-start | bytes 393224 | tf_op jit(solution)/shard_map/gather_rows/ppermute | solution.py:340
  67.8 0.4 collective-permute-start.22
  68.2 0.8 gather_rows.4
  69.0 1.8 %collective-permute-start.25 = (f32[64,256]{1,0:T(8,128)S(1)}, f32[64,256]{1,0:T(8,128)S(1)}, u32[]{:S(2)}, u32[]{:S(2)}) collective-permute-start(f32[64,256]{1,0:T(8,128)S(1)} %get-tuple-element.115), channel_id=1, source_target_pairs={{0,2},{1,3},{8,10},{9,11},{2,4},{3,5},{10,12},{11,13},{4,6},{5,7},... | collective-permute-start | bytes 196616 | tf_op jit(solution)/shard_map/gather_rows/ppermute | solution.py:337
  70.7 2.1 %collective-permute-start.26 = (f32[64,256]{1,0:T(8,128)S(1)}, f32[64,256]{1,0:T(8,128)S(1)}, u32[]{:S(2)}, u32[]{:S(2)}) collective-permute-start(f32[64,256]{1,0:T(8,128)S(1)} %get-tuple-element.116), channel_id=1, source_target_pairs={{0,4},{1,5},{8,12},{9,13},{2,6},{3,7},{10,14},{11,15},{4,0},{5,1},... | collective-permute-start | bytes 196616 | tf_op jit(solution)/shard_map/gather_rows/ppermute | solution.py:337
  72.9 0.4 collective-permute-start.27
  73.3 0.4 collective-permute-done.22
  73.7 1.2 collective-permute-start.23
  74.9 1.5 collective-permute-start.24
  76.4 0.6 gather_rows.5
  77.0 1.1 collective-permute-start.30
  78.1 2.5 %collective-permute-start.31 = (f32[16,256]{1,0:T(8,128)S(1)}, f32[16,256]{1,0:T(8,128)S(1)}, u32[]{:S(2)}, u32[]{:S(2)}) collective-permute-start(f32[16,256]{1,0:T(8,128)S(1)} %get-tuple-element.127), channel_id=1, source_target_pairs={{0,8},{1,9},{8,0},{9,1},{2,10},{3,11},{10,2},{11,3},{4,12},{5,13},... | collective-permute-start | bytes 49160 | tf_op jit(solution)/shard_map/gather_rows/ppermute | solution.py:337
  80.6 2.0 %collective-permute-start.32 = (f32[16,256]{1,0:T(8,128)S(1)}, f32[16,256]{1,0:T(8,128)S(1)}, u32[]{:S(2)}, u32[]{:S(2)}) collective-permute-start(f32[16,256]{1,0:T(8,128)S(1)} %get-tuple-element.128), channel_id=1, source_target_pairs={{0,9},{1,0},{8,1},{9,8},{2,11},{3,2},{10,3},{11,10},{4,13},{5,4},{... | collective-permute-start | bytes 49160 | tf_op jit(solution)/shard_map/gather_rows/ppermute | solution.py:337
  82.7 2.7 %collective-permute-start.29 = (bf16[256,256]{1,0:T(8,128)(2,1)S(1)}, bf16[256,256]{1,0:T(8,128)(2,1)S(1)}, u32[]{:S(2)}, u32[]{:S(2)}) collective-permute-start(bf16[256,256]{1,0:T(8,128)(2,1)S(1)} %collective-permute-done.24), channel_id=1, source_target_pairs={{0,224},{32,0},{64,32},{96,64},{128,96},{160,128},{192,160},{224,1... | collective-permute-start | bytes 393224 | tf_op jit(solution)/shard_map/gather_rows/ppermute | solution.py:340
  85.4 0.5 gather_rows.6
  86.1 2.9 %collective-permute-done.28 = bf16[256,256]{1,0:T(8,128)(2,1)S(1)} collective-permute-done((bf16[256,256]{1,0:T(8,128)(2,1)S(1)}, bf16[256,256]{1,0:T(8,128)(2,1)S(1)}, u32[]{:S(2)}, u32[]{:S(2)}) %collective-permute-start.28) | collective-permute-done | bytes 131104 | tf_op jit(solution)/shard_map/gather_rows/ppermute | solution.py:340
  89.1 2.7 %collective-permute-start.34 = (bf16[128,256]{1,0:T(8,128)(2,1)S(1)}, bf16[128,256]{1,0:T(8,128)(2,1)S(1)}, u32[]{:S(2)}, u32[]{:S(2)}) collective-permute-start(bf16[128,256]{1,0:T(8,128)(2,1)S(1)} %slice.114), channel_id=1, source_target_pairs={{0,224},{32,0},{64,32},{96,64},{128,96},{160,128},{192,160},{224,1... | collective-permute-start | bytes 196616 | tf_op jit(solution)/shard_map/gather_rows/ppermute | solution.py:340
  91.9 1.5 %collective-permute-done.33 = bf16[128,256]{1,0:T(8,128)(2,1)S(1)} collective-permute-done((bf16[128,256]{1,0:T(8,128)(2,1)S(1)}, bf16[128,256]{1,0:T(8,128)(2,1)S(1)}, u32[]{:S(2)}, u32[]{:S(2)}) %collective-permute-start.33) | collective-permute-done | bytes 65568 | tf_op jit(solution)/shard_map/gather_rows/ppermute | solution.py:340
  93.5 2.0 %collective-permute-done.36 = f32[16,256]{1,0:T(8,128)S(1)} collective-permute-done((f32[16,256]{1,0:T(8,128)S(1)}, f32[16,256]{1,0:T(8,128)S(1)}, u32[]{:S(2)}, u32[]{:S(2)}) %collective-permute-start.36) | collective-permute-done | bytes 16416 | tf_op jit(solution)/shard_map/gather_rows/ppermute | solution.py:344
  95.5 10.3 %collective-permute-start.37 = (bf16[16,128,256]{2,1,0:T(8,128)(2,1)S(1)}, bf16[16,128,256]{2,1,0:T(8,128)(2,1)S(1)}, u32[]{:S(2)}, u32[]{:S(2)}) collective-permute-start(bf16[16,128,256]{2,1,0:T(8,128)(2,1)S(1)} %bitcast.44), channel_id=1, source_target_pairs={{0,16},{16,0},{32,48},{48,32},{64,80},{80,64},{96,112},{112,96},{1... | collective-permute-start | bytes 3145736 | tf_op jit(solution)/shard_map/gather_rows/ppermute | solution.py:344
  105.9 1.9 %gather_rows.7 = (bf16[256,128,128]{2,1,0:T(8,128)(2,1)S(1)}, f32[8,128]{1,0:T(8,128)S(1)}) custom-call(s32[1]{0:T(128)} %bitcast.42.count_ref, bf16[256,128,128]{2,1,0:T(8,128)(2,1)} %bitcast.48), custom_call_target="tpu_custom_call" | custom-call | tf_op jit(solution)/shard_map/gather_rows/pallas_call | solution.py:210
  107.8 0.5 slice.115
  108.4 0.7 add_add_fusion
  109.0 2.2 %collective-permute-start.39 = (f32[16,256]{1,0:T(8,128)S(1)}, f32[16,256]{1,0:T(8,128)S(1)}, u32[]{:S(2)}, u32[]{:S(2)}) collective-permute-start(f32[16,256]{1,0:T(8,128)S(1)} %add_add_fusion), channel_id=1, source_target_pairs={{0,128},{16,144},{32,160},{48,176},{64,192},{80,208},{96,224},{112... | collective-permute-start | bytes 49160 | tf_op jit(solution)/shard_map/gather_rows/ppermute | solution.py:344
  111.2 4.2 %backward.1 = bf16[16,272,256]{2,1,0:T(8,128)(2,1)S(1)} custom-call(s32[8,384]{1,0:T(8,128)S(1)} %tables.2.table_ref, s32[4]{0:T(128)S(1)} %pad_add_fusion.place_ref, bf16[256,128,128]{2,1,0:T(8,128)(2,1)S(1)} %get-tuple-element.143.blocks_ref, bf16[16,128,256]{2,1,0:T(8,128)(2,1)S(1)} %collective-permute-done.37.sibling_ref, bf16[16,128,256]{2,1,0:T(8,128)(2,1)S(1)} %bitcast.45), custom_call_target="tpu_custom_call" | custom-call | flops 4000000000 | tf_op jit(solution)/shard_map/backward/pallas_call | solution.py:169
  115.6 35.1 %all_to_all.5.arrived_ref = bf16[16,272,256]{2,1,0:T(8,128)(2,1)S(1)} all-to-all(bf16[16,272,256]{2,1,0:T(8,128)(2,1)S(1)} %broadcast_dynamic-update-slice_fusion), channel_id=1, replica_groups=mesh['z'=8,'c'=2,'yh'=2,'x'=4,'yl'=2] {'yh','x','yl'}, dimensions={0} | all-to-all | bytes 4456448 | tf_op jit(solution)/shard_map/sum_columns/all_to_all | solution.py:437
  150.7 1.0 sum_columns.1
  (63 shorter events, 1.9 us)
Async XLA Ops:
  1.5 7.6 %collective-permute-start = (bf16[256,128]{1,0:T(8,128)(2,1)S(1)}, bf16[256,128]{1,0:T(8,128)(2,1)S(1)}, u32[]{:S(2)}, u32[]{:S(2)}) collective-permute-start(bf16[256,128]{1,0:T(8,128)(2,1)S(1)} %get-tuple-element.162), channel_id=1, source_target_pairs={{0,6},{1,7},{8,14},{9,15},{2,0},{3,1},{10,8},{11,9},{4,2},{5,3},{1... | collective-permute-start | bytes 196616 | tf_op jit(solution)/shard_map/gather_features/ppermute | solution.py:337
  4.9 4.9 %collective-permute-start.1 = (bf16[256,128]{1,0:T(8,128)(2,1)S(1)}, bf16[256,128]{1,0:T(8,128)(2,1)S(1)}, u32[]{:S(2)}, u32[]{:S(2)}) collective-permute-start(bf16[256,128]{1,0:T(8,128)(2,1)S(1)} %get-tuple-element.162), channel_id=1, source_target_pairs={{0,4},{1,5},{8,12},{9,13},{2,6},{3,7},{10,14},{11,15},{4,0},{5,1},... | collective-permute-start | bytes 196616 | tf_op jit(solution)/shard_map/gather_features/ppermute | solution.py:337
  5.4 4.8 %collective-permute-start.2 = (bf16[256,128]{1,0:T(8,128)(2,1)S(1)}, bf16[256,128]{1,0:T(8,128)(2,1)S(1)}, u32[]{:S(2)}, u32[]{:S(2)}) collective-permute-start(bf16[256,128]{1,0:T(8,128)(2,1)S(1)} %get-tuple-element.162), channel_id=1, source_target_pairs={{0,2},{1,3},{8,10},{9,11},{2,4},{3,5},{10,12},{11,13},{4,6},{5,7},... | collective-permute-start | bytes 196616 | tf_op jit(solution)/shard_map/gather_features/ppermute | solution.py:337
  6.0 4.2 %collective-permute-start.3 = (bf16[256,128]{1,0:T(8,128)(2,1)S(1)}, bf16[256,128]{1,0:T(8,128)(2,1)S(1)}, u32[]{:S(2)}, u32[]{:S(2)}) collective-permute-start(bf16[256,128]{1,0:T(8,128)(2,1)S(1)} %get-tuple-element.161), channel_id=1, source_target_pairs={{0,9},{1,0},{8,1},{9,8},{2,11},{3,2},{10,3},{11,10},{4,13},{5,4},{... | collective-permute-start | bytes 196616 | tf_op jit(solution)/shard_map/gather_features/ppermute | solution.py:337
  8.8 4.7 %collective-permute-start.4 = (bf16[256,128]{1,0:T(8,128)(2,1)S(1)}, bf16[256,128]{1,0:T(8,128)(2,1)S(1)}, u32[]{:S(2)}, u32[]{:S(2)}) collective-permute-start(bf16[256,128]{1,0:T(8,128)(2,1)S(1)} %get-tuple-element.161), channel_id=1, source_target_pairs={{0,8},{1,9},{8,0},{9,1},{2,10},{3,11},{10,2},{11,3},{4,12},{5,13},... | collective-permute-start | bytes 196616 | tf_op jit(solution)/shard_map/gather_features/ppermute | solution.py:337
  9.1 5.0 %collective-permute-start.5 = (bf16[256,128]{1,0:T(8,128)(2,1)S(1)}, bf16[256,128]{1,0:T(8,128)(2,1)S(1)}, u32[]{:S(2)}, u32[]{:S(2)}) collective-permute-start(bf16[256,128]{1,0:T(8,128)(2,1)S(1)} %get-tuple-element.161), channel_id=1, source_target_pairs={{0,1},{1,8},{8,9},{9,0},{2,3},{3,10},{10,11},{11,2},{4,5},{5,12},{... | collective-permute-start | bytes 196616 | tf_op jit(solution)/shard_map/gather_features/ppermute | solution.py:337
  14.1 5.3 %collective-permute-start.6 = (bf16[1024,128]{1,0:T(8,128)(2,1)S(1)}, bf16[1024,128]{1,0:T(8,128)(2,1)S(1)}, u32[]{:S(2)}, u32[]{:S(2)}) collective-permute-start(bf16[1024,128]{1,0:T(8,128)(2,1)S(1)} %pad_maximum_fusion.refs_0_), channel_id=1, source_target_pairs={{0,9},{1,0},{8,1},{9,8},{2,11},{3,2},{10,3},{11,10},{4,13},{5,4},{... | collective-permute-start | bytes 786440 | tf_op jit(solution)/shard_map/gather_features/ppermute | solution.py:337
  14.8 11.4 %collective-permute-start.7 = (bf16[1024,128]{1,0:T(8,128)(2,1)S(1)}, bf16[1024,128]{1,0:T(8,128)(2,1)S(1)}, u32[]{:S(2)}, u32[]{:S(2)}) collective-permute-start(bf16[1024,128]{1,0:T(8,128)(2,1)S(1)} %pad_maximum_fusion.refs_0_), channel_id=1, source_target_pairs={{0,8},{1,9},{8,0},{9,1},{2,10},{3,11},{10,2},{11,3},{4,12},{5,13},... | collective-permute-start | bytes 786440 | tf_op jit(solution)/shard_map/gather_features/ppermute | solution.py:337
  15.1 14.1 %collective-permute-start.8 = (bf16[1024,128]{1,0:T(8,128)(2,1)S(1)}, bf16[1024,128]{1,0:T(8,128)(2,1)S(1)}, u32[]{:S(2)}, u32[]{:S(2)}) collective-permute-start(bf16[1024,128]{1,0:T(8,128)(2,1)S(1)} %pad_maximum_fusion.refs_0_), channel_id=1, source_target_pairs={{0,1},{1,8},{8,9},{9,0},{2,3},{3,10},{10,11},{11,2},{4,5},{5,12},{... | collective-permute-start | bytes 786440 | tf_op jit(solution)/shard_map/gather_features/ppermute | solution.py:337
  15.8 13.4 %collective-permute-start.9 = (bf16[1024,128]{1,0:T(8,128)(2,1)S(1)}, bf16[1024,128]{1,0:T(8,128)(2,1)S(1)}, u32[]{:S(2)}, u32[]{:S(2)}) collective-permute-start(bf16[1024,128]{1,0:T(8,128)(2,1)S(1)} %pad_maximum_fusion.1.refs_4_), channel_id=1, source_target_pairs={{0,6},{1,7},{8,14},{9,15},{2,0},{3,1},{10,8},{11,9},{4,2},{5,3},{1... | collective-permute-start | bytes 786440 | tf_op jit(solution)/shard_map/gather_features/ppermute | solution.py:337
  18.0 11.2 %collective-permute-start.10 = (bf16[1024,128]{1,0:T(8,128)(2,1)S(1)}, bf16[1024,128]{1,0:T(8,128)(2,1)S(1)}, u32[]{:S(2)}, u32[]{:S(2)}) collective-permute-start(bf16[1024,128]{1,0:T(8,128)(2,1)S(1)} %pad_maximum_fusion.1.refs_4_), channel_id=1, source_target_pairs={{0,4},{1,5},{8,12},{9,13},{2,6},{3,7},{10,14},{11,15},{4,0},{5,1},... | collective-permute-start | bytes 786440 | tf_op jit(solution)/shard_map/gather_features/ppermute | solution.py:337
  19.4 9.8 %collective-permute-start.11 = (bf16[1024,128]{1,0:T(8,128)(2,1)S(1)}, bf16[1024,128]{1,0:T(8,128)(2,1)S(1)}, u32[]{:S(2)}, u32[]{:S(2)}) collective-permute-start(bf16[1024,128]{1,0:T(8,128)(2,1)S(1)} %pad_maximum_fusion.1.refs_4_), channel_id=1, source_target_pairs={{0,2},{1,3},{8,10},{9,11},{2,4},{3,5},{10,12},{11,13},{4,6},{5,7},... | collective-permute-start | bytes 786440 | tf_op jit(solution)/shard_map/gather_features/ppermute | solution.py:337
  21.7 0.7 copy-start.2
  32.1 6.7 %collective-permute-start.12 = (bf16[16,128,256]{2,1,0:T(8,128)(2,1)S(1)}, bf16[16,128,256]{2,1,0:T(8,128)(2,1)S(1)}, u32[]{:S(2)}, u32[]{:S(2)}) collective-permute-start(bf16[16,128,256]{2,1,0:T(8,128)(2,1)S(1)} %forward.2), channel_id=1, source_target_pairs={{0,16},{16,0},{32,48},{48,32},{64,80},{80,64},{96,112},{112,96},{1... | collective-permute-start | bytes 3145736 | tf_op jit(solution)/shard_map/forward/ppermute | solution.py:344
  39.1 25.5 %copy-start = (bf16[256,256]{1,0:T(8,128)(2,1)S(1)}, bf16[256,256]{1,0:T(8,128)(2,1)}, u32[]{:S(2)}) copy-start(bf16[256,256]{1,0:T(8,128)(2,1)} %weight_ref.1) | copy-start | bytes 393220
  39.1 25.5 %copy-start.1 = (bf16[256,256]{1,0:T(8,128)(2,1)S(1)}, bf16[256,256]{1,0:T(8,128)(2,1)}, u32[]{:S(2)}) copy-start(bf16[256,256]{1,0:T(8,128)(2,1)} %cotangent_ref.1) | copy-start | bytes 393220
  39.1 7.7 %collective-permute-start.13 = (bf16[128,256]{1,0:T(8,128)(2,1)S(1)}, bf16[128,256]{1,0:T(8,128)(2,1)S(1)}, u32[]{:S(2)}, u32[]{:S(2)}) collective-permute-start(bf16[128,256]{1,0:T(8,128)(2,1)S(1)} %get-tuple-element.160), channel_id=1, source_target_pairs={{0,32},{32,64},{64,96},{96,128},{128,160},{160,192},{192,224},{224... | collective-permute-start | bytes 196616 | tf_op jit(solution)/shard_map/sum_rows/ppermute | solution.py:340
  41.4 5.5 %collective-permute-start.14 = (bf16[128,256]{1,0:T(8,128)(2,1)S(1)}, bf16[128,256]{1,0:T(8,128)(2,1)S(1)}, u32[]{:S(2)}, u32[]{:S(2)}) collective-permute-start(bf16[128,256]{1,0:T(8,128)(2,1)S(1)} %get-tuple-element.159), channel_id=1, source_target_pairs={{0,224},{32,0},{64,32},{96,64},{128,96},{160,128},{192,160},{224,1... | collective-permute-start | bytes 196616 | tf_op jit(solution)/shard_map/sum_rows/ppermute | solution.py:340
  46.9 5.4 %collective-permute-start.15 = (bf16[256,256]{1,0:T(8,128)(2,1)S(1)}, bf16[256,256]{1,0:T(8,128)(2,1)S(1)}, u32[]{:S(2)}, u32[]{:S(2)}) collective-permute-start(bf16[256,256]{1,0:T(8,128)(2,1)S(1)} %fusion.3), channel_id=1, source_target_pairs={{0,32},{32,64},{64,96},{96,128},{128,160},{160,192},{192,224},{224... | collective-permute-start | bytes 393224 | tf_op jit(solution)/shard_map/sum_rows/ppermute | solution.py:340
  47.0 5.9 %collective-permute-start.16 = (bf16[256,256]{1,0:T(8,128)(2,1)S(1)}, bf16[256,256]{1,0:T(8,128)(2,1)S(1)}, u32[]{:S(2)}, u32[]{:S(2)}) collective-permute-start(bf16[256,256]{1,0:T(8,128)(2,1)S(1)} %fusion.2), channel_id=1, source_target_pairs={{0,224},{32,0},{64,32},{96,64},{128,96},{160,128},{192,160},{224,1... | collective-permute-start | bytes 393224 | tf_op jit(solution)/shard_map/sum_rows/ppermute | solution.py:340
  53.0 5.1 %collective-permute-start.17 = (bf16[256,256]{1,0:T(8,128)(2,1)S(1)}, bf16[256,256]{1,0:T(8,128)(2,1)S(1)}, u32[]{:S(2)}, u32[]{:S(2)}) collective-permute-start(bf16[256,256]{1,0:T(8,128)(2,1)S(1)} %fusion.4), channel_id=1, source_target_pairs={{0,32},{32,64},{64,96},{96,128},{128,160},{160,192},{192,224},{224... | collective-permute-start | bytes 393224 | tf_op jit(solution)/shard_map/sum_rows/ppermute | solution.py:340
  54.4 3.8 %collective-permute-start.18 = (bf16[256,256]{1,0:T(8,128)(2,1)S(1)}, bf16[256,256]{1,0:T(8,128)(2,1)S(1)}, u32[]{:S(2)}, u32[]{:S(2)}) collective-permute-start(bf16[256,256]{1,0:T(8,128)(2,1)S(1)} %fusion.1), channel_id=1, source_target_pairs={{0,224},{32,0},{64,32},{96,64},{128,96},{160,128},{192,160},{224,1... | collective-permute-start | bytes 393224 | tf_op jit(solution)/shard_map/sum_rows/ppermute | solution.py:340
  58.3 5.1 %collective-permute-start.19 = (bf16[256,256]{1,0:T(8,128)(2,1)S(1)}, bf16[256,256]{1,0:T(8,128)(2,1)S(1)}, u32[]{:S(2)}, u32[]{:S(2)}) collective-permute-start(bf16[256,256]{1,0:T(8,128)(2,1)S(1)} %get-tuple-element.104), channel_id=1, source_target_pairs={{0,32},{32,64},{64,96},{96,128},{128,160},{160,192},{192,224},{224... | collective-permute-start | bytes 393224 | tf_op jit(solution)/shard_map/sum_rows/ppermute | solution.py:340
  60.7 3.8 %collective-permute-start.20 = (bf16[256,256]{1,0:T(8,128)(2,1)S(1)}, bf16[256,256]{1,0:T(8,128)(2,1)S(1)}, u32[]{:S(2)}, u32[]{:S(2)}) collective-permute-start(bf16[256,256]{1,0:T(8,128)(2,1)S(1)} %get-tuple-element.105), channel_id=1, source_target_pairs={{0,224},{32,0},{64,32},{96,64},{128,96},{160,128},{192,160},{224,1... | collective-permute-start | bytes 393224 | tf_op jit(solution)/shard_map/sum_rows/ppermute | solution.py:340
  65.5 7.8 %collective-permute-start.21 = (bf16[256,256]{1,0:T(8,128)(2,1)S(1)}, bf16[256,256]{1,0:T(8,128)(2,1)S(1)}, u32[]{:S(2)}, u32[]{:S(2)}) collective-permute-start(bf16[256,256]{1,0:T(8,128)(2,1)S(1)} %get-tuple-element.109), channel_id=1, source_target_pairs={{0,32},{32,64},{64,96},{96,128},{128,160},{160,192},{192,224},{224... | collective-permute-start | bytes 393224 | tf_op jit(solution)/shard_map/gather_rows/ppermute | solution.py:340
  67.8 5.9 %collective-permute-start.22 = (bf16[256,256]{1,0:T(8,128)(2,1)S(1)}, bf16[256,256]{1,0:T(8,128)(2,1)S(1)}, u32[]{:S(2)}, u32[]{:S(2)}) collective-permute-start(bf16[256,256]{1,0:T(8,128)(2,1)S(1)} %get-tuple-element.109), channel_id=1, source_target_pairs={{0,224},{32,0},{64,32},{96,64},{128,96},{160,128},{192,160},{224,1... | collective-permute-start | bytes 393224 | tf_op jit(solution)/shard_map/gather_rows/ppermute | solution.py:340
  69.0 7.4 %collective-permute-start.25 = (f32[64,256]{1,0:T(8,128)S(1)}, f32[64,256]{1,0:T(8,128)S(1)}, u32[]{:S(2)}, u32[]{:S(2)}) collective-permute-start(f32[64,256]{1,0:T(8,128)S(1)} %get-tuple-element.115), channel_id=1, source_target_pairs={{0,2},{1,3},{8,10},{9,11},{2,4},{3,5},{10,12},{11,13},{4,6},{5,7},... | collective-permute-start | bytes 196616 | tf_op jit(solution)/shard_map/gather_rows/ppermute | solution.py:337
  70.7 5.6 %collective-permute-start.26 = (f32[64,256]{1,0:T(8,128)S(1)}, f32[64,256]{1,0:T(8,128)S(1)}, u32[]{:S(2)}, u32[]{:S(2)}) collective-permute-start(f32[64,256]{1,0:T(8,128)S(1)} %get-tuple-element.116), channel_id=1, source_target_pairs={{0,4},{1,5},{8,12},{9,13},{2,6},{3,7},{10,14},{11,15},{4,0},{5,1},... | collective-permute-start | bytes 196616 | tf_op jit(solution)/shard_map/gather_rows/ppermute | solution.py:337
  72.9 3.5 %collective-permute-start.27 = (f32[64,256]{1,0:T(8,128)S(1)}, f32[64,256]{1,0:T(8,128)S(1)}, u32[]{:S(2)}, u32[]{:S(2)}) collective-permute-start(f32[64,256]{1,0:T(8,128)S(1)} %get-tuple-element.117), channel_id=1, source_target_pairs={{0,6},{1,7},{8,14},{9,15},{2,0},{3,1},{10,8},{11,9},{4,2},{5,3},{1... | collective-permute-start | bytes 196616 | tf_op jit(solution)/shard_map/gather_rows/ppermute | solution.py:337
  73.7 8.9 %collective-permute-start.23 = (bf16[256,256]{1,0:T(8,128)(2,1)S(1)}, bf16[256,256]{1,0:T(8,128)(2,1)S(1)}, u32[]{:S(2)}, u32[]{:S(2)}) collective-permute-start(bf16[256,256]{1,0:T(8,128)(2,1)S(1)} %collective-permute-done.21), channel_id=1, source_target_pairs={{0,32},{32,64},{64,96},{96,128},{128,160},{160,192},{192,224},{224... | collective-permute-start | bytes 393224 | tf_op jit(solution)/shard_map/gather_rows/ppermute | solution.py:340
  74.9 7.7 %collective-permute-start.24 = (bf16[256,256]{1,0:T(8,128)(2,1)S(1)}, bf16[256,256]{1,0:T(8,128)(2,1)S(1)}, u32[]{:S(2)}, u32[]{:S(2)}) collective-permute-start(bf16[256,256]{1,0:T(8,128)(2,1)S(1)} %collective-permute-done.22), channel_id=1, source_target_pairs={{0,224},{32,0},{64,32},{96,64},{128,96},{160,128},{192,160},{224,1... | collective-permute-start | bytes 393224 | tf_op jit(solution)/shard_map/gather_rows/ppermute | solution.py:340
  77.0 8.4 %collective-permute-start.30 = (f32[16,256]{1,0:T(8,128)S(1)}, f32[16,256]{1,0:T(8,128)S(1)}, u32[]{:S(2)}, u32[]{:S(2)}) collective-permute-start(f32[16,256]{1,0:T(8,128)S(1)} %get-tuple-element.126), channel_id=1, source_target_pairs={{0,1},{1,8},{8,9},{9,0},{2,3},{3,10},{10,11},{11,2},{4,5},{5,12},{... | collective-permute-start | bytes 49160 | tf_op jit(solution)/shard_map/gather_rows/ppermute | solution.py:337
  78.1 7.3 %collective-permute-start.31 = (f32[16,256]{1,0:T(8,128)S(1)}, f32[16,256]{1,0:T(8,128)S(1)}, u32[]{:S(2)}, u32[]{:S(2)}) collective-permute-start(f32[16,256]{1,0:T(8,128)S(1)} %get-tuple-element.127), channel_id=1, source_target_pairs={{0,8},{1,9},{8,0},{9,1},{2,10},{3,11},{10,2},{11,3},{4,12},{5,13},... | collective-permute-start | bytes 49160 | tf_op jit(solution)/shard_map/gather_rows/ppermute | solution.py:337
  80.6 4.8 %collective-permute-start.32 = (f32[16,256]{1,0:T(8,128)S(1)}, f32[16,256]{1,0:T(8,128)S(1)}, u32[]{:S(2)}, u32[]{:S(2)}) collective-permute-start(f32[16,256]{1,0:T(8,128)S(1)} %get-tuple-element.128), channel_id=1, source_target_pairs={{0,9},{1,0},{8,1},{9,8},{2,11},{3,2},{10,3},{11,10},{4,13},{5,4},{... | collective-permute-start | bytes 49160 | tf_op jit(solution)/shard_map/gather_rows/ppermute | solution.py:337
  82.6 6.3 %collective-permute-start.28 = (bf16[256,256]{1,0:T(8,128)(2,1)S(1)}, bf16[256,256]{1,0:T(8,128)(2,1)S(1)}, u32[]{:S(2)}, u32[]{:S(2)}) collective-permute-start(bf16[256,256]{1,0:T(8,128)(2,1)S(1)} %collective-permute-done.23), channel_id=1, source_target_pairs={{0,32},{32,64},{64,96},{96,128},{128,160},{160,192},{192,224},{224... | collective-permute-start | bytes 393224 | tf_op jit(solution)/shard_map/gather_rows/ppermute | solution.py:340
  82.7 6.3 %collective-permute-start.29 = (bf16[256,256]{1,0:T(8,128)(2,1)S(1)}, bf16[256,256]{1,0:T(8,128)(2,1)S(1)}, u32[]{:S(2)}, u32[]{:S(2)}) collective-permute-start(bf16[256,256]{1,0:T(8,128)(2,1)S(1)} %collective-permute-done.24), channel_id=1, source_target_pairs={{0,224},{32,0},{64,32},{96,64},{128,96},{160,128},{192,160},{224,1... | collective-permute-start | bytes 393224 | tf_op jit(solution)/shard_map/gather_rows/ppermute | solution.py:340
  86.0 5.8 %collective-permute-start.35 = (f32[16,256]{1,0:T(8,128)S(1)}, f32[16,256]{1,0:T(8,128)S(1)}, u32[]{:S(2)}, u32[]{:S(2)}) collective-permute-start(f32[16,256]{1,0:T(8,128)S(1)} %gather_rows.6), channel_id=1, source_target_pairs={{0,32},{16,48},{32,0},{48,16},{64,96},{80,112},{96,64},{112,80},{1... | collective-permute-start | bytes 49160 | tf_op jit(solution)/shard_map/gather_rows/ppermute | solution.py:344
  89.0 4.4 %collective-permute-start.33 = (bf16[128,256]{1,0:T(8,128)(2,1)S(1)}, bf16[128,256]{1,0:T(8,128)(2,1)S(1)}, u32[]{:S(2)}, u32[]{:S(2)}) collective-permute-start(bf16[128,256]{1,0:T(8,128)(2,1)S(1)} %slice.113), channel_id=1, source_target_pairs={{0,32},{32,64},{64,96},{96,128},{128,160},{160,192},{192,224},{224... | collective-permute-start | bytes 196616 | tf_op jit(solution)/shard_map/gather_rows/ppermute | solution.py:340
  89.1 4.3 %collective-permute-start.34 = (bf16[128,256]{1,0:T(8,128)(2,1)S(1)}, bf16[128,256]{1,0:T(8,128)(2,1)S(1)}, u32[]{:S(2)}, u32[]{:S(2)}) collective-permute-start(bf16[128,256]{1,0:T(8,128)(2,1)S(1)} %slice.114), channel_id=1, source_target_pairs={{0,224},{32,0},{64,32},{96,64},{128,96},{160,128},{192,160},{224,1... | collective-permute-start | bytes 196616 | tf_op jit(solution)/shard_map/gather_rows/ppermute | solution.py:340
  91.8 3.7 %collective-permute-start.36 = (f32[16,256]{1,0:T(8,128)S(1)}, f32[16,256]{1,0:T(8,128)S(1)}, u32[]{:S(2)}, u32[]{:S(2)}) collective-permute-start(f32[16,256]{1,0:T(8,128)S(1)} %add.123), channel_id=1, source_target_pairs={{0,64},{16,80},{32,96},{48,112},{64,0},{80,16},{96,32},{112,48},{1... | collective-permute-start | bytes 49160 | tf_op jit(solution)/shard_map/gather_rows/ppermute | solution.py:344
  95.5 15.7 %collective-permute-start.37 = (bf16[16,128,256]{2,1,0:T(8,128)(2,1)S(1)}, bf16[16,128,256]{2,1,0:T(8,128)(2,1)S(1)}, u32[]{:S(2)}, u32[]{:S(2)}) collective-permute-start(bf16[16,128,256]{2,1,0:T(8,128)(2,1)S(1)} %bitcast.44), channel_id=1, source_target_pairs={{0,16},{16,0},{32,48},{48,32},{64,80},{80,64},{96,112},{112,96},{1... | collective-permute-start | bytes 3145736 | tf_op jit(solution)/shard_map/gather_rows/ppermute | solution.py:344
  105.8 2.5 %collective-permute-start.38 = (f32[16,256]{1,0:T(8,128)S(1)}, f32[16,256]{1,0:T(8,128)S(1)}, u32[]{:S(2)}, u32[]{:S(2)}) collective-permute-start(f32[16,256]{1,0:T(8,128)S(1)} %add.124), channel_id=1, source_target_pairs={{0,16},{16,0},{32,48},{48,32},{64,80},{80,64},{96,112},{112,96},{1... | collective-permute-start | bytes 49160 | tf_op jit(solution)/shard_map/gather_rows/ppermute | solution.py:344
  109.0 6.6 %collective-permute-start.39 = (f32[16,256]{1,0:T(8,128)S(1)}, f32[16,256]{1,0:T(8,128)S(1)}, u32[]{:S(2)}, u32[]{:S(2)}) collective-permute-start(f32[16,256]{1,0:T(8,128)S(1)} %add_add_fusion), channel_id=1, source_target_pairs={{0,128},{16,144},{32,160},{48,176},{64,192},{80,208},{96,224},{112... | collective-permute-start | bytes 49160 | tf_op jit(solution)/shard_map/gather_rows/ppermute | solution.py:344

commit v4 on v3

--- a/solution.py
+++ b/solution.py
@@ -13,6 +13,7 @@
 QUADS_A_STEP = 8
 PARTS = 8
 TABLE = 384
+LINES = 32
 PLANE = ("yh", "x", "yl")
 BF16 = jnp.bfloat16
 F32 = jnp.float32
@@ -23,6 +24,11 @@
 SMEM = pl.BlockSpec(memory_space=pltpu.SMEM)
 
 
+def own_steps(depth):
+    middle = depth // 2
+    return [(2 * depth, 2)] + [(2 * depth + 2 + 4 * i, 4) for i in range(middle - 1)] + [(4 * depth - 2, 2)]
+
+
 def slot_tables_kernel(sizes, coords_ref, count_ref, place_ref, table_ref):
     depth, nx, ny = sizes
     slots = coords_ref.shape[1]
@@ -30,7 +36,10 @@
     row = coords_ref[0:1, :]
     col = coords_ref[1:2, :]
     away = jnp.bitwise_and((row >> 2) - at_z, depth - 1)
-    line_row = jnp.where(jnp.bitwise_and(row >> 1, 1) == at_c, 2 * depth, 0) + away * 2 + jnp.bitwise_and(row, 1)
+    middle = depth // 2
+    spot = jnp.where(away <= middle, 2 * (middle - away) - 1, 2 * (away - middle))
+    spot = jnp.where(away == middle, 0, jnp.where(away == 0, depth - 1, spot))
+    line_row = jnp.where(jnp.bitwise_and(row >> 1, 1) == at_c, 2 * depth, 0) + spot * 2 + jnp.bitwise_and(row, 1)
     rank = col >> 1
     col_x = jnp.bitwise_and(rank >> 1, nx - 1)
     col_y = rank // (2 * nx) * 2 + jnp.bitwise_and(rank, 1)
@@ -65,13 +74,16 @@
         def placed(value):
             return jnp.sum(jnp.where(here, jnp.broadcast_to(value, (slots, TABLE)), 0.0), axis=0, keepdims=True)
 
-        rows.append(placed(iota(1, 0).astype(F32) + 1.0))
-        rows.append(placed(columns[:, 1 - by : 2 - by]))
-        rows.append(placed(columns[:, by : by + 1]))
-        whole = jnp.sum(quads, axis=1, keepdims=True)
-        first = jnp.sum(jnp.where(spot[:1] < 2 * depth, quads, 0.0), axis=1, keepdims=True)
+        spare = (1.0 - placed(jnp.ones((slots, 1), F32))) * LINES
+        rows.append(placed(iota(1, 0).astype(F32)))
+        rows.append(placed(columns[:, 1 - by : 2 - by]) + spare)
+        rows.append(placed(columns[:, by : by + 1]) + spare)
         which = lax.broadcasted_iota(jnp.int32, (1, TABLE), 1)
-        rows.append(jnp.where(which == 0, jnp.broadcast_to(whole, (1, TABLE)), jnp.broadcast_to(first, (1, TABLE))))
+        marks = jnp.zeros((1, TABLE), F32)
+        for i, line in enumerate([LINES] + [begin for begin, _ in own_steps(depth)]):
+            ahead = jnp.sum(jnp.where(spot[:1] < line, quads, 0.0), axis=1, keepdims=True)
+            marks = jnp.where(which == i, jnp.broadcast_to(ahead, (1, TABLE)), marks)
+        rows.append(marks)
     table_ref[...] = jnp.concatenate(rows, axis=0).astype(jnp.int32)
 
 
@@ -87,23 +99,16 @@
 
 def add_quads(table_ref, base, begin, end, first_line, blocks_ref, source_ref, total_ref, contract):
     def quad(at):
-        inside = at < end
-        parts = []
-        for u in range(QUAD):
-            tag = table_ref[base, at * QUAD + u]
-            block = blocks_ref[jnp.maximum(tag - 1, 0)]
-            valid = jnp.logical_and(inside, tag > 0)
-            parts.append(
-                (jnp.where(valid, block, jnp.zeros_like(block)), source_ref[table_ref[base + 1, at * QUAD + u]])
-            )
+        entries = [at * QUAD + u for u in range(QUAD)]
+        lefts = [blocks_ref[table_ref[base, e]] for e in entries]
+        rights = [source_ref[table_ref[base + 1, e]] for e in entries]
         product = None
         for u in range(0, QUAD, 2):
-            left = jnp.concatenate([parts[u][0], parts[u + 1][0]], axis=contract)
-            right = jnp.concatenate([parts[u][1], parts[u + 1][1]], axis=0)
+            left = jnp.concatenate(lefts[u : u + 2], axis=contract)
+            right = jnp.concatenate(rights[u : u + 2], axis=0)
             term = lax.dot_general(left, right, (((contract,), (0,)), ((), ())), preferred_element_type=F32)
             product = term if product is None else product + term
-        line = jnp.where(inside, table_ref[base + 2, at * QUAD] - first_line, 0)
-        return line, product
+        return table_ref[base + 2, entries[0]] - first_line, product
 
     @pl.loop(0, (end - begin + QUADS_A_STEP - 1) // QUADS_A_STEP)
     def _(i):
@@ -112,7 +117,7 @@
             total_ref[line] += product
 
 
-def forward_kernel(own_half, sizes, table_ref, blocks_ref, *refs):
+def sibling_rows_kernel(sizes, table_ref, blocks_ref, *refs):
     depth, nx, ny = sizes
     *piece_refs, out_ref, source_ref, total_ref = refs
     lanes = piece_refs[0].shape[-1]
@@ -124,35 +129,58 @@
                     source_ref[(oy * nx + ox) * 2 + h, :, half * lanes : (half + 1) * lanes] = piece[
                         pl.ds((minor * 2 + h) * BLK, BLK), :
                     ]
-    total_ref[...] = jnp.zeros_like(total_ref)
-    whole, first = table_ref[3, 0], table_ref[3, 1]
-    begin, end, line = (first, whole, 2 * depth) if own_half else (0, first, 0)
-    add_quads(table_ref, 0, begin, end, line, blocks_ref, source_ref, total_ref, 1)
-    out_ref[...] = total_ref[...].astype(BF16)
-
-
-def forward_product(own_half, table, blocks, pieces, sizes):
-    depth, nx, ny = sizes
+    source_ref[LINES] = jnp.zeros_like(source_ref[LINES])
+    count = out_ref.shape[0]
+    total_ref[0:count] = jnp.zeros(out_ref.shape, F32)
+    add_quads(table_ref, 0, 0, table_ref[3, 1], 0, blocks_ref, source_ref, total_ref, 1)
+    out_ref[...] = total_ref[0:count].astype(BF16)
+
+
+def sibling_rows(table, blocks, pieces, sizes):
     width = 2 * pieces[0].shape[-1]
-    lines = 2 * depth
-    return pl.pallas_call(
-        functools.partial(forward_kernel, own_half, sizes),
-        out_shape=jax.ShapeDtypeStruct((lines, BLK, width), BF16),
+    return pl.pallas_call(
+        functools.partial(sibling_rows_kernel, sizes),
+        out_shape=(
+            jax.ShapeDtypeStruct((2 * sizes[0], BLK, width), BF16),
+            jax.ShapeDtypeStruct((LINES + 1, BLK, width), BF16),
+        ),
         in_specs=[SMEM] + [VMEM] * (1 + len(pieces)),
-        out_specs=VMEM,
-        scratch_shapes=[
-            pltpu.VMEM((nx * ny * 2, BLK, width), BF16),
-            pltpu.VMEM((lines, BLK, width), F32),
-        ],
+        out_specs=(VMEM, VMEM),
+        scratch_shapes=[pltpu.VMEM((LINES + 1, BLK, width), F32)],
         compiler_params=pltpu.CompilerParams(vmem_limit_bytes=VMEM_LIMIT),
     )(table, blocks, *pieces)
+
+
+def own_rows_kernel(step, depth, table_ref, blocks_ref, source_ref, out_ref, total_ref):
+    steps = own_steps(depth)
+    first, count = steps[step]
+    total_ref[0:count] = jnp.zeros(out_ref.shape, F32)
+    begin = table_ref[3, 1 + step]
+    end = table_ref[3, 2 + step] if step + 1 < len(steps) else table_ref[3, 0]
+    add_quads(table_ref, 0, begin, end, first, blocks_ref, source_ref, total_ref, 1)
+    out_ref[...] = total_ref[0:count].astype(BF16)
+
+
+def own_rows(step, table, blocks, source, depth):
+    first, count = own_steps(depth)[step]
+    width = source.shape[2]
+    return pl.pallas_call(
+        functools.partial(own_rows_kernel, step, depth),
+        out_shape=jax.ShapeDtypeStruct((count, BLK, width), BF16),
+        in_specs=[SMEM, VMEM, VMEM],
+        out_specs=VMEM,
+        scratch_shapes=[pltpu.VMEM((LINES + 1 - first, BLK, width), F32)],
+        cost_estimate=BESIDE,
+        compiler_params=pltpu.CompilerParams(vmem_limit_bytes=VMEM_LIMIT),
+    )(table, blocks, source)
 
 
 def backward_kernel(sizes, table_ref, place_ref, blocks_ref, sibling_ref, own_ref, out_ref, source_ref, total_ref):
     depth, nx, ny = sizes
     source_ref[0 : 2 * depth] = sibling_ref[...]
-    source_ref[2 * depth :] = own_ref[...]
-    total_ref[...] = jnp.zeros_like(total_ref)
+    source_ref[2 * depth : LINES] = own_ref[...]
+    source_ref[LINES] = jnp.zeros_like(source_ref[LINES])
+    total_ref[0:LINES] = jnp.zeros((LINES, *total_ref.shape[1:]), F32)
     add_quads(table_ref, 4, 0, table_ref[7, 0], 0, blocks_ref, source_ref, total_ref, 0)
     at_x, at_y = place_ref[2], place_ref[3]
     for oy in range(ny):
@@ -172,8 +200,8 @@
         in_specs=[SMEM] * 2 + [VMEM] * 3,
         out_specs=VMEM,
         scratch_shapes=[
-            pltpu.VMEM((2 * lines, BLK, width), BF16),
-            pltpu.VMEM((nx * ny * 2, BLK, width), F32),
+            pltpu.VMEM((LINES + 1, BLK, width), BF16),
+            pltpu.VMEM((LINES + 1, BLK, width), F32),
         ],
         cost_estimate=BESIDE,
         compiler_params=pltpu.CompilerParams(vmem_limit_bytes=VMEM_LIMIT),
@@ -215,6 +243,27 @@
         scratch_shapes=[pltpu.SemaphoreType.DMA((PARTS,))],
         compiler_params=pltpu.CompilerParams(vmem_limit_bytes=VMEM_LIMIT),
     )(count, pltpu.with_memory_space_constraint(blocks, pltpu.MemorySpace.HBM))
+
+
+def panel_kernel(*refs):
+    *chunk_refs, panel_ref = refs
+    at = 0
+    for ref in chunk_refs:
+        for begin in range(0, ref.shape[0], BLK):
+            panel_ref[at] = ref[begin : begin + BLK, :]
+            at += 1
+
+
+def own_rows_panel(chunks):
+    width = chunks[0].shape[1]
+    lines = sum(chunk.shape[0] for chunk in chunks) // BLK
+    return pl.pallas_call(
+        panel_kernel,
+        out_shape=jax.ShapeDtypeStruct((lines, BLK, width), BF16),
+        in_specs=[VMEM] * len(chunks),
+        out_specs=VMEM,
+        compiler_params=pltpu.CompilerParams(vmem_limit_bytes=SMALL_LIMIT),
+    )(*chunks)
 
 
 def dense_kernel(mixed_ref, weight_ref, cotangent_ref, hidden_ref, act_ref, grad_ref):
@@ -345,15 +394,19 @@
 
     with jax.named_scope("gather_features"):
         upright, level = node_features[:, :lanes], node_features[:, lanes:]
-        got = together(
-            tuple(send(upright, -o, 0) for o in range(1, nx)) + tuple(send(level, 0, -o) for o in range(1, ny))
-        )
-        upright = jnp.concatenate((upright,) + got[: nx - 1], axis=0)
-        level = jnp.concatenate((level,) + got[nx - 1 :], axis=0)
-        got = together(
-            tuple(send(upright, 0, -o) for o in range(1, ny)) + tuple(send(level, -o, 0) for o in range(1, nx))
-        )
-        pieces = (upright,) + got[: ny - 1] + (level,) + got[ny - 1 :]
+        shifts = [1, nx - 1] + list(range(2, nx - 1))
+
+        def halves(across, along):
+            got = [(send(across, -o, 0), send(along, 0, -o)) for o in shifts]
+            got = together(tuple(value for pair in got for value in pair))
+            first, second = dict(zip(shifts, got[0::2])), dict(zip(shifts, got[1::2]))
+            return [first[o] for o in range(1, nx)], [second[o] for o in range(1, ny)]
+
+        at_side, at_line = halves(upright, level)
+        upright = jnp.concatenate([upright] + at_side, axis=0)
+        level = jnp.concatenate([level] + at_line, axis=0)
+        at_side, at_line = halves(level, upright)
+        pieces = (upright, *at_line, level, *at_side)
 
     with jax.named_scope("tables"):
         table = slot_tables(block_coords[0, 0], count, place, sizes)
@@ -361,29 +414,33 @@
         blocks, _ = hold_blocks(adjacency_blocks[0, 0], early)
 
     with jax.named_scope("forward"):
-        for_sibling = forward_product(False, table, blocks, pieces, sizes)
+        for_sibling, source = sibling_rows(table, blocks, pieces, sizes)
         sibling = swap(for_sibling)
-        own = forward_product(True, table, blocks, pieces, sizes)
+        own = own_rows(0, table, blocks, source, depth)
         sibling, own = together((sibling, own))
-        own = own.reshape(depth, local, width)
         sibling = sibling.reshape(depth, local, width)
 
-    def term(step):
-        return own[step].astype(F32) + sibling[step].astype(F32)
+    def term(mine, spot):
+        return mine.astype(F32) + sibling[spot].astype(F32)
 
     with jax.named_scope("sum_rows"):
         half = local // 2
         middle = depth // 2
-        far = term(middle).astype(BF16)
-        up, down = together((climb(far[:half], 1), climb(far[half:], -1)))
-        up = jnp.concatenate([up, jnp.zeros_like(up)], axis=0)
-        down = jnp.concatenate([jnp.zeros_like(down), down], axis=0)
-        for step in range(middle - 1, 0, -1):
-            up, down = together(
-                ((term(step) + up.astype(F32)).astype(BF16), (term(depth - step) + down.astype(F32)).astype(BF16))
-            )
+        far = term(own.reshape(local, width), 0).astype(BF16)
+        up, down = far[:half], far[half:]
+        for step in range(1, middle + 1):
+            pace, up, down = together((table, up, down))
+            own = own_rows(step, pace, blocks, source, depth)
             up, down = together((climb(up, 1), climb(down, -1)))
-        mixed = (term(0) + (up.astype(F32) + down.astype(F32))).astype(BF16)
+            if step == 1:
+                up = jnp.concatenate([up, jnp.zeros_like(up)], axis=0)
+                down = jnp.concatenate([jnp.zeros_like(down), down], axis=0)
+            mine = own.reshape(-1, local, width)
+            if step < middle:
+                up = (term(mine[0], 2 * step - 1) + up.astype(F32)).astype(BF16)
+                down = (term(mine[1], 2 * step) + down.astype(F32)).astype(BF16)
+            else:
+                mixed = (term(mine[0], depth - 1) + (up.astype(F32) + down.astype(F32))).astype(BF16)
 
     with jax.named_scope("dense"):
         hidden, act_grad, mixed_grad = dense(mixed, weight, cotangent)
@@ -412,18 +469,16 @@
                 first = terms[0] + terms[1]
                 terms = [first, swap(first, 2, False)]
             ahead, behind, terms[0] = together(moved + (terms[0],))
+            if step > 2:
+                ahead, behind, *terms = together((ahead, behind, *terms))
             if step < middle:
                 chunks[depth - step] = ahead
                 chunks[step] = behind
-        chunks[middle] = jnp.concatenate([ahead, behind], axis=0)
-        own_panel = jnp.concatenate([chunks[step] for step in range(depth)], axis=0)
-        own_panel = own_panel.reshape(2 * depth, BLK, width)
+        order = [d for i in range(1, middle) for d in (middle - i, middle + i)] + [0]
+        own_panel = own_rows_panel([ahead, behind] + [chunks[d] for d in order])
         own_panel, part = together((own_panel, terms[0] + terms[1]))
         sibling_panel = swap(own_panel)
-        late, _ = together((count, own_panel))
         part = part + swap(part)
-        blocks, mark = hold_blocks(adjacency_blocks[0, 0], late)
-        part = part + mark[:1, :1]
         got = swap(part, 4, False)
 
     with jax.named_scope("backward"):

time: 152 us -> 156 us (1.026); the launches traced: 152 us -> 154 us
  Pallas kernels: 19 us -> 22.7 us
  waiting for transfers between devices: 25.8 us -> 29.1 us
  blocking collectives: 35.1 us -> 32.3 us
    ppermute x18, waiting for transfers between devices: 7.5 us -> 14.5 us  [send(): return lax.ppermute(value, PLANE, pairs)]
    ppermute x16, waiting for transfers between devices: 16.1 us -> 9.36 us  [climb(): lax.ppermute(value, 'z', [(i, (i + dz) % depth) for i in range(depth)])]
    pallas_call x2 -> x7, Pallas kernels: 5.19 us -> 9.89 us  [the longest x5 6.56 us: own_rows(): pl.pallas_call(functools.partial(own_rows_kernel, step, depth), out_shape...]
    ppermute x6, waiting for transfers between devices: 2.2 us -> 5.24 us  [swap(): return lax.ppermute(value, ('z', 'c'), pairs)]
    all_to_all x1, blocking collectives: 35.1 us -> 32.3 us  [body(): arrived = lax.all_to_all(outs, PLANE, 0, 0, tiled=True)]
    ppermute x16, starting transfers between devices: 24.8 us -> 22.9 us  [climb(): lax.ppermute(value, 'z', [(i, (i + dz) % depth) for i in range(depth)])]
    ppermute x6, starting transfers between devices: 17.2 us -> 18.8 us  [swap(): return lax.ppermute(value, ('z', 'c'), pairs)]
    pallas_call x2 -> x1, Pallas kernels: 4.45 us -> 3.16 us  [hold_blocks(): pl.pallas_call(hold_kernel, out_shape=(pltpu.VMEM(blocks.shape, blocks.dt...]
  transfers between devices with their start and end apart: 40 -> 40, of which waited for: 17 -> 21; matrix products, arithmetic and copies ran while one was open for 1% -> 0% of each run, Pallas kernels for 9% -> 11%
where the time goes in v4:
time: 156 us; the launch traced here: 154 us
  starting transfers between devices  66.2 us (42%)
  blocking collectives  32.3 us (21%)
  waiting for transfers between devices  29.1 us (19%)
  Pallas kernels  22.7 us (15%)
  local copies, waits for them, and re-layouts  1.61 us (1%)
  between operations  1.58 us (1%)
    all_to_all x1, blocking collectives, body(): arrived = lax.all_to_all(outs, PLANE, 0, 0, tiled=True)  32.3 us
    ppermute x18, starting transfers between devices, send(): return lax.ppermute(value, PLANE, pairs)  24.5 us
    ppermute x16, starting transfers between devices, climb(): lax.ppermute(value, 'z', [(i, (i + dz) % depth) for i in range(depth)])  22.9 us
    ppermute x6, starting transfers between devices, swap(): return lax.ppermute(value, ('z', 'c'), pairs)  18.8 us
    ppermute x18, waiting for transfers between devices, send(): return lax.ppermute(value, PLANE, pairs)  14.5 us
    ppermute x16, waiting for transfers between devices, climb(): lax.ppermute(value, 'z', [(i, (i + dz) % depth) for i in range(depth)])  9.36 us
    pallas_call x5, Pallas kernels, own_rows(): pl.pallas_call(functools.partial(own_rows_kernel, step, depth), out_shape...  6.56 us
    ppermute x6, waiting for transfers between devices, swap(): return lax.ppermute(value, ('z', 'c'), pairs)  5.24 us
  transfers between devices with their start and end apart: 40, of which 21 were waited for; matrix products, arithmetic and copies ran while one was open for 0% of the time, Pallas kernels for 11%

profile of v4, /device:TPU:1, one launch (start us, length us, event | category | flops | bytes accessed | tf_op | source)
XLA Modules:
  0.0 154.1 jit_solution(3258140296736008972)
XLA Ops:
  0.6 0.9 fusion.7
  1.5 3.8 %collective-permute-start.5 = (bf16[256,128]{1,0:T(8,128)(2,1)S(1)}, bf16[256,128]{1,0:T(8,128)(2,1)S(1)}, u32[]{:S(2)}, u32[]{:S(2)}) collective-permute-start(bf16[256,128]{1,0:T(8,128)(2,1)S(1)} %get-tuple-element.185), channel_id=1, source_target_pairs={{0,8},{1,9},{8,0},{9,1},{2,10},{3,11},{10,2},{11,3},{4,12},{5,13},... | collective-permute-start | bytes 196616 | tf_op jit(solution)/shard_map/gather_features/ppermute | solution.py:386
  5.3 0.4 collective-permute-start.3
  5.7 2.3 %collective-permute-start.1 = (bf16[256,128]{1,0:T(8,128)(2,1)S(1)}, bf16[256,128]{1,0:T(8,128)(2,1)S(1)}, u32[]{:S(2)}, u32[]{:S(2)}) collective-permute-start(bf16[256,128]{1,0:T(8,128)(2,1)S(1)} %get-tuple-element.185), channel_id=1, source_target_pairs={{0,9},{1,0},{8,1},{9,8},{2,11},{3,2},{10,3},{11,10},{4,13},{5,4},{... | collective-permute-start | bytes 196616 | tf_op jit(solution)/shard_map/gather_features/ppermute | solution.py:386
  8.0 2.7 %collective-permute-start.4 = (bf16[256,128]{1,0:T(8,128)(2,1)S(1)}, bf16[256,128]{1,0:T(8,128)(2,1)S(1)}, u32[]{:S(2)}, u32[]{:S(2)}) collective-permute-start(bf16[256,128]{1,0:T(8,128)(2,1)S(1)} %get-tuple-element.186), channel_id=1, source_target_pairs={{0,4},{1,5},{8,12},{9,13},{2,6},{3,7},{10,14},{11,15},{4,0},{5,1},... | collective-permute-start | bytes 196616 | tf_op jit(solution)/shard_map/gather_features/ppermute | solution.py:386
  11.1 2.4 %collective-permute-start = (bf16[256,128]{1,0:T(8,128)(2,1)S(1)}, bf16[256,128]{1,0:T(8,128)(2,1)S(1)}, u32[]{:S(2)}, u32[]{:S(2)}) collective-permute-start(bf16[256,128]{1,0:T(8,128)(2,1)S(1)} %get-tuple-element.186), channel_id=1, source_target_pairs={{0,6},{1,7},{8,14},{9,15},{2,0},{3,1},{10,8},{11,9},{4,2},{5,3},{1... | collective-permute-start | bytes 196616 | tf_op jit(solution)/shard_map/gather_features/ppermute | solution.py:386
  13.5 2.1 %collective-permute-done.2 = bf16[256,128]{1,0:T(8,128)(2,1)S(1)} collective-permute-done((bf16[256,128]{1,0:T(8,128)(2,1)S(1)}, bf16[256,128]{1,0:T(8,128)(2,1)S(1)}, u32[]{:S(2)}, u32[]{:S(2)}) %collective-permute-start.2) | collective-permute-done | bytes 65568 | tf_op jit(solution)/shard_map/gather_features/ppermute | solution.py:386
  15.6 1.7 %collective-permute-start.10 = (bf16[1024,128]{1,0:T(8,128)(2,1)S(1)}, bf16[1024,128]{1,0:T(8,128)(2,1)S(1)}, u32[]{:S(2)}, u32[]{:S(2)}) collective-permute-start(bf16[1024,128]{1,0:T(8,128)(2,1)S(1)} %pad_maximum_fusion.1.refs_4_), channel_id=1, source_target_pairs={{0,4},{1,5},{8,12},{9,13},{2,6},{3,7},{10,14},{11,15},{4,0},{5,1},... | collective-permute-start | bytes 786440 | tf_op jit(solution)/shard_map/gather_features/ppermute | solution.py:386
  17.2 1.4 collective-permute-start.8
  18.7 1.2 collective-permute-start.6
  20.0 0.6 collective-permute-start.9
  20.6 1.9 %collective-permute-done.10.refs_6_ = bf16[1024,128]{1,0:T(8,128)(2,1)S(1)} collective-permute-done((bf16[1024,128]{1,0:T(8,128)(2,1)S(1)}, bf16[1024,128]{1,0:T(8,128)(2,1)S(1)}, u32[]{:S(2)}, u32[]{:S(2)}) %collective-permute-start.10) | collective-permute-done | bytes 262176 | tf_op jit(solution)/shard_map/gather_features/ppermute | solution.py:386
  23.5 0.7 copy-done.2
  24.2 1.4 tables.2.table_ref
  25.6 3.2 %tables.3 = (bf16[256,128,128]{2,1,0:T(8,128)(2,1)S(1)}, f32[8,128]{1,0:T(8,128)}) custom-call(s32[1]{0:T(128)} %bitcast.39.count_ref, bf16[256,128,128]{2,1,0:T(8,128)(2,1)} %bitcast.42), custom_call_target="tpu_custom_call" | custom-call | tf_op jit(solution)/shard_map/tables/pallas_call | solution.py:238
  28.7 1.6 %collective-permute-done.8.refs_7_ = bf16[1024,128]{1,0:T(8,128)(2,1)S(1)} collective-permute-done((bf16[1024,128]{1,0:T(8,128)(2,1)S(1)}, bf16[1024,128]{1,0:T(8,128)(2,1)S(1)}, u32[]{:S(2)}, u32[]{:S(2)}) %collective-permute-start.8) | collective-permute-done | bytes 262176 | tf_op jit(solution)/shard_map/gather_features/ppermute | solution.py:386
  30.3 4.3 %collective-permute-done.9.refs_3_ = bf16[1024,128]{1,0:T(8,128)(2,1)S(1)} collective-permute-done((bf16[1024,128]{1,0:T(8,128)(2,1)S(1)}, bf16[1024,128]{1,0:T(8,128)(2,1)S(1)}, u32[]{:S(2)}, u32[]{:S(2)}) %collective-permute-start.9) | collective-permute-done | bytes 262176 | tf_op jit(solution)/shard_map/gather_features/ppermute | solution.py:386
  34.6 3.3 %forward.2 = (bf16[16,128,256]{2,1,0:T(8,128)(2,1)S(1)}, bf16[33,128,256]{2,1,0:T(8,128)(2,1)S(1)}) custom-call(s32[8,384]{1,0:T(8,128)S(1)} %tables.2.table_ref, bf16[256,128,128]{2,1,0:T(8,128)(2,1)S(1)} %get-tuple-element.92.blocks_ref, bf16[1024,128]{1,0:T(8,128)(2,1)S(1)} %pad_maximum_fusion.refs_0_, ...), custom_call_target="tpu_custom_call" | custom-call | tf_op jit(solution)/shard_map/forward/pallas_call | solution.py:141
  37.9 0.7 collective-permute-start.12
  38.5 1.4 forward.3
  40.0 0.8 collective-permute-done.12
  40.9 1.0 collective-permute-start.13
  41.9 4.5 %collective-permute-start.14 = (bf16[128,256]{1,0:T(8,128)(2,1)S(1)}, bf16[128,256]{1,0:T(8,128)(2,1)S(1)}, u32[]{:S(2)}, u32[]{:S(2)}) collective-permute-start(bf16[128,256]{1,0:T(8,128)(2,1)S(1)} %get-tuple-element.111), channel_id=1, source_target_pairs={{0,224},{32,0},{64,32},{96,64},{128,96},{160,128},{192,160},{224,1... | collective-permute-start | bytes 196616 | tf_op jit(solution)/shard_map/sum_rows/ppermute | solution.py:389
  46.4 1.3 sum_rows.4
  47.8 0.9 collective-permute-done.13
  48.8 2.7 %collective-permute-start.16 = (bf16[256,256]{1,0:T(8,128)(2,1)S(1)}, bf16[256,256]{1,0:T(8,128)(2,1)S(1)}, u32[]{:S(2)}, u32[]{:S(2)}) collective-permute-start(bf16[256,256]{1,0:T(8,128)(2,1)S(1)} %get-tuple-element.116), channel_id=1, source_target_pairs={{0,224},{32,0},{64,32},{96,64},{128,96},{160,128},{192,160},{224,1... | collective-permute-start | bytes 393224 | tf_op jit(solution)/shard_map/sum_rows/ppermute | solution.py:389
  51.4 1.3 sum_rows.5
  52.8 1.5 collective-permute-done.15
  54.4 1.6 %collective-permute-start.17 = (bf16[256,256]{1,0:T(8,128)(2,1)S(1)}, bf16[256,256]{1,0:T(8,128)(2,1)S(1)}, u32[]{:S(2)}, u32[]{:S(2)}) collective-permute-start(bf16[256,256]{1,0:T(8,128)(2,1)S(1)} %fusion.4), channel_id=1, source_target_pairs={{0,32},{32,64},{64,96},{96,128},{128,160},{160,192},{192,224},{224... | collective-permute-start | bytes 393224 | tf_op jit(solution)/shard_map/sum_rows/ppermute | solution.py:389
  55.9 1.2 collective-permute-start.18
  57.1 1.3 sum_rows.6
  58.5 1.0 collective-permute-done.17
  59.8 1.3 sum_rows.7
  61.1 1.7 %collective-permute-start.19 = (bf16[256,256]{1,0:T(8,128)(2,1)S(1)}, bf16[256,256]{1,0:T(8,128)(2,1)S(1)}, u32[]{:S(2)}, u32[]{:S(2)}) collective-permute-start(bf16[256,256]{1,0:T(8,128)(2,1)S(1)} %fusion.2), channel_id=1, source_target_pairs={{0,32},{32,64},{64,96},{96,128},{128,160},{160,192},{192,224},{224... | collective-permute-start | bytes 393224 | tf_op jit(solution)/shard_map/sum_rows/ppermute | solution.py:389
  62.8 1.0 collective-permute-start.20
  63.9 2.3 %collective-permute-done.19 = bf16[256,256]{1,0:T(8,128)(2,1)S(1)} collective-permute-done((bf16[256,256]{1,0:T(8,128)(2,1)S(1)}, bf16[256,256]{1,0:T(8,128)(2,1)S(1)}, u32[]{:S(2)}, u32[]{:S(2)}) %collective-permute-start.19) | collective-permute-done | bytes 131104 | tf_op jit(solution)/shard_map/sum_rows/ppermute | solution.py:389
  66.2 0.4 collective-permute-done.20
  66.7 0.9 dense.1
  67.6 2.2 %collective-permute-start.22 = (bf16[256,256]{1,0:T(8,128)(2,1)S(1)}, bf16[256,256]{1,0:T(8,128)(2,1)S(1)}, u32[]{:S(2)}, u32[]{:S(2)}) collective-permute-start(bf16[256,256]{1,0:T(8,128)(2,1)S(1)} %get-tuple-element.130.refs_8_), channel_id=1, source_target_pairs={{0,224},{32,0},{64,32},{96,64},{128,96},{160,128},{192,160},{224,1... | collective-permute-start | bytes 393224 | tf_op jit(solution)/shard_map/gather_rows/ppermute | solution.py:389
  69.9 0.8 gather_rows.4
  70.8 4.3 %collective-permute-start.26 = (f32[64,256]{1,0:T(8,128)S(1)}, f32[64,256]{1,0:T(8,128)S(1)}, u32[]{:S(2)}, u32[]{:S(2)}) collective-permute-start(f32[64,256]{1,0:T(8,128)S(1)} %get-tuple-element.137), channel_id=1, source_target_pairs={{0,4},{1,5},{8,12},{9,13},{2,6},{3,7},{10,14},{11,15},{4,0},{5,1},... | collective-permute-start | bytes 196616 | tf_op jit(solution)/shard_map/gather_rows/ppermute | solution.py:386
  75.1 0.4 collective-permute-start.23
  75.6 1.9 %collective-permute-done.26.refs_2_ = f32[64,256]{1,0:T(8,128)S(1)} collective-permute-done((f32[64,256]{1,0:T(8,128)S(1)}, f32[64,256]{1,0:T(8,128)S(1)}, u32[]{:S(2)}, u32[]{:S(2)}) %collective-permute-start.26) | collective-permute-done | bytes 65568 | tf_op jit(solution)/shard_map/gather_rows/ppermute | solution.py:386
  77.4 1.1 collective-permute-done.27.refs_3_
  78.5 2.7 %collective-permute-start.24 = (bf16[256,256]{1,0:T(8,128)(2,1)S(1)}, bf16[256,256]{1,0:T(8,128)(2,1)S(1)}, u32[]{:S(2)}, u32[]{:S(2)}) collective-permute-start(bf16[256,256]{1,0:T(8,128)(2,1)S(1)} %collective-permute-done.22.refs_6_), channel_id=1, source_target_pairs={{0,224},{32,0},{64,32},{96,64},{128,96},{160,128},{192,160},{224,1... | collective-permute-start | bytes 393224 | tf_op jit(solution)/shard_map/gather_rows/ppermute | solution.py:389
  81.2 0.6 gather_rows.5
  81.7 0.4 collective-permute-start.30
  82.4 2.2 %collective-permute-start.32 = (f32[16,256]{1,0:T(8,128)S(1)}, f32[16,256]{1,0:T(8,128)S(1)}, u32[]{:S(2)}, u32[]{:S(2)}) collective-permute-start(f32[16,256]{1,0:T(8,128)S(1)} %get-tuple-element.149), channel_id=1, source_target_pairs={{0,9},{1,0},{8,1},{9,8},{2,11},{3,2},{10,3},{11,10},{4,13},{5,4},{... | collective-permute-start | bytes 49160 | tf_op jit(solution)/shard_map/gather_rows/ppermute | solution.py:386
  84.7 1.0 collective-permute-done.30.refs_1_
  85.6 0.6 collective-permute-done.31.refs_2_
  86.4 1.1 collective-permute-start.29
  87.4 0.5 gather_rows.6
  88.0 0.5 collective-permute-start.33
  88.5 2.8 %collective-permute-done.29.refs_2_ = bf16[256,256]{1,0:T(8,128)(2,1)S(1)} collective-permute-done((bf16[256,256]{1,0:T(8,128)(2,1)S(1)}, bf16[256,256]{1,0:T(8,128)(2,1)S(1)}, u32[]{:S(2)}, u32[]{:S(2)}) %collective-permute-start.29) | collective-permute-done | bytes 131104 | tf_op jit(solution)/shard_map/gather_rows/ppermute | solution.py:389
  91.3 0.3 collective-permute-done.33
  91.8 2.7 %collective-permute-start.35 = (bf16[128,256]{1,0:T(8,128)(2,1)S(1)}, bf16[128,256]{1,0:T(8,128)(2,1)S(1)}, u32[]{:S(2)}, u32[]{:S(2)}) collective-permute-start(bf16[128,256]{1,0:T(8,128)(2,1)S(1)} %slice.101), channel_id=1, source_target_pairs={{0,224},{32,0},{64,32},{96,64},{128,96},{160,128},{192,160},{224,1... | collective-permute-start | bytes 196616 | tf_op jit(solution)/shard_map/gather_rows/ppermute | solution.py:389
  94.4 1.5 collective-permute-start.36
  96.1 1.8 %collective-permute-done.36 = f32[16,256]{1,0:T(8,128)S(1)} collective-permute-done((f32[16,256]{1,0:T(8,128)S(1)}, f32[16,256]{1,0:T(8,128)S(1)}, u32[]{:S(2)}, u32[]{:S(2)}) %collective-permute-start.36) | collective-permute-done | bytes 16416 | tf_op jit(solution)/shard_map/gather_rows/ppermute | solution.py:393
  98.0 11.7 %collective-permute-start.37 = (bf16[16,128,256]{2,1,0:T(8,128)(2,1)S(1)}, bf16[16,128,256]{2,1,0:T(8,128)(2,1)S(1)}, u32[]{:S(2)}, u32[]{:S(2)}) collective-permute-start(bf16[16,128,256]{2,1,0:T(8,128)(2,1)S(1)} %gather_rows.7.own_ref), channel_id=1, source_target_pairs={{0,16},{16,0},{32,48},{48,32},{64,80},{80,64},{96,112},{112,96},{1... | collective-permute-start | bytes 3145736 | tf_op jit(solution)/shard_map/gather_rows/ppermute | solution.py:393
  109.8 2.2 %collective-permute-done.38 = f32[16,256]{1,0:T(8,128)S(1)} collective-permute-done((f32[16,256]{1,0:T(8,128)S(1)}, f32[16,256]{1,0:T(8,128)S(1)}, u32[]{:S(2)}, u32[]{:S(2)}) %collective-permute-start.38) | collective-permute-done | bytes 16416 | tf_op jit(solution)/shard_map/gather_rows/ppermute | solution.py:393
  112.0 4.2 %collective-permute-start.39 = (f32[16,256]{1,0:T(8,128)S(1)}, f32[16,256]{1,0:T(8,128)S(1)}, u32[]{:S(2)}, u32[]{:S(2)}) collective-permute-start(f32[16,256]{1,0:T(8,128)S(1)} %add.115), channel_id=1, source_target_pairs={{0,128},{16,144},{32,160},{48,176},{64,192},{80,208},{96,224},{112... | collective-permute-start | bytes 49160 | tf_op jit(solution)/shard_map/gather_rows/ppermute | solution.py:393
  116.3 4.4 %backward.1 = bf16[16,272,256]{2,1,0:T(8,128)(2,1)S(1)} custom-call(s32[8,384]{1,0:T(8,128)S(1)} %tables.2.table_ref, s32[4]{0:T(128)S(1)} %pad_add_fusion.place_ref, bf16[256,128,128]{2,1,0:T(8,128)(2,1)S(1)} %get-tuple-element.92.blocks_ref, bf16[16,128,256]{2,1,0:T(8,128)(2,1)S(1)} %collective-permute-done.37.sibling_ref, ...), custom_call_target="tpu_custom_call" | custom-call | flops 4000000000 | tf_op jit(solution)/shard_map/backward/pallas_call | solution.py:197
  120.8 32.3 %all_to_all.5.arrived_ref = bf16[16,272,256]{2,1,0:T(8,128)(2,1)S(1)} all-to-all(bf16[16,272,256]{2,1,0:T(8,128)(2,1)S(1)} %broadcast_dynamic-update-slice_fusion), channel_id=1, replica_groups=mesh['z'=8,'c'=2,'yh'=2,'x'=4,'yl'=2] {'yh','x','yl'}, dimensions={0} | all-to-all | bytes 4456448 | tf_op jit(solution)/shard_map/sum_columns/all_to_all | solution.py:492
  153.0 1.0 sum_columns.1
  (61 shorter events, 2.6 us)
Async XLA Ops:
  1.5 9.6 %collective-permute-start.5 = (bf16[256,128]{1,0:T(8,128)(2,1)S(1)}, bf16[256,128]{1,0:T(8,128)(2,1)S(1)}, u32[]{:S(2)}, u32[]{:S(2)}) collective-permute-start(bf16[256,128]{1,0:T(8,128)(2,1)S(1)} %get-tuple-element.185), channel_id=1, source_target_pairs={{0,8},{1,9},{8,0},{9,1},{2,10},{3,11},{10,2},{11,3},{4,12},{5,13},... | collective-permute-start | bytes 196616 | tf_op jit(solution)/shard_map/gather_features/ppermute | solution.py:386
  5.3 8.1 %collective-permute-start.3 = (bf16[256,128]{1,0:T(8,128)(2,1)S(1)}, bf16[256,128]{1,0:T(8,128)(2,1)S(1)}, u32[]{:S(2)}, u32[]{:S(2)}) collective-permute-start(bf16[256,128]{1,0:T(8,128)(2,1)S(1)} %get-tuple-element.185), channel_id=1, source_target_pairs={{0,1},{1,8},{8,9},{9,0},{2,3},{3,10},{10,11},{11,2},{4,5},{5,12},{... | collective-permute-start | bytes 196616 | tf_op jit(solution)/shard_map/gather_features/ppermute | solution.py:386
  5.7 7.7 %collective-permute-start.1 = (bf16[256,128]{1,0:T(8,128)(2,1)S(1)}, bf16[256,128]{1,0:T(8,128)(2,1)S(1)}, u32[]{:S(2)}, u32[]{:S(2)}) collective-permute-start(bf16[256,128]{1,0:T(8,128)(2,1)S(1)} %get-tuple-element.185), channel_id=1, source_target_pairs={{0,9},{1,0},{8,1},{9,8},{2,11},{3,2},{10,3},{11,10},{4,13},{5,4},{... | collective-permute-start | bytes 196616 | tf_op jit(solution)/shard_map/gather_features/ppermute | solution.py:386
  8.0 5.4 %collective-permute-start.4 = (bf16[256,128]{1,0:T(8,128)(2,1)S(1)}, bf16[256,128]{1,0:T(8,128)(2,1)S(1)}, u32[]{:S(2)}, u32[]{:S(2)}) collective-permute-start(bf16[256,128]{1,0:T(8,128)(2,1)S(1)} %get-tuple-element.186), channel_id=1, source_target_pairs={{0,4},{1,5},{8,12},{9,13},{2,6},{3,7},{10,14},{11,15},{4,0},{5,1},... | collective-permute-start | bytes 196616 | tf_op jit(solution)/shard_map/gather_features/ppermute | solution.py:386
  10.8 4.8 %collective-permute-start.2 = (bf16[256,128]{1,0:T(8,128)(2,1)S(1)}, bf16[256,128]{1,0:T(8,128)(2,1)S(1)}, u32[]{:S(2)}, u32[]{:S(2)}) collective-permute-start(bf16[256,128]{1,0:T(8,128)(2,1)S(1)} %get-tuple-element.186), channel_id=1, source_target_pairs={{0,2},{1,3},{8,10},{9,11},{2,4},{3,5},{10,12},{11,13},{4,6},{5,7},... | collective-permute-start | bytes 196616 | tf_op jit(solution)/shard_map/gather_features/ppermute | solution.py:386
  11.1 4.5 %collective-permute-start = (bf16[256,128]{1,0:T(8,128)(2,1)S(1)}, bf16[256,128]{1,0:T(8,128)(2,1)S(1)}, u32[]{:S(2)}, u32[]{:S(2)}) collective-permute-start(bf16[256,128]{1,0:T(8,128)(2,1)S(1)} %get-tuple-element.186), channel_id=1, source_target_pairs={{0,6},{1,7},{8,14},{9,15},{2,0},{3,1},{10,8},{11,9},{4,2},{5,3},{1... | collective-permute-start | bytes 196616 | tf_op jit(solution)/shard_map/gather_features/ppermute | solution.py:386
  15.6 6.9 %collective-permute-start.10 = (bf16[1024,128]{1,0:T(8,128)(2,1)S(1)}, bf16[1024,128]{1,0:T(8,128)(2,1)S(1)}, u32[]{:S(2)}, u32[]{:S(2)}) collective-permute-start(bf16[1024,128]{1,0:T(8,128)(2,1)S(1)} %pad_maximum_fusion.1.refs_4_), channel_id=1, source_target_pairs={{0,4},{1,5},{8,12},{9,13},{2,6},{3,7},{10,14},{11,15},{4,0},{5,1},... | collective-permute-start | bytes 786440 | tf_op jit(solution)/shard_map/gather_features/ppermute | solution.py:386
  17.2 13.1 %collective-permute-start.8 = (bf16[1024,128]{1,0:T(8,128)(2,1)S(1)}, bf16[1024,128]{1,0:T(8,128)(2,1)S(1)}, u32[]{:S(2)}, u32[]{:S(2)}) collective-permute-start(bf16[1024,128]{1,0:T(8,128)(2,1)S(1)} %pad_maximum_fusion.1.refs_4_), channel_id=1, source_target_pairs={{0,2},{1,3},{8,10},{9,11},{2,4},{3,5},{10,12},{11,13},{4,6},{5,7},... | collective-permute-start | bytes 786440 | tf_op jit(solution)/shard_map/gather_features/ppermute | solution.py:386
  18.7 11.6 %collective-permute-start.6 = (bf16[1024,128]{1,0:T(8,128)(2,1)S(1)}, bf16[1024,128]{1,0:T(8,128)(2,1)S(1)}, u32[]{:S(2)}, u32[]{:S(2)}) collective-permute-start(bf16[1024,128]{1,0:T(8,128)(2,1)S(1)} %pad_maximum_fusion.1.refs_4_), channel_id=1, source_target_pairs={{0,6},{1,7},{8,14},{9,15},{2,0},{3,1},{10,8},{11,9},{4,2},{5,3},{1... | collective-permute-start | bytes 786440 | tf_op jit(solution)/shard_map/gather_features/ppermute | solution.py:386
  19.9 10.4 %collective-permute-start.11 = (bf16[1024,128]{1,0:T(8,128)(2,1)S(1)}, bf16[1024,128]{1,0:T(8,128)(2,1)S(1)}, u32[]{:S(2)}, u32[]{:S(2)}) collective-permute-start(bf16[1024,128]{1,0:T(8,128)(2,1)S(1)} %pad_maximum_fusion.refs_0_), channel_id=1, source_target_pairs={{0,8},{1,9},{8,0},{9,1},{2,10},{3,11},{10,2},{11,3},{4,12},{5,13},... | collective-permute-start | bytes 786440 | tf_op jit(solution)/shard_map/gather_features/ppermute | solution.py:386
  20.0 14.5 %collective-permute-start.9 = (bf16[1024,128]{1,0:T(8,128)(2,1)S(1)}, bf16[1024,128]{1,0:T(8,128)(2,1)S(1)}, u32[]{:S(2)}, u32[]{:S(2)}) collective-permute-start(bf16[1024,128]{1,0:T(8,128)(2,1)S(1)} %pad_maximum_fusion.refs_0_), channel_id=1, source_target_pairs={{0,1},{1,8},{8,9},{9,0},{2,3},{3,10},{10,11},{11,2},{4,5},{5,12},{... | collective-permute-start | bytes 786440 | tf_op jit(solution)/shard_map/gather_features/ppermute | solution.py:386
  22.5 12.1 %collective-permute-start.7 = (bf16[1024,128]{1,0:T(8,128)(2,1)S(1)}, bf16[1024,128]{1,0:T(8,128)(2,1)S(1)}, u32[]{:S(2)}, u32[]{:S(2)}) collective-permute-start(bf16[1024,128]{1,0:T(8,128)(2,1)S(1)} %pad_maximum_fusion.refs_0_), channel_id=1, source_target_pairs={{0,9},{1,0},{8,1},{9,8},{2,11},{3,2},{10,3},{11,10},{4,13},{5,4},{... | collective-permute-start | bytes 786440 | tf_op jit(solution)/shard_map/gather_features/ppermute | solution.py:386
  23.5 0.7 copy-start.2
  37.9 3.0 %collective-permute-start.12 = (bf16[16,128,256]{2,1,0:T(8,128)(2,1)S(1)}, bf16[16,128,256]{2,1,0:T(8,128)(2,1)S(1)}, u32[]{:S(2)}, u32[]{:S(2)}) collective-permute-start(bf16[16,128,256]{2,1,0:T(8,128)(2,1)S(1)} %get-tuple-element.105), channel_id=1, source_target_pairs={{0,16},{16,0},{32,48},{48,32},{64,80},{80,64},{96,112},{112,96},{1... | collective-permute-start | bytes 3145736 | tf_op jit(solution)/shard_map/forward/ppermute | solution.py:393
  40.9 7.8 %collective-permute-start.13 = (bf16[128,256]{1,0:T(8,128)(2,1)S(1)}, bf16[128,256]{1,0:T(8,128)(2,1)S(1)}, u32[]{:S(2)}, u32[]{:S(2)}) collective-permute-start(bf16[128,256]{1,0:T(8,128)(2,1)S(1)} %get-tuple-element.110), channel_id=1, source_target_pairs={{0,32},{32,64},{64,96},{96,128},{128,160},{160,192},{192,224},{224... | collective-permute-start | bytes 196616 | tf_op jit(solution)/shard_map/sum_rows/ppermute | solution.py:389
  41.9 6.8 %collective-permute-start.14 = (bf16[128,256]{1,0:T(8,128)(2,1)S(1)}, bf16[128,256]{1,0:T(8,128)(2,1)S(1)}, u32[]{:S(2)}, u32[]{:S(2)}) collective-permute-start(bf16[128,256]{1,0:T(8,128)(2,1)S(1)} %get-tuple-element.111), channel_id=1, source_target_pairs={{0,224},{32,0},{64,32},{96,64},{128,96},{160,128},{192,160},{224,1... | collective-permute-start | bytes 196616 | tf_op jit(solution)/shard_map/sum_rows/ppermute | solution.py:389
  48.7 5.6 %collective-permute-start.15 = (bf16[256,256]{1,0:T(8,128)(2,1)S(1)}, bf16[256,256]{1,0:T(8,128)(2,1)S(1)}, u32[]{:S(2)}, u32[]{:S(2)}) collective-permute-start(bf16[256,256]{1,0:T(8,128)(2,1)S(1)} %get-tuple-element.115), channel_id=1, source_target_pairs={{0,32},{32,64},{64,96},{96,128},{128,160},{160,192},{192,224},{224... | collective-permute-start | bytes 393224 | tf_op jit(solution)/shard_map/sum_rows/ppermute | solution.py:389
  48.8 5.5 %collective-permute-start.16 = (bf16[256,256]{1,0:T(8,128)(2,1)S(1)}, bf16[256,256]{1,0:T(8,128)(2,1)S(1)}, u32[]{:S(2)}, u32[]{:S(2)}) collective-permute-start(bf16[256,256]{1,0:T(8,128)(2,1)S(1)} %get-tuple-element.116), channel_id=1, source_target_pairs={{0,224},{32,0},{64,32},{96,64},{128,96},{160,128},{192,160},{224,1... | collective-permute-start | bytes 393224 | tf_op jit(solution)/shard_map/sum_rows/ppermute | solution.py:389
  54.4 5.1 %collective-permute-start.17 = (bf16[256,256]{1,0:T(8,128)(2,1)S(1)}, bf16[256,256]{1,0:T(8,128)(2,1)S(1)}, u32[]{:S(2)}, u32[]{:S(2)}) collective-permute-start(bf16[256,256]{1,0:T(8,128)(2,1)S(1)} %fusion.4), channel_id=1, source_target_pairs={{0,32},{32,64},{64,96},{96,128},{128,160},{160,192},{192,224},{224... | collective-permute-start | bytes 393224 | tf_op jit(solution)/shard_map/sum_rows/ppermute | solution.py:389
  55.9 3.8 %collective-permute-start.18 = (bf16[256,256]{1,0:T(8,128)(2,1)S(1)}, bf16[256,256]{1,0:T(8,128)(2,1)S(1)}, u32[]{:S(2)}, u32[]{:S(2)}) collective-permute-start(bf16[256,256]{1,0:T(8,128)(2,1)S(1)} %fusion.3), channel_id=1, source_target_pairs={{0,224},{32,0},{64,32},{96,64},{128,96},{160,128},{192,160},{224,1... | collective-permute-start | bytes 393224 | tf_op jit(solution)/shard_map/sum_rows/ppermute | solution.py:389
  59.8 6.9 %copy-start = (bf16[256,256]{1,0:T(8,128)(2,1)S(1)}, bf16[256,256]{1,0:T(8,128)(2,1)}, u32[]{:S(2)}) copy-start(bf16[256,256]{1,0:T(8,128)(2,1)} %weight_ref.1) | copy-start | bytes 393220
  59.8 6.9 %copy-start.1 = (bf16[256,256]{1,0:T(8,128)(2,1)S(1)}, bf16[256,256]{1,0:T(8,128)(2,1)}, u32[]{:S(2)}) copy-start(bf16[256,256]{1,0:T(8,128)(2,1)} %cotangent_ref.1) | copy-start | bytes 393220
  61.1 5.1 %collective-permute-start.19 = (bf16[256,256]{1,0:T(8,128)(2,1)S(1)}, bf16[256,256]{1,0:T(8,128)(2,1)S(1)}, u32[]{:S(2)}, u32[]{:S(2)}) collective-permute-start(bf16[256,256]{1,0:T(8,128)(2,1)S(1)} %fusion.2), channel_id=1, source_target_pairs={{0,32},{32,64},{64,96},{96,128},{128,160},{160,192},{192,224},{224... | collective-permute-start | bytes 393224 | tf_op jit(solution)/shard_map/sum_rows/ppermute | solution.py:389
  62.8 3.8 %collective-permute-start.20 = (bf16[256,256]{1,0:T(8,128)(2,1)S(1)}, bf16[256,256]{1,0:T(8,128)(2,1)S(1)}, u32[]{:S(2)}, u32[]{:S(2)}) collective-permute-start(bf16[256,256]{1,0:T(8,128)(2,1)S(1)} %fusion.1), channel_id=1, source_target_pairs={{0,224},{32,0},{64,32},{96,64},{128,96},{160,128},{192,160},{224,1... | collective-permute-start | bytes 393224 | tf_op jit(solution)/shard_map/sum_rows/ppermute | solution.py:389
  67.6 7.5 %collective-permute-start.22 = (bf16[256,256]{1,0:T(8,128)(2,1)S(1)}, bf16[256,256]{1,0:T(8,128)(2,1)S(1)}, u32[]{:S(2)}, u32[]{:S(2)}) collective-permute-start(bf16[256,256]{1,0:T(8,128)(2,1)S(1)} %get-tuple-element.130.refs_8_), channel_id=1, source_target_pairs={{0,224},{32,0},{64,32},{96,64},{128,96},{160,128},{192,160},{224,1... | collective-permute-start | bytes 393224 | tf_op jit(solution)/shard_map/gather_rows/ppermute | solution.py:389
  69.9 5.2 %collective-permute-start.21 = (bf16[256,256]{1,0:T(8,128)(2,1)S(1)}, bf16[256,256]{1,0:T(8,128)(2,1)S(1)}, u32[]{:S(2)}, u32[]{:S(2)}) collective-permute-start(bf16[256,256]{1,0:T(8,128)(2,1)S(1)} %get-tuple-element.130.refs_8_), channel_id=1, source_target_pairs={{0,32},{32,64},{64,96},{96,128},{128,160},{160,192},{192,224},{224... | collective-permute-start | bytes 393224 | tf_op jit(solution)/shard_map/gather_rows/ppermute | solution.py:389
  70.7 4.9 %collective-permute-start.25 = (f32[64,256]{1,0:T(8,128)S(1)}, f32[64,256]{1,0:T(8,128)S(1)}, u32[]{:S(2)}, u32[]{:S(2)}) collective-permute-start(f32[64,256]{1,0:T(8,128)S(1)} %get-tuple-element.136), channel_id=1, source_target_pairs={{0,2},{1,3},{8,10},{9,11},{2,4},{3,5},{10,12},{11,13},{4,6},{5,7},... | collective-permute-start | bytes 196616 | tf_op jit(solution)/shard_map/gather_rows/ppermute | solution.py:386
  70.8 6.7 %collective-permute-start.26 = (f32[64,256]{1,0:T(8,128)S(1)}, f32[64,256]{1,0:T(8,128)S(1)}, u32[]{:S(2)}, u32[]{:S(2)}) collective-permute-start(f32[64,256]{1,0:T(8,128)S(1)} %get-tuple-element.137), channel_id=1, source_target_pairs={{0,4},{1,5},{8,12},{9,13},{2,6},{3,7},{10,14},{11,15},{4,0},{5,1},... | collective-permute-start | bytes 196616 | tf_op jit(solution)/shard_map/gather_rows/ppermute | solution.py:386
  75.1 3.4 %collective-permute-start.27 = (f32[64,256]{1,0:T(8,128)S(1)}, f32[64,256]{1,0:T(8,128)S(1)}, u32[]{:S(2)}, u32[]{:S(2)}) collective-permute-start(f32[64,256]{1,0:T(8,128)S(1)} %get-tuple-element.138), channel_id=1, source_target_pairs={{0,6},{1,7},{8,14},{9,15},{2,0},{3,1},{10,8},{11,9},{4,2},{5,3},{1... | collective-permute-start | bytes 196616 | tf_op jit(solution)/shard_map/gather_rows/ppermute | solution.py:386
  75.1 9.6 %collective-permute-start.23 = (bf16[256,256]{1,0:T(8,128)(2,1)S(1)}, bf16[256,256]{1,0:T(8,128)(2,1)S(1)}, u32[]{:S(2)}, u32[]{:S(2)}) collective-permute-start(bf16[256,256]{1,0:T(8,128)(2,1)S(1)} %collective-permute-done.21.refs_7_), channel_id=1, source_target_pairs={{0,32},{32,64},{64,96},{96,128},{128,160},{160,192},{192,224},{224... | collective-permute-start | bytes 393224 | tf_op jit(solution)/shard_map/gather_rows/ppermute | solution.py:389
  78.5 6.2 %collective-permute-start.24 = (bf16[256,256]{1,0:T(8,128)(2,1)S(1)}, bf16[256,256]{1,0:T(8,128)(2,1)S(1)}, u32[]{:S(2)}, u32[]{:S(2)}) collective-permute-start(bf16[256,256]{1,0:T(8,128)(2,1)S(1)} %collective-permute-done.22.refs_6_), channel_id=1, source_target_pairs={{0,224},{32,0},{64,32},{96,64},{128,96},{160,128},{192,160},{224,1... | collective-permute-start | bytes 393224 | tf_op jit(solution)/shard_map/gather_rows/ppermute | solution.py:389
  81.7 3.9 %collective-permute-start.30 = (f32[16,256]{1,0:T(8,128)S(1)}, f32[16,256]{1,0:T(8,128)S(1)}, u32[]{:S(2)}, u32[]{:S(2)}) collective-permute-start(f32[16,256]{1,0:T(8,128)S(1)} %get-tuple-element.147), channel_id=1, source_target_pairs={{0,1},{1,8},{8,9},{9,0},{2,3},{3,10},{10,11},{11,2},{4,5},{5,12},{... | collective-permute-start | bytes 49160 | tf_op jit(solution)/shard_map/gather_rows/ppermute | solution.py:386
  82.2 4.1 %collective-permute-start.31 = (f32[16,256]{1,0:T(8,128)S(1)}, f32[16,256]{1,0:T(8,128)S(1)}, u32[]{:S(2)}, u32[]{:S(2)}) collective-permute-start(f32[16,256]{1,0:T(8,128)S(1)} %get-tuple-element.148), channel_id=1, source_target_pairs={{0,8},{1,9},{8,0},{9,1},{2,10},{3,11},{10,2},{11,3},{4,12},{5,13},... | collective-permute-start | bytes 49160 | tf_op jit(solution)/shard_map/gather_rows/ppermute | solution.py:386
  82.4 3.9 %collective-permute-start.32 = (f32[16,256]{1,0:T(8,128)S(1)}, f32[16,256]{1,0:T(8,128)S(1)}, u32[]{:S(2)}, u32[]{:S(2)}) collective-permute-start(f32[16,256]{1,0:T(8,128)S(1)} %get-tuple-element.149), channel_id=1, source_target_pairs={{0,9},{1,0},{8,1},{9,8},{2,11},{3,2},{10,3},{11,10},{4,13},{5,4},{... | collective-permute-start | bytes 49160 | tf_op jit(solution)/shard_map/gather_rows/ppermute | solution.py:386
  84.7 6.7 %collective-permute-start.28 = (bf16[256,256]{1,0:T(8,128)(2,1)S(1)}, bf16[256,256]{1,0:T(8,128)(2,1)S(1)}, u32[]{:S(2)}, u32[]{:S(2)}) collective-permute-start(bf16[256,256]{1,0:T(8,128)(2,1)S(1)} %collective-permute-done.23.refs_5_), channel_id=1, source_target_pairs={{0,32},{32,64},{64,96},{96,128},{128,160},{160,192},{192,224},{224... | collective-permute-start | bytes 393224 | tf_op jit(solution)/shard_map/gather_rows/ppermute | solution.py:389
  86.4 4.9 %collective-permute-start.29 = (bf16[256,256]{1,0:T(8,128)(2,1)S(1)}, bf16[256,256]{1,0:T(8,128)(2,1)S(1)}, u32[]{:S(2)}, u32[]{:S(2)}) collective-permute-start(bf16[256,256]{1,0:T(8,128)(2,1)S(1)} %collective-permute-done.24.refs_4_), channel_id=1, source_target_pairs={{0,224},{32,0},{64,32},{96,64},{128,96},{160,128},{192,160},{224,1... | collective-permute-start | bytes 393224 | tf_op jit(solution)/shard_map/gather_rows/ppermute | solution.py:389
  88.0 3.7 %collective-permute-start.33 = (f32[16,256]{1,0:T(8,128)S(1)}, f32[16,256]{1,0:T(8,128)S(1)}, u32[]{:S(2)}, u32[]{:S(2)}) collective-permute-start(f32[16,256]{1,0:T(8,128)S(1)} %gather_rows.6), channel_id=1, source_target_pairs={{0,32},{16,48},{32,0},{48,16},{64,96},{80,112},{96,64},{112,80},{1... | collective-permute-start | bytes 49160 | tf_op jit(solution)/shard_map/gather_rows/ppermute | solution.py:393
  91.7 4.4 %collective-permute-start.34 = (bf16[128,256]{1,0:T(8,128)(2,1)S(1)}, bf16[128,256]{1,0:T(8,128)(2,1)S(1)}, u32[]{:S(2)}, u32[]{:S(2)}) collective-permute-start(bf16[128,256]{1,0:T(8,128)(2,1)S(1)} %slice.100), channel_id=1, source_target_pairs={{0,32},{32,64},{64,96},{96,128},{128,160},{160,192},{192,224},{224... | collective-permute-start | bytes 196616 | tf_op jit(solution)/shard_map/gather_rows/ppermute | solution.py:389
  91.8 4.3 %collective-permute-start.35 = (bf16[128,256]{1,0:T(8,128)(2,1)S(1)}, bf16[128,256]{1,0:T(8,128)(2,1)S(1)}, u32[]{:S(2)}, u32[]{:S(2)}) collective-permute-start(bf16[128,256]{1,0:T(8,128)(2,1)S(1)} %slice.101), channel_id=1, source_target_pairs={{0,224},{32,0},{64,32},{96,64},{128,96},{160,128},{192,160},{224,1... | collective-permute-start | bytes 196616 | tf_op jit(solution)/shard_map/gather_rows/ppermute | solution.py:389
  94.4 3.5 %collective-permute-start.36 = (f32[16,256]{1,0:T(8,128)S(1)}, f32[16,256]{1,0:T(8,128)S(1)}, u32[]{:S(2)}, u32[]{:S(2)}) collective-permute-start(f32[16,256]{1,0:T(8,128)S(1)} %add.113), channel_id=1, source_target_pairs={{0,64},{16,80},{32,96},{48,112},{64,0},{80,16},{96,32},{112,48},{1... | collective-permute-start | bytes 49160 | tf_op jit(solution)/shard_map/gather_rows/ppermute | solution.py:393
  98.0 18.2 %collective-permute-start.37 = (bf16[16,128,256]{2,1,0:T(8,128)(2,1)S(1)}, bf16[16,128,256]{2,1,0:T(8,128)(2,1)S(1)}, u32[]{:S(2)}, u32[]{:S(2)}) collective-permute-start(bf16[16,128,256]{2,1,0:T(8,128)(2,1)S(1)} %gather_rows.7.own_ref), channel_id=1, source_target_pairs={{0,16},{16,0},{32,48},{48,32},{64,80},{80,64},{96,112},{112,96},{1... | collective-permute-start | bytes 3145736 | tf_op jit(solution)/shard_map/gather_rows/ppermute | solution.py:393
  109.7 2.3 %collective-permute-start.38 = (f32[16,256]{1,0:T(8,128)S(1)}, f32[16,256]{1,0:T(8,128)S(1)}, u32[]{:S(2)}, u32[]{:S(2)}) collective-permute-start(f32[16,256]{1,0:T(8,128)S(1)} %add.114), channel_id=1, source_target_pairs={{0,16},{16,0},{32,48},{48,32},{64,80},{80,64},{96,112},{112,96},{1... | collective-permute-start | bytes 49160 | tf_op jit(solution)/shard_map/gather_rows/ppermute | solution.py:393
  112.0 8.7 %collective-permute-start.39 = (f32[16,256]{1,0:T(8,128)S(1)}, f32[16,256]{1,0:T(8,128)S(1)}, u32[]{:S(2)}, u32[]{:S(2)}) collective-permute-start(f32[16,256]{1,0:T(8,128)S(1)} %add.115), channel_id=1, source_target_pairs={{0,128},{16,144},{32,160},{48,176},{64,192},{80,208},{96,224},{112... | collective-permute-start | bytes 49160 | tf_op jit(solution)/shard_map/gather_rows/ppermute | solution.py:393

commit v5 on v4

--- a/solution.py
+++ b/solution.py
@@ -25,8 +25,7 @@
 
 
 def own_steps(depth):
-    middle = depth // 2
-    return [(2 * depth, 2)] + [(2 * depth + 2 + 4 * i, 4) for i in range(middle - 1)] + [(4 * depth - 2, 2)]
+    return [(2 * depth + 4 * i, 4) for i in range(depth // 2)]
 
 
 def slot_tables_kernel(sizes, coords_ref, count_ref, place_ref, table_ref):
@@ -37,8 +36,8 @@
     col = coords_ref[1:2, :]
     away = jnp.bitwise_and((row >> 2) - at_z, depth - 1)
     middle = depth // 2
-    spot = jnp.where(away <= middle, 2 * (middle - away) - 1, 2 * (away - middle))
-    spot = jnp.where(away == middle, 0, jnp.where(away == 0, depth - 1, spot))
+    spot = jnp.where(away < middle, 2 * (middle - away), 2 * (away - middle) + 1)
+    spot = jnp.where(away == middle, 0, jnp.where(away == 0, 1, spot))
     line_row = jnp.where(jnp.bitwise_and(row >> 1, 1) == at_c, 2 * depth, 0) + spot * 2 + jnp.bitwise_and(row, 1)
     rank = col >> 1
     col_x = jnp.bitwise_and(rank >> 1, nx - 1)
@@ -394,19 +393,15 @@
 
     with jax.named_scope("gather_features"):
         upright, level = node_features[:, :lanes], node_features[:, lanes:]
-        shifts = [1, nx - 1] + list(range(2, nx - 1))
-
-        def halves(across, along):
-            got = [(send(across, -o, 0), send(along, 0, -o)) for o in shifts]
-            got = together(tuple(value for pair in got for value in pair))
-            first, second = dict(zip(shifts, got[0::2])), dict(zip(shifts, got[1::2]))
-            return [first[o] for o in range(1, nx)], [second[o] for o in range(1, ny)]
-
-        at_side, at_line = halves(upright, level)
-        upright = jnp.concatenate([upright] + at_side, axis=0)
-        level = jnp.concatenate([level] + at_line, axis=0)
-        at_side, at_line = halves(level, upright)
-        pieces = (upright, *at_line, level, *at_side)
+        got = together(
+            tuple(send(upright, -o, 0) for o in range(1, nx)) + tuple(send(level, 0, -o) for o in range(1, ny))
+        )
+        upright = jnp.concatenate((upright,) + got[: nx - 1], axis=0)
+        level = jnp.concatenate((level,) + got[nx - 1 :], axis=0)
+        got = together(
+            tuple(send(upright, 0, -o) for o in range(1, ny)) + tuple(send(level, -o, 0) for o in range(1, nx))
+        )
+        pieces = (upright,) + got[: ny - 1] + (level,) + got[ny - 1 :]
 
     with jax.named_scope("tables"):
         table = slot_tables(block_coords[0, 0], count, place, sizes)
@@ -426,21 +421,22 @@
     with jax.named_scope("sum_rows"):
         half = local // 2
         middle = depth // 2
-        far = term(own.reshape(local, width), 0).astype(BF16)
+        ends = own.reshape(2, local, width)
+        far = term(ends[0], 0).astype(BF16)
         up, down = far[:half], far[half:]
         for step in range(1, middle + 1):
             pace, up, down = together((table, up, down))
-            own = own_rows(step, pace, blocks, source, depth)
+            if step < middle:
+                mine = own_rows(step, pace, blocks, source, depth).reshape(2, local, width)
             up, down = together((climb(up, 1), climb(down, -1)))
             if step == 1:
                 up = jnp.concatenate([up, jnp.zeros_like(up)], axis=0)
                 down = jnp.concatenate([jnp.zeros_like(down), down], axis=0)
-            mine = own.reshape(-1, local, width)
             if step < middle:
-                up = (term(mine[0], 2 * step - 1) + up.astype(F32)).astype(BF16)
-                down = (term(mine[1], 2 * step) + down.astype(F32)).astype(BF16)
+                up = (term(mine[0], 2 * step) + up.astype(F32)).astype(BF16)
+                down = (term(mine[1], 2 * step + 1) + down.astype(F32)).astype(BF16)
             else:
-                mixed = (term(mine[0], depth - 1) + (up.astype(F32) + down.astype(F32))).astype(BF16)
+                mixed = (term(ends[1], 1) + (up.astype(F32) + down.astype(F32))).astype(BF16)
 
     with jax.named_scope("dense"):
         hidden, act_grad, mixed_grad = dense(mixed, weight, cotangent)
@@ -458,23 +454,23 @@
                 first, *rest = weight_shares(place, mixed, act_grad, nx)
                 terms = [first] + [send(value, d + 1, 0) for d, value in enumerate(rest)]
             elif step <= 3:
-                terms, _ = together((tuple(terms), ahead))
+                terms = together((tuple(terms), ahead, behind))[0]
                 first, *rest = add_cut(place, terms, ny if step == 2 else 1)
                 if step == 2:
                     terms = [first] + [send(value, 0, d + 1) for d, value in enumerate(rest)]
                 else:
                     terms = [first, swap(first, 1, False)]
             else:
-                terms, _ = together((tuple(terms), ahead))
+                terms = together((tuple(terms), ahead, behind))[0]
                 first = terms[0] + terms[1]
                 terms = [first, swap(first, 2, False)]
             ahead, behind, terms[0] = together(moved + (terms[0],))
-            if step > 2:
+            if step == 3:
                 ahead, behind, *terms = together((ahead, behind, *terms))
             if step < middle:
                 chunks[depth - step] = ahead
                 chunks[step] = behind
-        order = [d for i in range(1, middle) for d in (middle - i, middle + i)] + [0]
+        order = [0] + [d for i in range(1, middle) for d in (middle - i, middle + i)]
         own_panel = own_rows_panel([ahead, behind] + [chunks[d] for d in order])
         own_panel, part = together((own_panel, terms[0] + terms[1]))
         sibling_panel = swap(own_panel)

time: 156 us -> 150 us (0.962)
  Pallas kernels: 22.7 us -> 17.7 us
  waiting for transfers between devices: 29.1 us -> 26.4 us
    ppermute x18, waiting for transfers between devices: 14.5 us -> 8.01 us  [send(): return lax.ppermute(value, PLANE, pairs)]
    ppermute x16, waiting for transfers between devices: 9.36 us -> 14.6 us  [climb(): lax.ppermute(value, 'z', [(i, (i + dz) % depth) for i in range(depth)])]
    ppermute x16, starting transfers between devices: 22.9 us -> 25.2 us  [climb(): lax.ppermute(value, 'z', [(i, (i + dz) % depth) for i in range(depth)])]
    ppermute x6, starting transfers between devices: 18.8 us -> 17 us  [swap(): return lax.ppermute(value, ('z', 'c'), pairs)]
    pallas_call x5 -> x4, Pallas kernels: 6.56 us -> 5.34 us  [own_rows(): pl.pallas_call(functools.partial(own_rows_kernel, step, depth), out_shape...]
  transfers between devices with their start and end apart: 40 -> 40, of which waited for: 21 -> 18; matrix products, arithmetic and copies ran while one was open for 0% -> 0% of each run, Pallas kernels for 11% -> 8%
where the time goes in v5:
time: 150 us; the launch traced here: 149 us
  starting transfers between devices  67.6 us (45%)
  blocking collectives  33.3 us (22%)
  waiting for transfers between devices  26.4 us (18%)
  Pallas kernels  17.7 us (12%)
  local copies, waits for them, and re-layouts  1.61 us (1%)
  between operations  1.57 us (1%)
    all_to_all x1, blocking collectives, body(): arrived = lax.all_to_all(outs, PLANE, 0, 0, tiled=True)  33.3 us
    ppermute x18, starting transfers between devices, send(): return lax.ppermute(value, PLANE, pairs)  25.4 us
    ppermute x16, starting transfers between devices, climb(): lax.ppermute(value, 'z', [(i, (i + dz) % depth) for i in range(depth)])  25.2 us
    ppermute x6, starting transfers between devices, swap(): return lax.ppermute(value, ('z', 'c'), pairs)  17 us
    ppermute x16, waiting for transfers between devices, climb(): lax.ppermute(value, 'z', [(i, (i + dz) % depth) for i in range(depth)])  14.6 us
    ppermute x18, waiting for transfers between devices, send(): return lax.ppermute(value, PLANE, pairs)  8.01 us
    pallas_call x4, Pallas kernels, own_rows(): pl.pallas_call(functools.partial(own_rows_kernel, step, depth), out_shape...  5.34 us
    ppermute x6, waiting for transfers between devices, swap(): return lax.ppermute(value, ('z', 'c'), pairs)  3.8 us
  transfers between devices with their start and end apart: 40, of which 18 were waited for; matrix products, arithmetic and copies ran while one was open for 0% of the time, Pallas kernels for 8%

profile of v5, /device:TPU:1, one launch (start us, length us, event | category | flops | bytes accessed | tf_op | source)
XLA Modules:
  0.0 148.8 jit_solution(584591536620244227)
XLA Ops:
  0.6 0.9 fusion.7
  1.5 2.2 %collective-permute-start.5 = (bf16[256,128]{1,0:T(8,128)(2,1)S(1)}, bf16[256,128]{1,0:T(8,128)(2,1)S(1)}, u32[]{:S(2)}, u32[]{:S(2)}) collective-permute-start(bf16[256,128]{1,0:T(8,128)(2,1)S(1)} %get-tuple-element.177), channel_id=1, source_target_pairs={{0,1},{1,8},{8,9},{9,0},{2,3},{3,10},{10,11},{11,2},{4,5},{5,12},{... | collective-permute-start | bytes 196616 | tf_op jit(solution)/shard_map/gather_features/ppermute | solution.py:385
  3.7 2.6 %collective-permute-start.4 = (bf16[256,128]{1,0:T(8,128)(2,1)S(1)}, bf16[256,128]{1,0:T(8,128)(2,1)S(1)}, u32[]{:S(2)}, u32[]{:S(2)}) collective-permute-start(bf16[256,128]{1,0:T(8,128)(2,1)S(1)} %get-tuple-element.177), channel_id=1, source_target_pairs={{0,8},{1,9},{8,0},{9,1},{2,10},{3,11},{10,2},{11,3},{4,12},{5,13},... | collective-permute-start | bytes 196616 | tf_op jit(solution)/shard_map/gather_features/ppermute | solution.py:385
  6.3 1.1 collective-permute-start.3
  7.4 1.2 collective-permute-start.2
  8.6 2.5 %collective-permute-start.1 = (bf16[256,128]{1,0:T(8,128)(2,1)S(1)}, bf16[256,128]{1,0:T(8,128)(2,1)S(1)}, u32[]{:S(2)}, u32[]{:S(2)}) collective-permute-start(bf16[256,128]{1,0:T(8,128)(2,1)S(1)} %get-tuple-element.178), channel_id=1, source_target_pairs={{0,4},{1,5},{8,12},{9,13},{2,6},{3,7},{10,14},{11,15},{4,0},{5,1},... | collective-permute-start | bytes 196616 | tf_op jit(solution)/shard_map/gather_features/ppermute | solution.py:385
  11.1 1.2 collective-permute-start
  12.2 1.2 collective-permute-done.1
  13.5 1.4 collective-permute-done
  15.0 3.5 %collective-permute-start.10 = (bf16[1024,128]{1,0:T(8,128)(2,1)S(1)}, bf16[1024,128]{1,0:T(8,128)(2,1)S(1)}, u32[]{:S(2)}, u32[]{:S(2)}) collective-permute-start(bf16[1024,128]{1,0:T(8,128)(2,1)S(1)} %pad_maximum_fusion.1.refs_4_), channel_id=1, source_target_pairs={{0,4},{1,5},{8,12},{9,13},{2,6},{3,7},{10,14},{11,15},{4,0},{5,1},... | collective-permute-start | bytes 786440 | tf_op jit(solution)/shard_map/gather_features/ppermute | solution.py:385
  18.5 0.5 collective-permute-start.8
  19.0 0.9 collective-permute-start.7
  19.9 1.5 %collective-permute-done.11.refs_7_ = bf16[1024,128]{1,0:T(8,128)(2,1)S(1)} collective-permute-done((bf16[1024,128]{1,0:T(8,128)(2,1)S(1)}, bf16[1024,128]{1,0:T(8,128)(2,1)S(1)}, u32[]{:S(2)}, u32[]{:S(2)}) %collective-permute-start.11) | collective-permute-done | bytes 262176 | tf_op jit(solution)/shard_map/gather_features/ppermute | solution.py:385
  21.4 0.5 collective-permute-start.6
  22.7 0.7 copy-done.2
  23.4 1.4 tables.2.table_ref
  24.7 1.9 %tables.3 = (bf16[256,128,128]{2,1,0:T(8,128)(2,1)S(1)}, f32[8,128]{1,0:T(8,128)}) custom-call(s32[1]{0:T(128)} %bitcast.39.count_ref, bf16[256,128,128]{2,1,0:T(8,128)(2,1)} %bitcast.42), custom_call_target="tpu_custom_call" | custom-call | tf_op jit(solution)/shard_map/tables/pallas_call | solution.py:237
  26.6 1.0 collective-permute-done.10.refs_6_
  27.6 1.2 collective-permute-done.9.refs_5_
  29.0 1.4 collective-permute-done.6.refs_1_
  30.4 2.3 %forward.2 = (bf16[16,128,256]{2,1,0:T(8,128)(2,1)S(1)}, bf16[33,128,256]{2,1,0:T(8,128)(2,1)S(1)}) custom-call(s32[8,384]{1,0:T(8,128)S(1)} %tables.2.table_ref, bf16[256,128,128]{2,1,0:T(8,128)(2,1)S(1)} %get-tuple-element.87.blocks_ref, bf16[1024,128]{1,0:T(8,128)(2,1)S(1)} %pad_maximum_fusion.refs_0_, ...), custom_call_target="tpu_custom_call" | custom-call | tf_op jit(solution)/shard_map/forward/pallas_call | solution.py:140
  32.7 5.0 %collective-permute-start.12 = (bf16[16,128,256]{2,1,0:T(8,128)(2,1)S(1)}, bf16[16,128,256]{2,1,0:T(8,128)(2,1)S(1)}, u32[]{:S(2)}, u32[]{:S(2)}) collective-permute-start(bf16[16,128,256]{2,1,0:T(8,128)(2,1)S(1)} %get-tuple-element.100), channel_id=1, source_target_pairs={{0,16},{16,0},{32,48},{48,32},{64,80},{80,64},{96,112},{112,96},{1... | collective-permute-start | bytes 3145736 | tf_op jit(solution)/shard_map/forward/ppermute | solution.py:392
  37.7 1.5 forward.3
  39.2 0.8 collective-permute-done.12
  40.1 0.8 collective-permute-start.13
  40.8 5.0 %collective-permute-start.14 = (bf16[128,256]{1,0:T(8,128)(2,1)S(1)}, bf16[128,256]{1,0:T(8,128)(2,1)S(1)}, u32[]{:S(2)}, u32[]{:S(2)}) collective-permute-start(bf16[128,256]{1,0:T(8,128)(2,1)S(1)} %get-tuple-element.106), channel_id=1, source_target_pairs={{0,224},{32,0},{64,32},{96,64},{128,96},{160,128},{192,160},{224,1... | collective-permute-start | bytes 196616 | tf_op jit(solution)/shard_map/sum_rows/ppermute | solution.py:388
  45.8 1.3 sum_rows.3
  47.2 0.7 collective-permute-done.13
  48.0 2.7 %collective-permute-start.16 = (bf16[256,256]{1,0:T(8,128)(2,1)S(1)}, bf16[256,256]{1,0:T(8,128)(2,1)S(1)}, u32[]{:S(2)}, u32[]{:S(2)}) collective-permute-start(bf16[256,256]{1,0:T(8,128)(2,1)S(1)} %get-tuple-element.111), channel_id=1, source_target_pairs={{0,224},{32,0},{64,32},{96,64},{128,96},{160,128},{192,160},{224,1... | collective-permute-start | bytes 393224 | tf_op jit(solution)/shard_map/sum_rows/ppermute | solution.py:388
  50.7 1.3 sum_rows.4
  52.1 1.3 collective-permute-done.15
  53.4 1.3 sum_rows.5
  54.8 0.5 collective-permute-start.17
  55.2 2.3 %collective-permute-start.18 = (bf16[256,256]{1,0:T(8,128)(2,1)S(1)}, bf16[256,256]{1,0:T(8,128)(2,1)S(1)}, u32[]{:S(2)}, u32[]{:S(2)}) collective-permute-start(bf16[256,256]{1,0:T(8,128)(2,1)S(1)} %fusion.2), channel_id=1, source_target_pairs={{0,224},{32,0},{64,32},{96,64},{128,96},{160,128},{192,160},{224,1... | collective-permute-start | bytes 393224 | tf_op jit(solution)/shard_map/sum_rows/ppermute | solution.py:388
  57.6 2.3 %collective-permute-done.17 = bf16[256,256]{1,0:T(8,128)(2,1)S(1)} collective-permute-done((bf16[256,256]{1,0:T(8,128)(2,1)S(1)}, bf16[256,256]{1,0:T(8,128)(2,1)S(1)}, u32[]{:S(2)}, u32[]{:S(2)}) %collective-permute-start.17) | collective-permute-done | bytes 131104 | tf_op jit(solution)/shard_map/sum_rows/ppermute | solution.py:388
  59.9 1.6 %collective-permute-start.19 = (bf16[256,256]{1,0:T(8,128)(2,1)S(1)}, bf16[256,256]{1,0:T(8,128)(2,1)S(1)}, u32[]{:S(2)}, u32[]{:S(2)}) collective-permute-start(bf16[256,256]{1,0:T(8,128)(2,1)S(1)} %fusion.1), channel_id=1, source_target_pairs={{0,32},{32,64},{64,96},{96,128},{128,160},{160,192},{192,224},{224... | collective-permute-start | bytes 393224 | tf_op jit(solution)/shard_map/sum_rows/ppermute | solution.py:388
  61.5 1.3 collective-permute-start.20
  62.8 2.3 %collective-permute-done.19 = bf16[256,256]{1,0:T(8,128)(2,1)S(1)} collective-permute-done((bf16[256,256]{1,0:T(8,128)(2,1)S(1)}, bf16[256,256]{1,0:T(8,128)(2,1)S(1)}, u32[]{:S(2)}, u32[]{:S(2)}) %collective-permute-start.19) | collective-permute-done | bytes 131104 | tf_op jit(solution)/shard_map/sum_rows/ppermute | solution.py:388
  65.0 0.3 collective-permute-done.20
  65.4 0.9 dense.1
  66.3 2.5 %collective-permute-start.22 = (bf16[256,256]{1,0:T(8,128)(2,1)S(1)}, bf16[256,256]{1,0:T(8,128)(2,1)S(1)}, u32[]{:S(2)}, u32[]{:S(2)}) collective-permute-start(bf16[256,256]{1,0:T(8,128)(2,1)S(1)} %get-tuple-element.124.refs_2_), channel_id=1, source_target_pairs={{0,224},{32,0},{64,32},{96,64},{128,96},{160,128},{192,160},{224,1... | collective-permute-start | bytes 393224 | tf_op jit(solution)/shard_map/gather_rows/ppermute | solution.py:388
  68.8 0.8 gather_rows.4
  69.6 2.5 %collective-permute-start.25 = (f32[64,256]{1,0:T(8,128)S(1)}, f32[64,256]{1,0:T(8,128)S(1)}, u32[]{:S(2)}, u32[]{:S(2)}) collective-permute-start(f32[64,256]{1,0:T(8,128)S(1)} %get-tuple-element.130), channel_id=1, source_target_pairs={{0,2},{1,3},{8,10},{9,11},{2,4},{3,5},{10,12},{11,13},{4,6},{5,7},... | collective-permute-start | bytes 196616 | tf_op jit(solution)/shard_map/gather_rows/ppermute | solution.py:385
  72.1 1.2 collective-permute-start.26
  73.3 1.3 collective-permute-start.27
  74.6 2.7 %collective-permute-start.24 = (bf16[256,256]{1,0:T(8,128)(2,1)S(1)}, bf16[256,256]{1,0:T(8,128)(2,1)S(1)}, u32[]{:S(2)}, u32[]{:S(2)}) collective-permute-start(bf16[256,256]{1,0:T(8,128)(2,1)S(1)} %collective-permute-done.22.refs_7_), channel_id=1, source_target_pairs={{0,224},{32,0},{64,32},{96,64},{128,96},{160,128},{192,160},{224,1... | collective-permute-start | bytes 393224 | tf_op jit(solution)/shard_map/gather_rows/ppermute | solution.py:388
  77.4 0.6 gather_rows.5
  77.9 1.8 %collective-permute-start.30 = (f32[16,256]{1,0:T(8,128)S(1)}, f32[16,256]{1,0:T(8,128)S(1)}, u32[]{:S(2)}, u32[]{:S(2)}) collective-permute-start(f32[16,256]{1,0:T(8,128)S(1)} %get-tuple-element.141), channel_id=1, source_target_pairs={{0,1},{1,8},{8,9},{9,0},{2,3},{3,10},{10,11},{11,2},{4,5},{5,12},{... | collective-permute-start | bytes 49160 | tf_op jit(solution)/shard_map/gather_rows/ppermute | solution.py:385
  79.7 1.3 collective-permute-start.31
  81.0 1.2 collective-permute-start.32
  82.2 2.7 %collective-permute-start.29 = (bf16[256,256]{1,0:T(8,128)(2,1)S(1)}, bf16[256,256]{1,0:T(8,128)(2,1)S(1)}, u32[]{:S(2)}, u32[]{:S(2)}) collective-permute-start(bf16[256,256]{1,0:T(8,128)(2,1)S(1)} %collective-permute-done.24.refs_5_), channel_id=1, source_target_pairs={{0,224},{32,0},{64,32},{96,64},{128,96},{160,128},{192,160},{224,1... | collective-permute-start | bytes 393224 | tf_op jit(solution)/shard_map/gather_rows/ppermute | solution.py:388
  84.9 0.5 gather_rows.6
  85.5 2.8 %collective-permute-done.28.refs_4_ = bf16[256,256]{1,0:T(8,128)(2,1)S(1)} collective-permute-done((bf16[256,256]{1,0:T(8,128)(2,1)S(1)}, bf16[256,256]{1,0:T(8,128)(2,1)S(1)}, u32[]{:S(2)}, u32[]{:S(2)}) %collective-permute-start.28) | collective-permute-done | bytes 131104 | tf_op jit(solution)/shard_map/gather_rows/ppermute | solution.py:388
  88.3 3.2 %collective-permute-start.35 = (bf16[128,256]{1,0:T(8,128)(2,1)S(1)}, bf16[128,256]{1,0:T(8,128)(2,1)S(1)}, u32[]{:S(2)}, u32[]{:S(2)}) collective-permute-start(bf16[128,256]{1,0:T(8,128)(2,1)S(1)} %slice.111), channel_id=1, source_target_pairs={{0,224},{32,0},{64,32},{96,64},{128,96},{160,128},{192,160},{224,1... | collective-permute-start | bytes 196616 | tf_op jit(solution)/shard_map/gather_rows/ppermute | solution.py:388
  91.5 0.3 collective-permute-start.36
  91.8 1.0 collective-permute-done.35.refs_1_
  92.9 3.9 %collective-permute-done.34.refs_0_ = bf16[128,256]{1,0:T(8,128)(2,1)S(1)} collective-permute-done((bf16[128,256]{1,0:T(8,128)(2,1)S(1)}, bf16[128,256]{1,0:T(8,128)(2,1)S(1)}, u32[]{:S(2)}, u32[]{:S(2)}) %collective-permute-start.34) | collective-permute-done | bytes 65568 | tf_op jit(solution)/shard_map/gather_rows/ppermute | solution.py:388
  96.9 8.7 %collective-permute-start.37 = (bf16[16,128,256]{2,1,0:T(8,128)(2,1)S(1)}, bf16[16,128,256]{2,1,0:T(8,128)(2,1)S(1)}, u32[]{:S(2)}, u32[]{:S(2)}) collective-permute-start(bf16[16,128,256]{2,1,0:T(8,128)(2,1)S(1)} %gather_rows.7.own_ref), channel_id=1, source_target_pairs={{0,16},{16,0},{32,48},{48,32},{64,80},{80,64},{96,112},{112,96},{1... | collective-permute-start | bytes 3145736 | tf_op jit(solution)/shard_map/gather_rows/ppermute | solution.py:392
  105.7 2.2 %collective-permute-done.38 = f32[16,256]{1,0:T(8,128)S(1)} collective-permute-done((f32[16,256]{1,0:T(8,128)S(1)}, f32[16,256]{1,0:T(8,128)S(1)}, u32[]{:S(2)}, u32[]{:S(2)}) %collective-permute-start.38) | collective-permute-done | bytes 16416 | tf_op jit(solution)/shard_map/gather_rows/ppermute | solution.py:392
  107.9 2.8 %collective-permute-start.39 = (f32[16,256]{1,0:T(8,128)S(1)}, f32[16,256]{1,0:T(8,128)S(1)}, u32[]{:S(2)}, u32[]{:S(2)}) collective-permute-start(f32[16,256]{1,0:T(8,128)S(1)} %add.115), channel_id=1, source_target_pairs={{0,128},{16,144},{32,160},{48,176},{64,192},{80,208},{96,224},{112... | collective-permute-start | bytes 49160 | tf_op jit(solution)/shard_map/gather_rows/ppermute | solution.py:392
  110.7 2.9 %backward.1 = bf16[16,272,256]{2,1,0:T(8,128)(2,1)S(1)} custom-call(s32[8,384]{1,0:T(8,128)S(1)} %tables.2.table_ref, s32[4]{0:T(128)S(1)} %pad_add_fusion.place_ref, bf16[256,128,128]{2,1,0:T(8,128)(2,1)S(1)} %get-tuple-element.87.blocks_ref, bf16[16,128,256]{2,1,0:T(8,128)(2,1)S(1)} %collective-permute-done.37.sibling_ref, ...), custom_call_target="tpu_custom_call" | custom-call | flops 4000000000 | tf_op jit(solution)/shard_map/backward/pallas_call | solution.py:196
  113.7 0.8 collective-permute-done.39
  114.5 33.3 %all_to_all.5.arrived_ref = bf16[16,272,256]{2,1,0:T(8,128)(2,1)S(1)} all-to-all(bf16[16,272,256]{2,1,0:T(8,128)(2,1)S(1)} %broadcast_dynamic-update-slice_fusion), channel_id=1, replica_groups=mesh['z'=8,'c'=2,'yh'=2,'x'=4,'yl'=2] {'yh','x','yl'}, dimensions={0} | all-to-all | bytes 4456448 | tf_op jit(solution)/shard_map/sum_columns/all_to_all | solution.py:488
  147.8 1.0 sum_columns.1
  (59 shorter events, 1.4 us)
Async XLA Ops:
  1.5 9.6 %collective-permute-start.5 = (bf16[256,128]{1,0:T(8,128)(2,1)S(1)}, bf16[256,128]{1,0:T(8,128)(2,1)S(1)}, u32[]{:S(2)}, u32[]{:S(2)}) collective-permute-start(bf16[256,128]{1,0:T(8,128)(2,1)S(1)} %get-tuple-element.177), channel_id=1, source_target_pairs={{0,1},{1,8},{8,9},{9,0},{2,3},{3,10},{10,11},{11,2},{4,5},{5,12},{... | collective-permute-start | bytes 196616 | tf_op jit(solution)/shard_map/gather_features/ppermute | solution.py:385
  3.7 8.5 %collective-permute-start.4 = (bf16[256,128]{1,0:T(8,128)(2,1)S(1)}, bf16[256,128]{1,0:T(8,128)(2,1)S(1)}, u32[]{:S(2)}, u32[]{:S(2)}) collective-permute-start(bf16[256,128]{1,0:T(8,128)(2,1)S(1)} %get-tuple-element.177), channel_id=1, source_target_pairs={{0,8},{1,9},{8,0},{9,1},{2,10},{3,11},{10,2},{11,3},{4,12},{5,13},... | collective-permute-start | bytes 196616 | tf_op jit(solution)/shard_map/gather_features/ppermute | solution.py:385
  6.3 5.9 %collective-permute-start.3 = (bf16[256,128]{1,0:T(8,128)(2,1)S(1)}, bf16[256,128]{1,0:T(8,128)(2,1)S(1)}, u32[]{:S(2)}, u32[]{:S(2)}) collective-permute-start(bf16[256,128]{1,0:T(8,128)(2,1)S(1)} %get-tuple-element.177), channel_id=1, source_target_pairs={{0,9},{1,0},{8,1},{9,8},{2,11},{3,2},{10,3},{11,10},{4,13},{5,4},{... | collective-permute-start | bytes 196616 | tf_op jit(solution)/shard_map/gather_features/ppermute | solution.py:385
  7.4 4.8 %collective-permute-start.2 = (bf16[256,128]{1,0:T(8,128)(2,1)S(1)}, bf16[256,128]{1,0:T(8,128)(2,1)S(1)}, u32[]{:S(2)}, u32[]{:S(2)}) collective-permute-start(bf16[256,128]{1,0:T(8,128)(2,1)S(1)} %get-tuple-element.178), channel_id=1, source_target_pairs={{0,2},{1,3},{8,10},{9,11},{2,4},{3,5},{10,12},{11,13},{4,6},{5,7},... | collective-permute-start | bytes 196616 | tf_op jit(solution)/shard_map/gather_features/ppermute | solution.py:385
  8.6 4.8 %collective-permute-start.1 = (bf16[256,128]{1,0:T(8,128)(2,1)S(1)}, bf16[256,128]{1,0:T(8,128)(2,1)S(1)}, u32[]{:S(2)}, u32[]{:S(2)}) collective-permute-start(bf16[256,128]{1,0:T(8,128)(2,1)S(1)} %get-tuple-element.178), channel_id=1, source_target_pairs={{0,4},{1,5},{8,12},{9,13},{2,6},{3,7},{10,14},{11,15},{4,0},{5,1},... | collective-permute-start | bytes 196616 | tf_op jit(solution)/shard_map/gather_features/ppermute | solution.py:385
  11.1 3.8 %collective-permute-start = (bf16[256,128]{1,0:T(8,128)(2,1)S(1)}, bf16[256,128]{1,0:T(8,128)(2,1)S(1)}, u32[]{:S(2)}, u32[]{:S(2)}) collective-permute-start(bf16[256,128]{1,0:T(8,128)(2,1)S(1)} %get-tuple-element.178), channel_id=1, source_target_pairs={{0,6},{1,7},{8,14},{9,15},{2,0},{3,1},{10,8},{11,9},{4,2},{5,3},{1... | collective-permute-start | bytes 196616 | tf_op jit(solution)/shard_map/gather_features/ppermute | solution.py:385
  14.9 6.5 %collective-permute-start.11 = (bf16[1024,128]{1,0:T(8,128)(2,1)S(1)}, bf16[1024,128]{1,0:T(8,128)(2,1)S(1)}, u32[]{:S(2)}, u32[]{:S(2)}) collective-permute-start(bf16[1024,128]{1,0:T(8,128)(2,1)S(1)} %pad_maximum_fusion.1.refs_4_), channel_id=1, source_target_pairs={{0,2},{1,3},{8,10},{9,11},{2,4},{3,5},{10,12},{11,13},{4,6},{5,7},... | collective-permute-start | bytes 786440 | tf_op jit(solution)/shard_map/gather_features/ppermute | solution.py:385
  15.0 12.6 %collective-permute-start.10 = (bf16[1024,128]{1,0:T(8,128)(2,1)S(1)}, bf16[1024,128]{1,0:T(8,128)(2,1)S(1)}, u32[]{:S(2)}, u32[]{:S(2)}) collective-permute-start(bf16[1024,128]{1,0:T(8,128)(2,1)S(1)} %pad_maximum_fusion.1.refs_4_), channel_id=1, source_target_pairs={{0,4},{1,5},{8,12},{9,13},{2,6},{3,7},{10,14},{11,15},{4,0},{5,1},... | collective-permute-start | bytes 786440 | tf_op jit(solution)/shard_map/gather_features/ppermute | solution.py:385
  18.5 10.3 %collective-permute-start.9 = (bf16[1024,128]{1,0:T(8,128)(2,1)S(1)}, bf16[1024,128]{1,0:T(8,128)(2,1)S(1)}, u32[]{:S(2)}, u32[]{:S(2)}) collective-permute-start(bf16[1024,128]{1,0:T(8,128)(2,1)S(1)} %pad_maximum_fusion.1.refs_4_), channel_id=1, source_target_pairs={{0,6},{1,7},{8,14},{9,15},{2,0},{3,1},{10,8},{11,9},{4,2},{5,3},{1... | collective-permute-start | bytes 786440 | tf_op jit(solution)/shard_map/gather_features/ppermute | solution.py:385
  18.5 10.3 %collective-permute-start.8 = (bf16[1024,128]{1,0:T(8,128)(2,1)S(1)}, bf16[1024,128]{1,0:T(8,128)(2,1)S(1)}, u32[]{:S(2)}, u32[]{:S(2)}) collective-permute-start(bf16[1024,128]{1,0:T(8,128)(2,1)S(1)} %pad_maximum_fusion.refs_0_), channel_id=1, source_target_pairs={{0,1},{1,8},{8,9},{9,0},{2,3},{3,10},{10,11},{11,2},{4,5},{5,12},{... | collective-permute-start | bytes 786440 | tf_op jit(solution)/shard_map/gather_features/ppermute | solution.py:385
  19.0 10.0 %collective-permute-start.7 = (bf16[1024,128]{1,0:T(8,128)(2,1)S(1)}, bf16[1024,128]{1,0:T(8,128)(2,1)S(1)}, u32[]{:S(2)}, u32[]{:S(2)}) collective-permute-start(bf16[1024,128]{1,0:T(8,128)(2,1)S(1)} %pad_maximum_fusion.refs_0_), channel_id=1, source_target_pairs={{0,8},{1,9},{8,0},{9,1},{2,10},{3,11},{10,2},{11,3},{4,12},{5,13},... | collective-permute-start | bytes 786440 | tf_op jit(solution)/shard_map/gather_features/ppermute | solution.py:385
  21.4 9.0 %collective-permute-start.6 = (bf16[1024,128]{1,0:T(8,128)(2,1)S(1)}, bf16[1024,128]{1,0:T(8,128)(2,1)S(1)}, u32[]{:S(2)}, u32[]{:S(2)}) collective-permute-start(bf16[1024,128]{1,0:T(8,128)(2,1)S(1)} %pad_maximum_fusion.refs_0_), channel_id=1, source_target_pairs={{0,9},{1,0},{8,1},{9,8},{2,11},{3,2},{10,3},{11,10},{4,13},{5,4},{... | collective-permute-start | bytes 786440 | tf_op jit(solution)/shard_map/gather_features/ppermute | solution.py:385
  22.7 0.7 copy-start.2
  32.7 7.2 %collective-permute-start.12 = (bf16[16,128,256]{2,1,0:T(8,128)(2,1)S(1)}, bf16[16,128,256]{2,1,0:T(8,128)(2,1)S(1)}, u32[]{:S(2)}, u32[]{:S(2)}) collective-permute-start(bf16[16,128,256]{2,1,0:T(8,128)(2,1)S(1)} %get-tuple-element.100), channel_id=1, source_target_pairs={{0,16},{16,0},{32,48},{48,32},{64,80},{80,64},{96,112},{112,96},{1... | collective-permute-start | bytes 3145736 | tf_op jit(solution)/shard_map/forward/ppermute | solution.py:392
  40.1 7.8 %collective-permute-start.13 = (bf16[128,256]{1,0:T(8,128)(2,1)S(1)}, bf16[128,256]{1,0:T(8,128)(2,1)S(1)}, u32[]{:S(2)}, u32[]{:S(2)}) collective-permute-start(bf16[128,256]{1,0:T(8,128)(2,1)S(1)} %get-tuple-element.105), channel_id=1, source_target_pairs={{0,32},{32,64},{64,96},{96,128},{128,160},{160,192},{192,224},{224... | collective-permute-start | bytes 196616 | tf_op jit(solution)/shard_map/sum_rows/ppermute | solution.py:388
  40.8 7.1 %collective-permute-start.14 = (bf16[128,256]{1,0:T(8,128)(2,1)S(1)}, bf16[128,256]{1,0:T(8,128)(2,1)S(1)}, u32[]{:S(2)}, u32[]{:S(2)}) collective-permute-start(bf16[128,256]{1,0:T(8,128)(2,1)S(1)} %get-tuple-element.106), channel_id=1, source_target_pairs={{0,224},{32,0},{64,32},{96,64},{128,96},{160,128},{192,160},{224,1... | collective-permute-start | bytes 196616 | tf_op jit(solution)/shard_map/sum_rows/ppermute | solution.py:388
  47.9 5.4 %collective-permute-start.15 = (bf16[256,256]{1,0:T(8,128)(2,1)S(1)}, bf16[256,256]{1,0:T(8,128)(2,1)S(1)}, u32[]{:S(2)}, u32[]{:S(2)}) collective-permute-start(bf16[256,256]{1,0:T(8,128)(2,1)S(1)} %get-tuple-element.110), channel_id=1, source_target_pairs={{0,32},{32,64},{64,96},{96,128},{128,160},{160,192},{192,224},{224... | collective-permute-start | bytes 393224 | tf_op jit(solution)/shard_map/sum_rows/ppermute | solution.py:388
  48.0 5.3 %collective-permute-start.16 = (bf16[256,256]{1,0:T(8,128)(2,1)S(1)}, bf16[256,256]{1,0:T(8,128)(2,1)S(1)}, u32[]{:S(2)}, u32[]{:S(2)}) collective-permute-start(bf16[256,256]{1,0:T(8,128)(2,1)S(1)} %get-tuple-element.111), channel_id=1, source_target_pairs={{0,224},{32,0},{64,32},{96,64},{128,96},{160,128},{192,160},{224,1... | collective-permute-start | bytes 393224 | tf_op jit(solution)/shard_map/sum_rows/ppermute | solution.py:388
  54.7 10.6 %copy-start = (bf16[256,256]{1,0:T(8,128)(2,1)S(1)}, bf16[256,256]{1,0:T(8,128)(2,1)}, u32[]{:S(2)}) copy-start(bf16[256,256]{1,0:T(8,128)(2,1)} %weight_ref.1) | copy-start | bytes 393220
  54.7 10.6 %copy-start.1 = (bf16[256,256]{1,0:T(8,128)(2,1)S(1)}, bf16[256,256]{1,0:T(8,128)(2,1)}, u32[]{:S(2)}) copy-start(bf16[256,256]{1,0:T(8,128)(2,1)} %cotangent_ref.1) | copy-start | bytes 393220
  54.8 5.1 %collective-permute-start.17 = (bf16[256,256]{1,0:T(8,128)(2,1)S(1)}, bf16[256,256]{1,0:T(8,128)(2,1)S(1)}, u32[]{:S(2)}, u32[]{:S(2)}) collective-permute-start(bf16[256,256]{1,0:T(8,128)(2,1)S(1)} %fusion.3), channel_id=1, source_target_pairs={{0,32},{32,64},{64,96},{96,128},{128,160},{160,192},{192,224},{224... | collective-permute-start | bytes 393224 | tf_op jit(solution)/shard_map/sum_rows/ppermute | solution.py:388
  55.2 4.6 %collective-permute-start.18 = (bf16[256,256]{1,0:T(8,128)(2,1)S(1)}, bf16[256,256]{1,0:T(8,128)(2,1)S(1)}, u32[]{:S(2)}, u32[]{:S(2)}) collective-permute-start(bf16[256,256]{1,0:T(8,128)(2,1)S(1)} %fusion.2), channel_id=1, source_target_pairs={{0,224},{32,0},{64,32},{96,64},{128,96},{160,128},{192,160},{224,1... | collective-permute-start | bytes 393224 | tf_op jit(solution)/shard_map/sum_rows/ppermute | solution.py:388
  59.9 5.1 %collective-permute-start.19 = (bf16[256,256]{1,0:T(8,128)(2,1)S(1)}, bf16[256,256]{1,0:T(8,128)(2,1)S(1)}, u32[]{:S(2)}, u32[]{:S(2)}) collective-permute-start(bf16[256,256]{1,0:T(8,128)(2,1)S(1)} %fusion.1), channel_id=1, source_target_pairs={{0,32},{32,64},{64,96},{96,128},{128,160},{160,192},{192,224},{224... | collective-permute-start | bytes 393224 | tf_op jit(solution)/shard_map/sum_rows/ppermute | solution.py:388
  61.5 3.8 %collective-permute-start.20 = (bf16[256,256]{1,0:T(8,128)(2,1)S(1)}, bf16[256,256]{1,0:T(8,128)(2,1)S(1)}, u32[]{:S(2)}, u32[]{:S(2)}) collective-permute-start(bf16[256,256]{1,0:T(8,128)(2,1)S(1)} %fusion), channel_id=1, source_target_pairs={{0,224},{32,0},{64,32},{96,64},{128,96},{160,128},{192,160},{224,1... | collective-permute-start | bytes 393224 | tf_op jit(solution)/shard_map/sum_rows/ppermute | solution.py:388
  66.3 8.3 %collective-permute-start.22 = (bf16[256,256]{1,0:T(8,128)(2,1)S(1)}, bf16[256,256]{1,0:T(8,128)(2,1)S(1)}, u32[]{:S(2)}, u32[]{:S(2)}) collective-permute-start(bf16[256,256]{1,0:T(8,128)(2,1)S(1)} %get-tuple-element.124.refs_2_), channel_id=1, source_target_pairs={{0,224},{32,0},{64,32},{96,64},{128,96},{160,128},{192,160},{224,1... | collective-permute-start | bytes 393224 | tf_op jit(solution)/shard_map/gather_rows/ppermute | solution.py:388
  68.8 5.8 %collective-permute-start.21 = (bf16[256,256]{1,0:T(8,128)(2,1)S(1)}, bf16[256,256]{1,0:T(8,128)(2,1)S(1)}, u32[]{:S(2)}, u32[]{:S(2)}) collective-permute-start(bf16[256,256]{1,0:T(8,128)(2,1)S(1)} %get-tuple-element.124.refs_2_), channel_id=1, source_target_pairs={{0,32},{32,64},{64,96},{96,128},{128,160},{160,192},{192,224},{224... | collective-permute-start | bytes 393224 | tf_op jit(solution)/shard_map/gather_rows/ppermute | solution.py:388
  69.6 7.8 %collective-permute-start.25 = (f32[64,256]{1,0:T(8,128)S(1)}, f32[64,256]{1,0:T(8,128)S(1)}, u32[]{:S(2)}, u32[]{:S(2)}) collective-permute-start(f32[64,256]{1,0:T(8,128)S(1)} %get-tuple-element.130), channel_id=1, source_target_pairs={{0,2},{1,3},{8,10},{9,11},{2,4},{3,5},{10,12},{11,13},{4,6},{5,7},... | collective-permute-start | bytes 196616 | tf_op jit(solution)/shard_map/gather_rows/ppermute | solution.py:385
  72.1 5.3 %collective-permute-start.26 = (f32[64,256]{1,0:T(8,128)S(1)}, f32[64,256]{1,0:T(8,128)S(1)}, u32[]{:S(2)}, u32[]{:S(2)}) collective-permute-start(f32[64,256]{1,0:T(8,128)S(1)} %get-tuple-element.131), channel_id=1, source_target_pairs={{0,4},{1,5},{8,12},{9,13},{2,6},{3,7},{10,14},{11,15},{4,0},{5,1},... | collective-permute-start | bytes 196616 | tf_op jit(solution)/shard_map/gather_rows/ppermute | solution.py:385
  73.3 4.1 %collective-permute-start.27 = (f32[64,256]{1,0:T(8,128)S(1)}, f32[64,256]{1,0:T(8,128)S(1)}, u32[]{:S(2)}, u32[]{:S(2)}) collective-permute-start(f32[64,256]{1,0:T(8,128)S(1)} %get-tuple-element.132), channel_id=1, source_target_pairs={{0,6},{1,7},{8,14},{9,15},{2,0},{3,1},{10,8},{11,9},{4,2},{5,3},{1... | collective-permute-start | bytes 196616 | tf_op jit(solution)/shard_map/gather_rows/ppermute | solution.py:385
  74.6 7.6 %collective-permute-start.23 = (bf16[256,256]{1,0:T(8,128)(2,1)S(1)}, bf16[256,256]{1,0:T(8,128)(2,1)S(1)}, u32[]{:S(2)}, u32[]{:S(2)}) collective-permute-start(bf16[256,256]{1,0:T(8,128)(2,1)S(1)} %collective-permute-done.21.refs_8_), channel_id=1, source_target_pairs={{0,32},{32,64},{64,96},{96,128},{128,160},{160,192},{192,224},{224... | collective-permute-start | bytes 393224 | tf_op jit(solution)/shard_map/gather_rows/ppermute | solution.py:388
  74.6 7.5 %collective-permute-start.24 = (bf16[256,256]{1,0:T(8,128)(2,1)S(1)}, bf16[256,256]{1,0:T(8,128)(2,1)S(1)}, u32[]{:S(2)}, u32[]{:S(2)}) collective-permute-start(bf16[256,256]{1,0:T(8,128)(2,1)S(1)} %collective-permute-done.22.refs_7_), channel_id=1, source_target_pairs={{0,224},{32,0},{64,32},{96,64},{128,96},{160,128},{192,160},{224,1... | collective-permute-start | bytes 393224 | tf_op jit(solution)/shard_map/gather_rows/ppermute | solution.py:388
  77.9 6.9 %collective-permute-start.30 = (f32[16,256]{1,0:T(8,128)S(1)}, f32[16,256]{1,0:T(8,128)S(1)}, u32[]{:S(2)}, u32[]{:S(2)}) collective-permute-start(f32[16,256]{1,0:T(8,128)S(1)} %get-tuple-element.141), channel_id=1, source_target_pairs={{0,1},{1,8},{8,9},{9,0},{2,3},{3,10},{10,11},{11,2},{4,5},{5,12},{... | collective-permute-start | bytes 49160 | tf_op jit(solution)/shard_map/gather_rows/ppermute | solution.py:385
  79.7 5.2 %collective-permute-start.31 = (f32[16,256]{1,0:T(8,128)S(1)}, f32[16,256]{1,0:T(8,128)S(1)}, u32[]{:S(2)}, u32[]{:S(2)}) collective-permute-start(f32[16,256]{1,0:T(8,128)S(1)} %get-tuple-element.142), channel_id=1, source_target_pairs={{0,8},{1,9},{8,0},{9,1},{2,10},{3,11},{10,2},{11,3},{4,12},{5,13},... | collective-permute-start | bytes 49160 | tf_op jit(solution)/shard_map/gather_rows/ppermute | solution.py:385
  81.0 3.9 %collective-permute-start.32 = (f32[16,256]{1,0:T(8,128)S(1)}, f32[16,256]{1,0:T(8,128)S(1)}, u32[]{:S(2)}, u32[]{:S(2)}) collective-permute-start(f32[16,256]{1,0:T(8,128)S(1)} %get-tuple-element.143), channel_id=1, source_target_pairs={{0,9},{1,0},{8,1},{9,8},{2,11},{3,2},{10,3},{11,10},{4,13},{5,4},{... | collective-permute-start | bytes 49160 | tf_op jit(solution)/shard_map/gather_rows/ppermute | solution.py:385
  82.2 6.1 %collective-permute-start.28 = (bf16[256,256]{1,0:T(8,128)(2,1)S(1)}, bf16[256,256]{1,0:T(8,128)(2,1)S(1)}, u32[]{:S(2)}, u32[]{:S(2)}) collective-permute-start(bf16[256,256]{1,0:T(8,128)(2,1)S(1)} %collective-permute-done.23.refs_6_), channel_id=1, source_target_pairs={{0,32},{32,64},{64,96},{96,128},{128,160},{160,192},{192,224},{224... | collective-permute-start | bytes 393224 | tf_op jit(solution)/shard_map/gather_rows/ppermute | solution.py:388
  82.2 6.1 %collective-permute-start.29 = (bf16[256,256]{1,0:T(8,128)(2,1)S(1)}, bf16[256,256]{1,0:T(8,128)(2,1)S(1)}, u32[]{:S(2)}, u32[]{:S(2)}) collective-permute-start(bf16[256,256]{1,0:T(8,128)(2,1)S(1)} %collective-permute-done.24.refs_5_), channel_id=1, source_target_pairs={{0,224},{32,0},{64,32},{96,64},{128,96},{160,128},{192,160},{224,1... | collective-permute-start | bytes 393224 | tf_op jit(solution)/shard_map/gather_rows/ppermute | solution.py:388
  85.4 2.9 %collective-permute-start.33 = (f32[16,256]{1,0:T(8,128)S(1)}, f32[16,256]{1,0:T(8,128)S(1)}, u32[]{:S(2)}, u32[]{:S(2)}) collective-permute-start(f32[16,256]{1,0:T(8,128)S(1)} %gather_rows.6), channel_id=1, source_target_pairs={{0,32},{16,48},{32,0},{48,16},{64,96},{80,112},{96,64},{112,80},{1... | collective-permute-start | bytes 49160 | tf_op jit(solution)/shard_map/gather_rows/ppermute | solution.py:392
  88.3 4.5 %collective-permute-start.35 = (bf16[128,256]{1,0:T(8,128)(2,1)S(1)}, bf16[128,256]{1,0:T(8,128)(2,1)S(1)}, u32[]{:S(2)}, u32[]{:S(2)}) collective-permute-start(bf16[128,256]{1,0:T(8,128)(2,1)S(1)} %slice.111), channel_id=1, source_target_pairs={{0,224},{32,0},{64,32},{96,64},{128,96},{160,128},{192,160},{224,1... | collective-permute-start | bytes 196616 | tf_op jit(solution)/shard_map/gather_rows/ppermute | solution.py:388
  91.5 5.3 %collective-permute-start.34 = (bf16[128,256]{1,0:T(8,128)(2,1)S(1)}, bf16[128,256]{1,0:T(8,128)(2,1)S(1)}, u32[]{:S(2)}, u32[]{:S(2)}) collective-permute-start(bf16[128,256]{1,0:T(8,128)(2,1)S(1)} %slice.110), channel_id=1, source_target_pairs={{0,32},{32,64},{64,96},{96,128},{128,160},{160,192},{192,224},{224... | collective-permute-start | bytes 196616 | tf_op jit(solution)/shard_map/gather_rows/ppermute | solution.py:388
  91.5 5.3 %collective-permute-start.36 = (f32[16,256]{1,0:T(8,128)S(1)}, f32[16,256]{1,0:T(8,128)S(1)}, u32[]{:S(2)}, u32[]{:S(2)}) collective-permute-start(f32[16,256]{1,0:T(8,128)S(1)} %add.113), channel_id=1, source_target_pairs={{0,64},{16,80},{32,96},{48,112},{64,0},{80,16},{96,32},{112,48},{1... | collective-permute-start | bytes 49160 | tf_op jit(solution)/shard_map/gather_rows/ppermute | solution.py:392
  96.9 13.8 %collective-permute-start.37 = (bf16[16,128,256]{2,1,0:T(8,128)(2,1)S(1)}, bf16[16,128,256]{2,1,0:T(8,128)(2,1)S(1)}, u32[]{:S(2)}, u32[]{:S(2)}) collective-permute-start(bf16[16,128,256]{2,1,0:T(8,128)(2,1)S(1)} %gather_rows.7.own_ref), channel_id=1, source_target_pairs={{0,16},{16,0},{32,48},{48,32},{64,80},{80,64},{96,112},{112,96},{1... | collective-permute-start | bytes 3145736 | tf_op jit(solution)/shard_map/gather_rows/ppermute | solution.py:392
  105.6 2.3 %collective-permute-start.38 = (f32[16,256]{1,0:T(8,128)S(1)}, f32[16,256]{1,0:T(8,128)S(1)}, u32[]{:S(2)}, u32[]{:S(2)}) collective-permute-start(f32[16,256]{1,0:T(8,128)S(1)} %add.114), channel_id=1, source_target_pairs={{0,16},{16,0},{32,48},{48,32},{64,80},{80,64},{96,112},{112,96},{1... | collective-permute-start | bytes 49160 | tf_op jit(solution)/shard_map/gather_rows/ppermute | solution.py:392
  107.9 6.5 %collective-permute-start.39 = (f32[16,256]{1,0:T(8,128)S(1)}, f32[16,256]{1,0:T(8,128)S(1)}, u32[]{:S(2)}, u32[]{:S(2)}) collective-permute-start(f32[16,256]{1,0:T(8,128)S(1)} %add.115), channel_id=1, source_target_pairs={{0,128},{16,144},{32,160},{48,176},{64,192},{80,208},{96,224},{112... | collective-permute-start | bytes 49160 | tf_op jit(solution)/shard_map/gather_rows/ppermute | solution.py:392
